TPU v7x, 32 devices: a whole 2x2x4 slice. The times are simulated.
32 devices in a mesh: round: 8 (over z, y), mp: 4 (over x, core).
Axes of the slice: x: 2, y: 2, z: 4, core: 2. Of those that a mesh axis runs over, the one named last changes fastest.
Arguments:
- tokens: bfloat16 [8, 32, 512], P('round'), may hold values from -8 to 8
- cell_order: int32 [32], replicated, may hold values from 0 to 31, each once
- seam_rows: int32 [8, 8, 2], P('round'), may hold values from -1 to 31, as said below
- obs_mask: int32 [16, 32], replicated, may hold values from 0 to 1, as said below
- norm_gain: float32 [512], replicated, may hold values from 0.1 to 1.9
- w_query: bfloat16 [512, 512], P(None, 'mp'), may hold values from -1 to 1
- w_key: bfloat16 [512, 512], P(None, 'mp'), may hold values from -1 to 1
- w_value: bfloat16 [512, 512], P(None, 'mp'), may hold values from -0.25 to 0.25
- w_out: bfloat16 [512, 512], P('mp'), may hold values from -0.25 to 0.25
- w_gate: bfloat16 [512, 2048], P(None, 'mp'), may hold values from -0.25 to 0.25
- w_up: bfloat16 [512, 2048], P(None, 'mp'), may hold values from -0.25 to 0.25
- w_down: bfloat16 [2048, 512], P('mp'), may hold values from -0.125 to 0.125
- w_read: float32 [512], replicated, may hold values from -0.25 to 0.25
Outputs:
- tiles_out: bfloat16 [8, 32, 512], P('mp', 'round')
- obs_logits: float32 [16], replicated
Inputs may be any that keep to these rules, and one draw needn't show every extreme that they name: `seam_rows`: each entry is a row of the sending tile or -1 for an empty slot; the live entries of one tile are all different; a tile's slots to itself are full, and some owner's slots are full from every tile. `obs_mask`: every observable's support holds at least one cell.
All inputs are finite; a program needn't handle non-finite values.
Results may differ from a plain program's by a relative error of at most 0.0052.
The roundings to bfloat16 on the way count: a program that leaves them out, or rounds other values in their place, can miss the bound.
Values may be sent and summed in bfloat16 or wider, within the bound.
No kernel may reach another device: no remote copies, remote signals or barrier semaphores. Data moves between devices by JAX's collectives and lax.ppermute only.
A program may use at most 64 MiB of HBM per device.

v0:
```python
import math

import jax
import jax.numpy as jnp
from jax import lax
from jax.sharding import PartitionSpec as P

HDIM = 64


norm_eps = 1e-06


def normalize(rows_in, norm_gain):
    values = rows_in.astype(jnp.float32)
    spread = jnp.mean(values * values, axis=-1, keepdims=True)
    return (values * lax.rsqrt(spread + norm_eps) * norm_gain).astype(jnp.bfloat16)


def attend(queries, keys_all, values_all, live_keys):
    scale_factor = 1.0 / math.sqrt(queries.shape[-1])
    scores = (
        jnp.einsum("qhe,khe->hqk", queries, keys_all, preferred_element_type=jnp.float32)
        * scale_factor
    )
    if live_keys is not None:
        scores = jnp.where(live_keys[None, None, :], scores, -1e30)
    row_max = jnp.max(scores, axis=-1, keepdims=True)
    weights = jnp.exp(scores - row_max)
    probabilities = (weights / jnp.sum(weights, axis=-1, keepdims=True)).astype(jnp.bfloat16)
    mixture = jnp.einsum(
        "hqk,khe->qhe", probabilities, values_all, preferred_element_type=jnp.float32
    )
    return mixture.reshape(mixture.shape[0], -1)


def shards(
    tokens,
    cell_order,
    seam_rows,
    obs_mask,
    norm_gain,
    w_query,
    w_key,
    w_value,
    w_out,
    w_gate,
    w_up,
    w_down,
    w_read,
):
    round_count = lax.axis_size("round")
    model_count = lax.axis_size("mp")
    model_index = lax.axis_index("mp")
    round_index = lax.axis_index("round")
    width = tokens.shape[2]
    cell_dev = tokens.shape[1] // round_count
    permuted = tokens[:, cell_order, :]
    tile_tokens = lax.all_to_all(permuted, "round", split_axis=1, concat_axis=0, tiled=True)
    tile_rows = tile_tokens.shape[0] * cell_dev
    flat_tokens = tile_tokens.reshape(tile_rows, width)
    normed = normalize(flat_tokens, norm_gain)
    queries = jnp.dot(normed, w_query, preferred_element_type=jnp.float32).astype(jnp.bfloat16)
    keys_all = jnp.dot(normed, w_key, preferred_element_type=jnp.float32).astype(jnp.bfloat16)
    values_all = jnp.dot(normed, w_value, preferred_element_type=jnp.float32).astype(jnp.bfloat16)
    head_width = queries.shape[1]
    heads_dev = head_width // HDIM
    block_rows = min(512, tile_rows)
    query_blocks = queries.reshape(tile_rows // block_rows, block_rows, heads_dev, HDIM)
    key_heads = keys_all.reshape(tile_rows, heads_dev, HDIM)
    value_heads = values_all.reshape(tile_rows, heads_dev, HDIM)
    local_attn = lax.map(
        lambda query_block: attend(query_block, key_heads, value_heads, None), query_blocks
    )
    local_attn = local_attn.reshape(tile_rows, head_width)
    live_slot = seam_rows[0] >= 0
    safe_rows = jnp.where(live_slot, seam_rows[0], 0)
    packet = (
        lax.all_to_all(queries[safe_rows], "round", split_axis=0, concat_axis=0, tiled=True),
        lax.all_to_all(keys_all[safe_rows], "round", split_axis=0, concat_axis=0, tiled=True),
        lax.all_to_all(values_all[safe_rows], "round", split_axis=0, concat_axis=0, tiled=True),
        lax.all_to_all(
            live_slot.astype(jnp.bfloat16), "round", split_axis=0, concat_axis=0, tiled=True
        ),
    )
    seam_queries = packet[0].reshape(-1, heads_dev, HDIM)
    seam_keys = packet[1].reshape(-1, heads_dev, HDIM)
    seam_values = packet[2].reshape(-1, heads_dev, HDIM)
    seam_live = packet[3].reshape(-1) > 0.5
    seam_attn = attend(seam_queries, seam_keys, seam_values, seam_live).astype(jnp.bfloat16)
    returned = lax.all_to_all(
        seam_attn.reshape(round_count, -1, head_width),
        "round",
        split_axis=0,
        concat_axis=0,
        tiled=True,
    )
    target = jnp.where(live_slot, seam_rows[0], tile_rows).reshape(-1)
    combined = (
        local_attn.at[target]
        .add(returned.reshape(-1, head_width).astype(jnp.float32), mode="drop")
        .astype(jnp.bfloat16)
    )
    share_rows = tile_rows // model_count
    own_first = model_index * share_rows
    gate_part = jnp.dot(normed, w_gate, preferred_element_type=jnp.float32)
    up_part = jnp.dot(normed, w_up, preferred_element_type=jnp.float32)
    hidden = (jax.nn.silu(gate_part) * up_part).astype(jnp.bfloat16)
    attn_part = jnp.dot(combined, w_out, preferred_element_type=jnp.float32)
    summed = lax.psum_scatter(
        attn_part + jnp.dot(hidden, w_down, preferred_element_type=jnp.float32),
        "mp",
        scatter_dimension=0,
        tiled=True,
    )
    own_rows = lax.dynamic_slice_in_dim(flat_tokens, own_first, share_rows, 0)
    result_rows = (own_rows.astype(jnp.float32) + summed).astype(jnp.bfloat16)
    tiles_out = result_rows.reshape(share_rows // cell_dev, cell_dev, width)
    my_cells = lax.dynamic_slice_in_dim(cell_order, round_index * cell_dev, cell_dev)
    support = obs_mask[:, my_cells].astype(jnp.float32)
    partial_sum = jnp.einsum(
        "oc,rcd->od", support, tiles_out.astype(jnp.float32), precision=lax.Precision.HIGHEST
    )
    support_count = round_count * jnp.sum(obs_mask.astype(jnp.float32), axis=1)
    divisor = jnp.sqrt(support_count)
    pooled = lax.psum(partial_sum, ("round", "mp"))
    obs_logits = jnp.dot(pooled, w_read, precision=lax.Precision.HIGHEST) / divisor
    return (tiles_out, obs_logits)


def solution(mesh):
    return jax.shard_map(
        shards,
        mesh=mesh,
        in_specs=(
            P("round", None, None),
            P(),
            P("round", None, None),
            P(),
            P(),
            P(None, "mp"),
            P(None, "mp"),
            P(None, "mp"),
            P("mp", None),
            P(None, "mp"),
            P(None, "mp"),
            P("mp", None),
            P(),
        ),
        out_specs=(P("mp", "round", None), P()),
        check_vma=False,
    )
```

profile of v0, /device:TPU:0, one launch (start us, length us, event | category | flops | bytes accessed | tf_op | source)
XLA Modules:
  0.0 142.2 jit_solution(12239700583370758431)
XLA Ops:
  7.2 0.7 fusion.36
  7.9 0.7 copy.47
  8.6 7.4 %all-to-all-start.2 = ((bf16[8,1,2]{2,1,0:T(2,128)(2,1)}), bf16[8,1,2]{2,1,0:T(2,128)(2,1)S(1)}, u32[]{:S(2)}, u32[]{:S(2)}) async-start(bf16[8,1,2]{2,1,0:T(2,128)(2,1)} %copy.47), calls=%async_computation.2 | async-start | bytes 8192 | tf_op jit(solution)/shard_map/all_to_all | solution.py:82
  18.0 0.8 reduce.2
  19.4 3.0 %all-to-all-done.2 = bf16[8,1,2]{2,1,0:T(2,128)(2,1)S(1)} async-done(((bf16[8,1,2]{2,1,0:T(2,128)(2,1)}), bf16[8,1,2]{2,1,0:T(2,128)(2,1)S(1)}, u32[]{:S(2)}, u32[]{:S(2)}) %all-to-all-start.2) | async-done | bytes 64 | tf_op jit(solution)/shard_map/all_to_all | solution.py:82
  22.4 3.3 %all-to-all-start = ((bf16[8,2,1024]{2,1,0:T(2,128)(2,1)}), bf16[8,2,1024]{2,1,0:T(2,128)(2,1)S(1)}, u32[]{:S(2)}, u32[]{:S(2)}) async-start(bf16[8,2,1024]{2,1,0:T(2,128)(2,1)} %reshape.218), calls=%async_computation | async-start | bytes 65536 | tf_op jit(solution)/shard_map/all_to_all | solution.py:59
  25.9 6.5 %all-to-all-done = bf16[8,2,1024]{2,1,0:T(2,128)(2,1)S(1)} async-done(((bf16[8,2,1024]{2,1,0:T(2,128)(2,1)}), bf16[8,2,1024]{2,1,0:T(2,128)(2,1)S(1)}, u32[]{:S(2)}, u32[]{:S(2)}) %all-to-all-start) | async-done | bytes 32800 | tf_op jit(solution)/shard_map/all_to_all | solution.py:59
  34.3 1.2 gather_fusion.2
  35.6 3.3 %all-to-all-start.3 = ((bf16[8,2,128]{2,1,0:T(2,128)(2,1)}), bf16[8,2,128]{2,1,0:T(2,128)(2,1)S(1)}, u32[]{:S(2)}, u32[]{:S(2)}) async-start(bf16[8,2,128]{2,1,0:T(2,128)(2,1)} %bitcast.8), calls=%async_computation.3 | async-start | bytes 8192 | tf_op jit(solution)/shard_map/all_to_all | solution.py:79
  39.7 1.2 gather_fusion.3
  40.8 4.5 %all-to-all-done.3 = bf16[8,2,128]{2,1,0:T(2,128)(2,1)S(1)} async-done(((bf16[8,2,128]{2,1,0:T(2,128)(2,1)}), bf16[8,2,128]{2,1,0:T(2,128)(2,1)S(1)}, u32[]{:S(2)}, u32[]{:S(2)}) %all-to-all-start.3) | async-done | bytes 4128 | tf_op jit(solution)/shard_map/all_to_all | solution.py:79
  45.3 3.3 %all-to-all-start.4 = ((bf16[8,2,128]{2,1,0:T(2,128)(2,1)}), bf16[8,2,128]{2,1,0:T(2,128)(2,1)S(1)}, u32[]{:S(2)}, u32[]{:S(2)}) async-start(bf16[8,2,128]{2,1,0:T(2,128)(2,1)} %bitcast.9), calls=%async_computation.4 | async-start | bytes 8192 | tf_op jit(solution)/shard_map/all_to_all | solution.py:80
  48.8 1.2 gather_fusion.1
  50.1 4.9 %all-to-all-done.4 = bf16[8,2,128]{2,1,0:T(2,128)(2,1)S(1)} async-done(((bf16[8,2,128]{2,1,0:T(2,128)(2,1)}), bf16[8,2,128]{2,1,0:T(2,128)(2,1)S(1)}, u32[]{:S(2)}, u32[]{:S(2)}) %all-to-all-start.4) | async-done | bytes 4128 | tf_op jit(solution)/shard_map/all_to_all | solution.py:80
  55.0 3.3 %all-to-all-start.1 = ((bf16[8,2,128]{2,1,0:T(2,128)(2,1)}), bf16[8,2,128]{2,1,0:T(2,128)(2,1)S(1)}, u32[]{:S(2)}, u32[]{:S(2)}) async-start(bf16[8,2,128]{2,1,0:T(2,128)(2,1)} %bitcast.6), calls=%async_computation.1 | async-start | bytes 8192 | tf_op jit(solution)/shard_map/all_to_all | solution.py:81
  58.7 6.0 %all-to-all-done.1 = bf16[8,2,128]{2,1,0:T(2,128)(2,1)S(1)} async-done(((bf16[8,2,128]{2,1,0:T(2,128)(2,1)}), bf16[8,2,128]{2,1,0:T(2,128)(2,1)S(1)}, u32[]{:S(2)}, u32[]{:S(2)}) %all-to-all-start.1) | async-done | bytes 4128 | tf_op jit(solution)/shard_map/all_to_all | solution.py:81
  65.0 0.7 convert_element_type.92
  65.7 3.3 %all-to-all-start.5 = ((bf16[8,2,128]{2,1,0:T(2,128)(2,1)}), bf16[8,2,128]{2,1,0:T(2,128)(2,1)S(1)}, u32[]{:S(2)}, u32[]{:S(2)}) async-start(bf16[8,2,128]{2,1,0:T(2,128)(2,1)} %convert_element_type.92), calls=%async_computation.5 | async-start | bytes 8192 | tf_op jit(solution)/shard_map/all_to_all | solution.py:91
  69.4 5.9 %all-to-all-done.5 = bf16[8,2,128]{2,1,0:T(2,128)(2,1)S(1)} async-done(((bf16[8,2,128]{2,1,0:T(2,128)(2,1)}), bf16[8,2,128]{2,1,0:T(2,128)(2,1)S(1)}, u32[]{:S(2)}, u32[]{:S(2)}) %all-to-all-start.5) | async-done | bytes 4128 | tf_op jit(solution)/shard_map/all_to_all | solution.py:91
  76.0 0.8 convolution_add_fusion
  77.4 16.2 %reduce-scatter.2.cloned.1.call-done = f32[8,512]{1,0:T(8,128)} async-done(((f32[32,512]{1,0:T(8,128)}), f32[8,512]{1,0:T(8,128)}) %reduce-scatter.2.cloned.1.call-update) | async-done | bytes 16400 | tf_op jit(solution)/shard_map/reduce_scatter | solution.py:110
  93.6 0.7 fusion.20
  95.2 39.5 %psum.7 = f32[16,512]{1,0:T(8,128)S(1)} all-reduce(f32[16,512]{1,0:T(8,128)S(1)} %fusion.32), channel_id=1, replica_groups=mesh['round'=8,'mp'=4] {'round','mp'}, use_global_device_ids=true, to_apply=%region_8.9 | all-reduce | flops 8192 | bytes 65536 | tf_op jit(solution)/shard_map/psum | solution.py:126
  134.7 0.7 fusion.10
  (80 shorter events, 8.9 us)
Async XLA Ops:
  7.2 31.8 %copy-start = (bf16[512,512]{1,0:T(8,128)(2,1)S(1)}, bf16[512,512]{1,0:T(8,128)(2,1)}, u32[]{:S(2)}) copy-start(bf16[512,512]{1,0:T(8,128)(2,1)} %param.22) | copy-start | bytes 1572868
  8.6 7.4 %copy-start.10 = (s32[1,8,2]{1,2,0:T(2,128)S(1)}, s32[1,8,2]{1,2,0:T(2,128)}, u32[]{:S(2)}) copy-start(s32[1,8,2]{1,2,0:T(2,128)} %param.15) | copy-start | bytes 196
  8.6 7.5 %copy-start.13 = (s32[32]{0:T(128)S(1)}, s32[32]{0:T(128)}, u32[]{:S(2)}) copy-start(s32[32]{0:T(128)} %param.14) | copy-start | bytes 388
  8.6 7.6 %copy-start.8 = (s32[16,32]{1,0:T(8,128)S(1)}, s32[16,32]{1,0:T(8,128)}, u32[]{:S(2)}) copy-start(s32[16,32]{1,0:T(8,128)} %param.16) | copy-start | bytes 6148
  8.6 13.8 %all-to-all-start.2 = ((bf16[8,1,2]{2,1,0:T(2,128)(2,1)}), bf16[8,1,2]{2,1,0:T(2,128)(2,1)S(1)}, u32[]{:S(2)}, u32[]{:S(2)}) async-start(bf16[8,1,2]{2,1,0:T(2,128)(2,1)} %copy.47), calls=%async_computation.2 | async-start | bytes 8192 | tf_op jit(solution)/shard_map/all_to_all | solution.py:82
  16.0 0.8 copy-start.1
  22.4 10.0 %all-to-all-start = ((bf16[8,2,1024]{2,1,0:T(2,128)(2,1)}), bf16[8,2,1024]{2,1,0:T(2,128)(2,1)S(1)}, u32[]{:S(2)}, u32[]{:S(2)}) async-start(bf16[8,2,1024]{2,1,0:T(2,128)(2,1)} %reshape.218), calls=%async_computation | async-start | bytes 65536 | tf_op jit(solution)/shard_map/all_to_all | solution.py:59
  32.4 0.9 copy-start.4
  32.5 0.7 copy-start.11
  33.2 0.9 copy-start.5
  33.3 2.2 %copy-start.6 = (bf16[512,128]{1,0:T(8,128)(2,1)S(1)}, bf16[512,128]{1,0:T(8,128)(2,1)}, u32[]{:S(2)}) copy-start(bf16[512,128]{1,0:T(8,128)(2,1)} %param.20) | copy-start | bytes 393220
  33.5 5.7 %copy-start.3 = (bf16[512,512]{1,0:T(8,128)(2,1)S(1)}, bf16[512,512]{1,0:T(8,128)(2,1)}, u32[]{:S(2)}) copy-start(bf16[512,512]{1,0:T(8,128)(2,1)} %param.23) | copy-start | bytes 1572868
  34.1 5.1 %copy-start.2 = (bf16[512,512]{1,0:T(8,128)(2,1)S(1)}, bf16[512,512]{1,0:T(8,128)(2,1)}, u32[]{:S(2)}) copy-start(bf16[512,512]{1,0:T(8,128)(2,1)} %param.24) | copy-start | bytes 1572868
  35.6 9.7 %all-to-all-start.3 = ((bf16[8,2,128]{2,1,0:T(2,128)(2,1)}), bf16[8,2,128]{2,1,0:T(2,128)(2,1)S(1)}, u32[]{:S(2)}, u32[]{:S(2)}) async-start(bf16[8,2,128]{2,1,0:T(2,128)(2,1)} %bitcast.8), calls=%async_computation.3 | async-start | bytes 8192 | tf_op jit(solution)/shard_map/all_to_all | solution.py:79
  45.3 9.7 %all-to-all-start.4 = ((bf16[8,2,128]{2,1,0:T(2,128)(2,1)}), bf16[8,2,128]{2,1,0:T(2,128)(2,1)S(1)}, u32[]{:S(2)}, u32[]{:S(2)}) async-start(bf16[8,2,128]{2,1,0:T(2,128)(2,1)} %bitcast.9), calls=%async_computation.4 | async-start | bytes 8192 | tf_op jit(solution)/shard_map/all_to_all | solution.py:80
  55.0 9.6 %all-to-all-start.1 = ((bf16[8,2,128]{2,1,0:T(2,128)(2,1)}), bf16[8,2,128]{2,1,0:T(2,128)(2,1)S(1)}, u32[]{:S(2)}, u32[]{:S(2)}) async-start(bf16[8,2,128]{2,1,0:T(2,128)(2,1)} %bitcast.6), calls=%async_computation.1 | async-start | bytes 8192 | tf_op jit(solution)/shard_map/all_to_all | solution.py:81
  65.7 9.6 %all-to-all-start.5 = ((bf16[8,2,128]{2,1,0:T(2,128)(2,1)}), bf16[8,2,128]{2,1,0:T(2,128)(2,1)S(1)}, u32[]{:S(2)}, u32[]{:S(2)}) async-start(bf16[8,2,128]{2,1,0:T(2,128)(2,1)} %convert_element_type.92), calls=%async_computation.5 | async-start | bytes 8192 | tf_op jit(solution)/shard_map/all_to_all | solution.py:91
  69.0 7.0 %copy-start.7 = (bf16[128,512]{1,0:T(8,128)(2,1)S(1)}, bf16[128,512]{1,0:T(8,128)(2,1)}, u32[]{:S(2)}) copy-start(bf16[128,512]{1,0:T(8,128)(2,1)} %param.21) | copy-start | bytes 393220
  69.0 24.6 %reduce-scatter.2.cloned.1.call-start = ((), (), s32[]{:S(2)}) async-start(), calls=%async_computation.7 | async-start | bytes 81920 | tf_op jit(solution)/shard_map/reduce_scatter | solution.py:110
  94.4 0.6 copy-start.9
  95.2 39.5 %copy-start.12 = (f32[512]{0:T(512)S(1)}, f32[512]{0:T(512)}, u32[]{:S(2)}) copy-start(f32[512]{0:T(512)} %param.25) | copy-start | bytes 6148
Sparse Core Ops, SparseCore 0:
  76.9 16.7 reduce-scatter.1
where the time goes:
time: 143 us; the launch traced here: 142 us
  waiting for transfers between devices  47 us (33%)
  blocking collectives  39.5 us (28%)
  starting transfers between devices  24.1 us (17%)
  between operations  14.3 us (10%)
  local copies, waits for them, and re-layouts  10.4 us (7%)
  matrix products  3.58 us (3%)
  other arithmetic  3.46 us (2%)
    psum x1, blocking collectives, shards(): pooled = lax.psum(partial_sum, ('round', 'mp'))  39.5 us
    reduce_scatter x1, waiting for transfers between devices, shards(): lax.psum_scatter(attn_part + jnp.dot(hidden, w_down, preferred_element_ty...  16.2 us
    all_to_all x1, starting transfers between devices, shards(): lax.all_to_all(live_slot.astype(jnp.bfloat16), 'round', split_axis=0, con...  7.41 us
    all_to_all x1, waiting for transfers between devices, shards(): lax.all_to_all(permuted, 'round', split_axis=1, concat_axis=0, tiled=True)  6.5 us
    all_to_all x1, waiting for transfers between devices, shards(): lax.all_to_all(values_all[safe_rows], 'round', split_axis=0, concat_axis=...  5.97 us
    all_to_all x1, waiting for transfers between devices, shards(): lax.all_to_all(seam_attn.reshape(round_count, -1, head_width), 'round', s...  5.93 us
    all_to_all x1, waiting for transfers between devices, shards(): lax.all_to_all(keys_all[safe_rows], 'round', split_axis=0, concat_axis=0,...  4.91 us
    all_to_all x1, waiting for transfers between devices, shards(): lax.all_to_all(queries[safe_rows], 'round', split_axis=0, concat_axis=0,...  4.45 us
  transfers between devices with their start and end apart: 7, of which 7 were waited for; matrix products, arithmetic and copies ran while one was open for 6% of the time, Pallas kernels for 0%

commit v1 on v0

--- a/solution.py
+++ b/solution.py
@@ -1,11 +1,16 @@
+import functools
 import math
 
 import jax
 import jax.numpy as jnp
 from jax import lax
+from jax.experimental import pallas as pl
+from jax.experimental.pallas import tpu as pltpu
 from jax.sharding import PartitionSpec as P
 
 HDIM = 64
+SEAM_PAD = 16
+VMEM_LIMIT = 32 * 1024 * 1024
 
 
 norm_eps = 1e-06
@@ -34,7 +39,7 @@
     return mixture.reshape(mixture.shape[0], -1)
 
 
-def shards(
+def shards_by_tile(
     tokens,
     cell_order,
     seam_rows,
@@ -128,7 +133,275 @@
     return (tiles_out, obs_logits)
 
 
+def iota(shape, dimension):
+    return lax.broadcasted_iota(jnp.int32, shape, dimension)
+
+
+def one_hot(condition):
+    return jnp.where(condition, 1.0, 0.0).astype(jnp.bfloat16)
+
+
+def dot(left, right):
+    return jnp.dot(left, right, preferred_element_type=jnp.float32)
+
+
+def dot_t(left, right):
+    return lax.dot_general(
+        left, right, (((1,), (1,)), ((), ())), preferred_element_type=jnp.float32
+    )
+
+
+def split_three(values):
+    high = values.astype(jnp.bfloat16)
+    rest = values - high.astype(jnp.float32)
+    middle = rest.astype(jnp.bfloat16)
+    low = (rest - middle.astype(jnp.float32)).astype(jnp.bfloat16)
+    return jnp.concatenate([high, middle, low], axis=0)
+
+
+def softmax(scores):
+    weights = jnp.exp(scores - jnp.max(scores, axis=-1, keepdims=True))
+    return (weights / jnp.sum(weights, axis=-1, keepdims=True)).astype(jnp.bfloat16)
+
+
+def layer_kernel(rounds, cells, slots, *refs):
+    place, blocks, rest = refs[0], refs[1 : 1 + slots], refs[1 + slots :]
+    order, mask_in, gain, w_query, w_key, w_value, w_out, w_gate, w_up, w_down, w_read = rest[:11]
+    send, keep, hidden_all, combined_all, tokens_all = rest[11:]
+    me, model, core = place[0], place[1], place[2]
+    tiles = rounds
+    cell_dev = cells // tiles
+    tile_rows = rounds * cell_dev
+    total = rounds * cells
+    width = gain.shape[1]
+    head_width = w_query.shape[1]
+    observables = mask_in.shape[0]
+
+    def slot_round(slot):
+        return me ^ slot ^ jnp.where(slot >= 2, core, 0)
+
+    row = iota((total, 1), 0)
+    tile = lax.div(row, tile_rows)
+    row_in_tile = lax.rem(row, tile_rows)
+    place_in_order = tile * cell_dev + lax.rem(row_in_tile, cell_dev)
+    cell = jnp.sum(
+        jnp.where(iota((total, cells), 1) == place_in_order, order[...], 0), axis=1, keepdims=True
+    )
+    source = lax.div(row_in_tile, cell_dev) * cells + cell
+    column = iota((1, total), 1)
+    held = slot_round(lax.div(column, cells)) * cells + lax.rem(column, cells)
+    arrived = jnp.concatenate([block[0, :cells] for block in blocks], axis=0)
+    tokens = dot(one_hot(source == held), arrived).astype(jnp.bfloat16)
+    tokens_all[...] = tokens
+
+    slots_all = 2 * tiles
+    entries = jnp.concatenate([block[0, cells : cells + 1, :slots_all] for block in blocks], axis=0)
+    tile_of_slot = slot_round(iota((1, slots), 1))
+    seam_entries = dot(one_hot(tile == tile_of_slot), entries)
+    matched = seam_entries == row_in_tile.astype(jnp.float32)
+    matched_bf = one_hot(matched)
+    same_owner = one_hot(
+        lax.div(iota((slots_all, slots_all), 0), 2) == lax.div(iota((slots_all, slots_all), 1), 2)
+    )
+    seam_mask = dot_t(dot(matched_bf, same_owner).astype(jnp.bfloat16), matched_bf) > 0.5
+    in_seam = jnp.sum(jnp.where(matched, 1.0, 0.0), axis=1, keepdims=True) > 0.5
+    tile_mask = tile == lax.div(column, tile_rows)
+
+    values = tokens.astype(jnp.float32)
+    spread = jnp.mean(values * values, axis=-1, keepdims=True)
+    normed = (values * lax.rsqrt(spread + norm_eps) * gain[...]).astype(jnp.bfloat16)
+    queries = dot(normed, w_query[...]).astype(jnp.bfloat16)
+    keys = dot(normed, w_key[...]).astype(jnp.bfloat16)
+    vals = dot(normed, w_value[...]).astype(jnp.bfloat16)
+    scale = 1.0 / math.sqrt(HDIM)
+    lane_head = lax.div(iota((1, head_width), 1), HDIM)
+    local = jnp.zeros((total, head_width), jnp.float32)
+    seam = jnp.zeros((total, head_width), jnp.float32)
+    for head in range(head_width // HDIM):
+        mine = lane_head == head
+        scores = dot_t(queries, jnp.where(mine, keys, jnp.zeros_like(keys))) * scale
+        head_vals = jnp.where(mine, vals, jnp.zeros_like(vals))
+        local = local + dot(softmax(jnp.where(tile_mask, scores, -1e30)), head_vals)
+        seam = seam + dot(softmax(jnp.where(seam_mask, scores, -1e30)), head_vals)
+    seam = seam.astype(jnp.bfloat16).astype(jnp.float32)
+    combined = (local + jnp.where(in_seam, seam, 0.0)).astype(jnp.bfloat16)
+    combined_all[...] = combined
+
+    gate = dot(normed, w_gate[...])
+    up = dot(normed, w_up[...])
+    hidden = (gate / (1.0 + jnp.exp(-gate)) * up).astype(jnp.bfloat16)
+    hidden_all[...] = hidden
+
+    mask_bf = mask_in[...].astype(jnp.float32).astype(jnp.bfloat16)
+    support = dot_t(mask_bf, one_hot(iota((total, cells), 1) == cell)).astype(jnp.bfloat16)
+    own = pl.ds(pl.multiple_of(me * tile_rows, tile_rows), tile_rows)
+    hidden_rows = jnp.concatenate([hidden_all[own, :], split_three(dot(support, hidden))], axis=0)
+    combined_rows = jnp.concatenate(
+        [combined_all[own, :], split_three(dot(support, combined))], axis=0
+    )
+    product = dot(hidden_rows, w_down[...]) + dot(combined_rows, w_out[...])
+    first, second, third = (tile_rows + observables * k for k in range(3))
+    pooled = (
+        product[first : first + observables]
+        + product[second : second + observables]
+        + product[third : third + observables]
+        + jnp.where(model == 0, dot(support, tokens), 0.0)
+    )
+    count = rounds * jnp.sum(mask_in[...].astype(jnp.float32), axis=1, keepdims=True)
+    logits = jnp.sum(pooled * w_read[...], axis=1, keepdims=True) / jnp.sqrt(count)
+    diagonal = iota((observables, width), 0) == iota((observables, width), 1)
+    logits_row = jnp.sum(jnp.where(diagonal, logits, 0.0), axis=0, keepdims=True)
+    logits_tile = jnp.broadcast_to(logits_row, (8, width))
+
+    pairs = send.shape[0]
+    share = tile_rows // 4
+    update = product[:tile_rows]
+    own_tokens = tokens_all[own, :].astype(jnp.float32)
+    update = update + jnp.where(lax.div(iota((tile_rows, 1), 0), share) == model, own_tokens, 0.0)
+    pair = lax.shift_right_logical(model, 1)
+    chunks = [update[share * k : share * (k + 1)] for k in range(4)]
+
+    def chunk(pair_index, core_index):
+        low = jnp.where(core_index == 0, chunks[0], chunks[1])
+        high = jnp.where(core_index == 0, chunks[2], chunks[3])
+        return jnp.where(pair_index == 0, low, high)
+
+    for target, core_index in ((send, 1 - core), (keep, core)):
+        target[:share] = chunk(1 - pair, core_index)
+        target[share : share + 8] = logits_tile
+        target[share + 8 :] = chunk(pair, core_index)
+
+
+def finish_kernel(share, own, arrived, tiles_out, logits_out):
+    cell_dev = tiles_out.shape[1]
+    rows = own[8 : 8 + share] + arrived[:share]
+    for k in range(tiles_out.shape[0]):
+        tiles_out[k] = rows[k * cell_dev : (k + 1) * cell_dev].astype(tiles_out.dtype)
+    logits = own[:1] + arrived[share : share + 1]
+    logits_out[...] = logits[:, : logits_out.shape[1]]
+
+
+def shards_whole(
+    tokens,
+    cell_order,
+    seam_rows,
+    obs_mask,
+    norm_gain,
+    w_query,
+    w_key,
+    w_value,
+    w_out,
+    w_gate,
+    w_up,
+    w_down,
+    w_read,
+):
+    rounds = lax.axis_size("round")
+    models = lax.axis_size("mp")
+    me = lax.axis_index("round")
+    model = lax.axis_index("mp")
+    cells, width = tokens.shape[1:]
+    cell_dev = cells // rounds
+    tile_rows = rounds * cell_dev
+    share = tile_rows // models
+    core = model & 1
+
+    seam_block = jnp.pad(
+        seam_rows.reshape(1, 1, -1).astype(jnp.bfloat16),
+        ((0, 0), (0, SEAM_PAD - 1), (0, width - seam_rows.size)),
+    )
+    block = jnp.concatenate([tokens, seam_block], axis=1)
+
+    def fetch(even_step, odd_step):
+        pairs = [
+            (r * models + m, (r ^ (odd_step if m & 1 else even_step)) * models + m)
+            for r in range(rounds)
+            for m in range(models)
+        ]
+        return lax.ppermute(block, ("round", "mp"), pairs)
+
+    def other_core(array):
+        return lax.ppermute(array, "mp", [(m, m ^ 1) for m in range(models)])
+
+    direct = {k: fetch(k, k + 1) for k in range(rounds - 2, 0, -2)}
+    next_door = fetch(1, 1)
+    blocks = [block, next_door]
+    for k in range(2, rounds, 2):
+        blocks += [direct[k], other_core(direct[k])]
+
+    place = jnp.stack([me, model, core]).astype(jnp.int32)
+    vmem = pl.BlockSpec(memory_space=pltpu.VMEM)
+    smem = pl.BlockSpec(memory_space=pltpu.SMEM)
+    total = rounds * cells
+    part = jax.ShapeDtypeStruct((2 * share + 8, width), jnp.float32)
+    send, keep = pl.pallas_call(
+        functools.partial(layer_kernel, rounds, cells, len(blocks)),
+        out_shape=(part, part),
+        in_specs=[smem] + [vmem] * (len(blocks) + 11),
+        out_specs=(vmem, vmem),
+        scratch_shapes=[
+            pltpu.VMEM((total, w_gate.shape[1]), jnp.bfloat16),
+            pltpu.VMEM((total, w_query.shape[1]), jnp.bfloat16),
+            pltpu.VMEM((total, width), jnp.bfloat16),
+        ],
+        compiler_params=pltpu.CompilerParams(vmem_limit_bytes=VMEM_LIMIT),
+    )(
+        place,
+        *blocks,
+        cell_order.reshape(1, -1),
+        obs_mask,
+        norm_gain.reshape(1, -1),
+        w_query,
+        w_key,
+        w_value,
+        w_out,
+        w_gate,
+        w_up,
+        w_down,
+        w_read.reshape(1, -1),
+    )
+    chip = keep + other_core(send)
+    arrived = lax.ppermute(chip[: share + 8], "mp", [(m, m ^ 2) for m in range(models)])
+    tiles_out, logits = pl.pallas_call(
+        functools.partial(finish_kernel, share),
+        out_shape=(
+            jax.ShapeDtypeStruct((share // cell_dev, cell_dev, width), jnp.bfloat16),
+            jax.ShapeDtypeStruct((1, obs_mask.shape[0]), jnp.float32),
+        ),
+        in_specs=[vmem, vmem],
+        out_specs=(vmem, vmem),
+    )(chip[share:], arrived)
+    return tiles_out, logits.reshape(-1)
+
+
+def fits_whole(mesh, tokens, seam_rows, w_query):
+    rounds, models = mesh.shape["round"], mesh.shape["mp"]
+    total = tokens.shape[0] * tokens.shape[1]
+    share = total // rounds // models
+    return (
+        models == 4
+        and rounds == tokens.shape[0]
+        and rounds & (rounds - 1) == 0
+        and rounds > 2
+        and total <= 512
+        and total // rounds <= 256
+        and share % 8 == 0
+        and tokens.shape[1] % 16 == 0
+        and seam_rows.shape[2] == 2
+        and w_query.shape[1] // models % HDIM == 0
+    )
+
+
 def solution(mesh):
+    def layer(*args):
+        tokens, seam_rows, w_query = args[0], args[2], args[5]
+        whole = fits_whole(mesh, tokens, seam_rows, w_query)
+        return placed(mesh, shards_whole if whole else shards_by_tile)(*args)
+
+    return layer
+
+
+def placed(mesh, shards):
     return jax.shard_map(
         shards,
         mesh=mesh,

time: 143 us -> 32.5 us (0.23)
  waiting for transfers between devices: 47 us -> 7.34 us
  blocking collectives: 39.5 us -> 0 us
  starting transfers between devices: 24.1 us -> 9.53 us
  between operations: 14.3 us -> 0.66 us
  Pallas kernels: 0 us -> 4.06 us
  matrix products: 3.58 us -> 0 us
  other arithmetic: 3.46 us -> 1.53 us
  local copies, waits for them, and re-layouts: 10.4 us -> 8.83 us
    psum x1 -> x0, blocking collectives: 39.5 us -> none  [shards(): pooled = lax.psum(partial_sum, ('round', 'mp'))]
    all_to_all x6 -> x0, waiting for transfers between devices: 30.7 us -> none  [the longest x1 6.5 us: shards(): lax.all_to_all(permuted, 'round', split_axis=1, concat_axis=0, tiled=True)]
    all_to_all x6 -> x0, starting transfers between devices: 24 us -> none  [the longest x1 7.41 us: shards(): lax.all_to_all(live_slot.astype(jnp.bfloat16), 'round', split_axis=0, con...]
    reduce_scatter x1 -> x0, waiting for transfers between devices: 16.2 us -> none  [shards(): lax.psum_scatter(attn_part + jnp.dot(hidden, w_down, preferred_element_ty...]
    ppermute x0 -> x9, starting transfers between devices: none -> 9.53 us  [the longest x4 7.35 us: fetch(): return lax.ppermute(block, ('round', 'mp'), pairs)]
    ppermute x0 -> x9, waiting for transfers between devices: none -> 7.34 us  [the longest x4 3.21 us: fetch(): return lax.ppermute(block, ('round', 'mp'), pairs)]
    gather x6 -> x0, local copies, waits for them, and re-layouts: 4.74 us -> none  [the longest x1 1.17 us: shards(): keys_all[safe_rows]]
    unnamed x33 -> x24, local copies, waits for them, and re-layouts: 3.3 us -> 8.04 us
  transfers between devices with their start and end apart: 7 -> 9, of which waited for: 7 -> 7; matrix products, arithmetic and copies ran while one was open for 6% -> 0% of each run, Pallas kernels for 0% -> 0%
where the time goes in v1:
time: 32.5 us; the launch traced here: 31.9 us
  starting transfers between devices  9.53 us (29%)
  local copies, waits for them, and re-layouts  8.83 us (27%)
  waiting for transfers between devices  7.34 us (23%)
  Pallas kernels  4.06 us (12%)
  other arithmetic  1.53 us (5%)
  between operations  0.66 us (2%)
    unnamed x24, local copies, waits for them, and re-layouts  8.04 us
    ppermute x4, starting transfers between devices, fetch(): return lax.ppermute(block, ('round', 'mp'), pairs)  7.35 us
    ppermute x4, waiting for transfers between devices, fetch(): return lax.ppermute(block, ('round', 'mp'), pairs)  3.21 us
    pallas_call x1, Pallas kernels, shards_whole(): pl.pallas_call(functools.partial(layer_kernel, rounds, cells, len(blocks)...  2.67 us
    ppermute x1, waiting for transfers between devices, shards_whole(): lax.ppermute(chip[:share + 8], 'mp', [(m, m ^ 2) for m in range(models)])  2.43 us
    ppermute x4, waiting for transfers between devices, other_core(): return lax.ppermute(array, 'mp', [(m, m ^ 1) for m in range(models)])  1.71 us
    ppermute x1, starting transfers between devices, shards_whole(): lax.ppermute(chip[:share + 8], 'mp', [(m, m ^ 2) for m in range(models)])  1.49 us
    pallas_call x1, Pallas kernels, shards_whole(): pl.pallas_call(functools.partial(finish_kernel, share), out_shape=(jax.Sh...  1.38 us
  transfers between devices with their start and end apart: 9, of which 7 were waited for; matrix products, arithmetic and copies ran while one was open for 0% of the time, Pallas kernels for 0%

profile of v1, /device:TPU:0, one launch (start us, length us, event | category | flops | bytes accessed | tf_op | source)
XLA Modules:
  0.0 31.9 jit_solution(10081552551262627978)
XLA Ops:
  0.6 0.7 %convert_element_type.16 = bf16[1,8,2]{1,2,0:T(2,128)(2,1)S(1)} convert(s32[1,8,2]{1,2,0:T(2,128)} %param.15) | non-fusion elementwise | flops 16 | bytes 96 | tf_op jit(solution)/shard_map/convert_element_type | solution.py:310
  1.5 0.8 %fusion.1.refs_1_ = bf16[1,48,512]{2,1,0:T(8,128)(2,1)S(1)} fusion(bf16[1,1,16]{2,1,0:T(2,128)(2,1)S(1)} %convert_element_type.17, bf16[1,32,512]{2,1,0:T(8,128)(2,1)} %param.13), kind=kLoop, calls=%fused_computation.2 | loop fusion | flops 147456 | bytes 81952 | tf_op jit(solution)/shard_map/concatenate | solution.py:313
  2.3 5.0 %collective-permute-start.5 = (bf16[1,48,512]{2,1,0:T(8,128)(2,1)S(1)}, bf16[1,48,512]{2,1,0:T(8,128)(2,1)S(1)}, u32[]{:S(2)}, u32[]{:S(2)}) collective-permute-start(bf16[1,48,512]{2,1,0:T(8,128)(2,1)S(1)} %fusion.1.refs_1_), channel_id=1, source_target_pairs={{0,24},{1,29},{2,26},{3,31},{4,28},{5,25},{6,30},{7,27},{8,16},{9,... | collective-permute-start | bytes 147464 | tf_op jit(solution)/shard_map/ppermute | solution.py:321
  7.3 0.6 %collective-permute-start.1 = (bf16[1,48,512]{2,1,0:T(8,128)(2,1)S(1)}, bf16[1,48,512]{2,1,0:T(8,128)(2,1)S(1)}, u32[]{:S(2)}, u32[]{:S(2)}) collective-permute-start(bf16[1,48,512]{2,1,0:T(8,128)(2,1)S(1)} %fusion.1.refs_1_), channel_id=1, source_target_pairs={{0,8},{1,13},{2,10},{3,15},{4,12},{5,9},{6,14},{7,11},{8,0},{9,5},... | collective-permute-start | bytes 147464 | tf_op jit(solution)/shard_map/ppermute | solution.py:321
  8.0 1.7 %collective-permute-start = (bf16[1,48,512]{2,1,0:T(8,128)(2,1)S(1)}, bf16[1,48,512]{2,1,0:T(8,128)(2,1)S(1)}, u32[]{:S(2)}, u32[]{:S(2)}) collective-permute-start(bf16[1,48,512]{2,1,0:T(8,128)(2,1)S(1)} %fusion.1.refs_1_), channel_id=1, source_target_pairs={{0,4},{1,5},{2,6},{3,7},{4,0},{5,1},{6,2},{7,3},{8,12},{9,13},{10,... | collective-permute-start | bytes 147464 | tf_op jit(solution)/shard_map/ppermute | solution.py:321
  10.0 2.5 %collective-permute-done.3.refs_5_ = bf16[1,48,512]{2,1,0:T(8,128)(2,1)S(1)} collective-permute-done((bf16[1,48,512]{2,1,0:T(8,128)(2,1)S(1)}, bf16[1,48,512]{2,1,0:T(8,128)(2,1)S(1)}, u32[]{:S(2)}, u32[]{:S(2)}) %collective-permute-start.3) | collective-permute-done | bytes 49184 | tf_op jit(solution)/shard_map/ppermute | solution.py:321
  12.5 0.4 %collective-permute-start.4 = (bf16[1,48,512]{2,1,0:T(8,128)(2,1)S(1)}, bf16[1,48,512]{2,1,0:T(8,128)(2,1)S(1)}, u32[]{:S(2)}, u32[]{:S(2)}) collective-permute-start(bf16[1,48,512]{2,1,0:T(8,128)(2,1)S(1)} %collective-permute-done.3.refs_5_), channel_id=1, source_target_pairs={{0,1},{1,0},{2,3},{3,2},{4,5},{5,4},{6,7},{7,6},{8,9},{9,8},{10,11... | collective-permute-start | bytes 147464 | tf_op jit(solution)/shard_map/ppermute | solution.py:324
  13.1 0.4 %collective-permute-done.refs_2_ = bf16[1,48,512]{2,1,0:T(8,128)(2,1)S(1)} collective-permute-done((bf16[1,48,512]{2,1,0:T(8,128)(2,1)S(1)}, bf16[1,48,512]{2,1,0:T(8,128)(2,1)S(1)}, u32[]{:S(2)}, u32[]{:S(2)}) %collective-permute-start) | collective-permute-done | bytes 49184 | tf_op jit(solution)/shard_map/ppermute | solution.py:321
  13.7 0.4 %collective-permute-done.2.refs_4_ = bf16[1,48,512]{2,1,0:T(8,128)(2,1)S(1)} collective-permute-done((bf16[1,48,512]{2,1,0:T(8,128)(2,1)S(1)}, bf16[1,48,512]{2,1,0:T(8,128)(2,1)S(1)}, u32[]{:S(2)}, u32[]{:S(2)}) %collective-permute-start.2) | collective-permute-done | bytes 49184 | tf_op jit(solution)/shard_map/ppermute | solution.py:324
  14.1 0.7 %copy-done.9 = f32[512]{0:T(512)S(1)} copy-done((f32[512]{0:T(512)S(1)}, f32[512]{0:T(512)}, u32[]{:S(2)}) %copy-start.9) | copy-done | bytes 2072
  14.8 1.0 %copy-done = bf16[512,512]{1,0:T(8,128)(2,1)S(1)} copy-done((bf16[512,512]{1,0:T(8,128)(2,1)S(1)}, bf16[512,512]{1,0:T(8,128)(2,1)}, u32[]{:S(2)}) %copy-start) | copy-done | bytes 524312
  15.8 1.0 %copy-done.1 = bf16[512,512]{1,0:T(8,128)(2,1)S(1)} copy-done((bf16[512,512]{1,0:T(8,128)(2,1)S(1)}, bf16[512,512]{1,0:T(8,128)(2,1)}, u32[]{:S(2)}) %copy-start.1) | copy-done | bytes 524312
  16.9 1.0 %copy-done.2 = bf16[512,512]{1,0:T(8,128)(2,1)S(1)} copy-done((bf16[512,512]{1,0:T(8,128)(2,1)S(1)}, bf16[512,512]{1,0:T(8,128)(2,1)}, u32[]{:S(2)}) %copy-start.2) | copy-done | bytes 524312
  17.9 0.9 %copy-done.3 = bf16[512,128]{1,0:T(8,128)(2,1)S(1)} copy-done((bf16[512,128]{1,0:T(8,128)(2,1)S(1)}, bf16[512,128]{1,0:T(8,128)(2,1)}, u32[]{:S(2)}) %copy-start.3) | copy-done | bytes 131096
  18.8 0.9 %copy-done.4 = bf16[512,128]{1,0:T(8,128)(2,1)S(1)} copy-done((bf16[512,128]{1,0:T(8,128)(2,1)S(1)}, bf16[512,128]{1,0:T(8,128)(2,1)}, u32[]{:S(2)}) %copy-start.4) | copy-done | bytes 131096
  19.7 0.9 %copy-done.5 = bf16[512,128]{1,0:T(8,128)(2,1)S(1)} copy-done((bf16[512,128]{1,0:T(8,128)(2,1)S(1)}, bf16[512,128]{1,0:T(8,128)(2,1)}, u32[]{:S(2)}) %copy-start.5) | copy-done | bytes 131096
  20.6 0.9 %copy-done.6 = bf16[128,512]{1,0:T(8,128)(2,1)S(1)} copy-done((bf16[128,512]{1,0:T(8,128)(2,1)S(1)}, bf16[128,512]{1,0:T(8,128)(2,1)}, u32[]{:S(2)}) %copy-start.6) | copy-done | bytes 131096
  21.5 2.7 %shard_map.140 = (f32[24,512]{1,0:T(8,128)S(1)}, f32[24,512]{1,0:T(8,128)S(1)}) custom-call(s32[3]{0:T(128)S(1)} %pad_add_fusion.refs_0_, bf16[1,48,512]{2,1,0:T(8,128)(2,1)S(1)} %fusion.1.refs_1_, bf16[1,48,512]{2,1,0:T(8,128)(2,1)S(1)} %collective-permute-done.refs_2_, bf16[1,48,512]{2,1,0:T(8,128)(2,1)S(1)} %collective-permute-done.1.refs_3_, ...), custom_call_target="tpu_custom_call" | custom-call | tf_op jit(solution)/shard_map/pallas_call | solution.py:337
  24.4 1.1 %collective-permute-done.7 = f32[24,512]{1,0:T(8,128)S(1)} collective-permute-done((f32[24,512]{1,0:T(8,128)S(1)}, f32[24,512]{1,0:T(8,128)S(1)}, u32[]{:S(2)}, u32[]{:S(2)}) %collective-permute-start.7) | collective-permute-done | bytes 49184 | tf_op jit(solution)/shard_map/ppermute | solution.py:324
  25.4 0.6 %fusion.2 = (f32[16,512]{1,0:T(8,128)S(1)}, f32[16,512]{1,0:T(8,128)}) fusion(f32[24,512]{1,0:T(8,128)S(1)} %add.5), kind=kLoop, calls=%fused_computation.4 | loop fusion | bytes 131072 | tf_op jit(solution)/shard_map/slice | solution.py:364
  26.0 1.5 %collective-permute-start.8 = (f32[16,512]{1,0:T(8,128)S(1)}, f32[16,512]{1,0:T(8,128)S(1)}, u32[]{:S(2)}, u32[]{:S(2)}) collective-permute-start(f32[16,512]{1,0:T(8,128)S(1)} %get-tuple-element.10), channel_id=1, source_target_pairs={{0,2},{1,3},{2,0},{3,1},{4,6},{5,7},{6,4},{7,5},{8,10},{9,11},{10,... | collective-permute-start | bytes 98312 | tf_op jit(solution)/shard_map/ppermute | solution.py:364
  27.5 2.4 %collective-permute-done.8.arrived = f32[16,512]{1,0:T(8,128)S(1)} collective-permute-done((f32[16,512]{1,0:T(8,128)S(1)}, f32[16,512]{1,0:T(8,128)S(1)}, u32[]{:S(2)}, u32[]{:S(2)}) %collective-permute-start.8) | collective-permute-done | bytes 32800 | tf_op jit(solution)/shard_map/ppermute | solution.py:364
  30.0 0.6 %copy-done.11 = f32[16,512]{1,0:T(8,128)} copy-done((f32[16,512]{1,0:T(8,128)}, f32[16,512]{1,0:T(8,128)S(1)}, u32[]{:S(2)}) %copy-start.11) | copy-done | bytes 32792
  30.6 1.4 %shard_map.141 = (bf16[2,4,512]{2,1,0:T(4,128)(2,1)}, f32[1,16]{1,0:T(1,128)}) custom-call(f32[16,512]{1,0:T(8,128)} %get-tuple-element.11.own, f32[16,512]{1,0:T(8,128)} %copy-done.11), custom_call_target="tpu_custom_call" | custom-call | tf_op jit(solution)/shard_map/pallas_call | solution.py:365
  (27 shorter events, 1.3 us)
Async XLA Ops:
  2.3 7.7 %collective-permute-start.5 = (bf16[1,48,512]{2,1,0:T(8,128)(2,1)S(1)}, bf16[1,48,512]{2,1,0:T(8,128)(2,1)S(1)}, u32[]{:S(2)}, u32[]{:S(2)}) collective-permute-start(bf16[1,48,512]{2,1,0:T(8,128)(2,1)S(1)} %fusion.1.refs_1_), channel_id=1, source_target_pairs={{0,24},{1,29},{2,26},{3,31},{4,28},{5,25},{6,30},{7,27},{8,16},{9,... | collective-permute-start | bytes 147464 | tf_op jit(solution)/shard_map/ppermute | solution.py:321
  7.3 5.1 %collective-permute-start.3 = (bf16[1,48,512]{2,1,0:T(8,128)(2,1)S(1)}, bf16[1,48,512]{2,1,0:T(8,128)(2,1)S(1)}, u32[]{:S(2)}, u32[]{:S(2)}) collective-permute-start(bf16[1,48,512]{2,1,0:T(8,128)(2,1)S(1)} %fusion.1.refs_1_), channel_id=1, source_target_pairs={{0,16},{1,21},{2,18},{3,23},{4,20},{5,17},{6,22},{7,19},{8,24},{9,... | collective-permute-start | bytes 147464 | tf_op jit(solution)/shard_map/ppermute | solution.py:321
  7.3 5.5 %collective-permute-start.1 = (bf16[1,48,512]{2,1,0:T(8,128)(2,1)S(1)}, bf16[1,48,512]{2,1,0:T(8,128)(2,1)S(1)}, u32[]{:S(2)}, u32[]{:S(2)}) collective-permute-start(bf16[1,48,512]{2,1,0:T(8,128)(2,1)S(1)} %fusion.1.refs_1_), channel_id=1, source_target_pairs={{0,8},{1,13},{2,10},{3,15},{4,12},{5,9},{6,14},{7,11},{8,0},{9,5},... | collective-permute-start | bytes 147464 | tf_op jit(solution)/shard_map/ppermute | solution.py:321
  8.0 5.5 %collective-permute-start = (bf16[1,48,512]{2,1,0:T(8,128)(2,1)S(1)}, bf16[1,48,512]{2,1,0:T(8,128)(2,1)S(1)}, u32[]{:S(2)}, u32[]{:S(2)}) collective-permute-start(bf16[1,48,512]{2,1,0:T(8,128)(2,1)S(1)} %fusion.1.refs_1_), channel_id=1, source_target_pairs={{0,4},{1,5},{2,6},{3,7},{4,0},{5,1},{6,2},{7,3},{8,12},{9,13},{10,... | collective-permute-start | bytes 147464 | tf_op jit(solution)/shard_map/ppermute | solution.py:321
  9.6 4.4 %copy-start.7 = (s32[16,32]{1,0:T(8,128)S(1)}, s32[16,32]{1,0:T(8,128)}, u32[]{:S(2)}) copy-start(s32[16,32]{1,0:T(8,128)} %refs_10_.1) | copy-start | bytes 6148
  10.0 3.5 %collective-permute-start.6 = (bf16[1,48,512]{2,1,0:T(8,128)(2,1)S(1)}, bf16[1,48,512]{2,1,0:T(8,128)(2,1)S(1)}, u32[]{:S(2)}, u32[]{:S(2)}) collective-permute-start(bf16[1,48,512]{2,1,0:T(8,128)(2,1)S(1)} %collective-permute-done.5.refs_7_), channel_id=1, source_target_pairs={{0,1},{1,0},{2,3},{3,2},{4,5},{5,4},{6,7},{7,6},{8,9},{9,8},{10,11... | collective-permute-start | bytes 147464 | tf_op jit(solution)/shard_map/ppermute | solution.py:324
  12.5 1.2 %collective-permute-start.4 = (bf16[1,48,512]{2,1,0:T(8,128)(2,1)S(1)}, bf16[1,48,512]{2,1,0:T(8,128)(2,1)S(1)}, u32[]{:S(2)}, u32[]{:S(2)}) collective-permute-start(bf16[1,48,512]{2,1,0:T(8,128)(2,1)S(1)} %collective-permute-done.3.refs_5_), channel_id=1, source_target_pairs={{0,1},{1,0},{2,3},{3,2},{4,5},{5,4},{6,7},{7,6},{8,9},{9,8},{10,11... | collective-permute-start | bytes 147464 | tf_op jit(solution)/shard_map/ppermute | solution.py:324
  12.8 1.2 %collective-permute-start.2 = (bf16[1,48,512]{2,1,0:T(8,128)(2,1)S(1)}, bf16[1,48,512]{2,1,0:T(8,128)(2,1)S(1)}, u32[]{:S(2)}, u32[]{:S(2)}) collective-permute-start(bf16[1,48,512]{2,1,0:T(8,128)(2,1)S(1)} %collective-permute-done.1.refs_3_), channel_id=1, source_target_pairs={{0,1},{1,0},{2,3},{3,2},{4,5},{5,4},{6,7},{7,6},{8,9},{9,8},{10,11... | collective-permute-start | bytes 147464 | tf_op jit(solution)/shard_map/ppermute | solution.py:324
  14.1 0.7 %copy-start.9 = (f32[512]{0:T(512)S(1)}, f32[512]{0:T(512)}, u32[]{:S(2)}) copy-start(f32[512]{0:T(512)} %param.25) | copy-start | bytes 6148
  14.1 0.7 %copy-start.8 = (f32[512]{0:T(512)S(1)}, f32[512]{0:T(512)}, u32[]{:S(2)}) copy-start(f32[512]{0:T(512)} %param.17) | copy-start | bytes 6148
  14.1 0.7 %copy-start.10 = (s32[32]{0:T(128)S(1)}, s32[32]{0:T(128)}, u32[]{:S(2)}) copy-start(s32[32]{0:T(128)} %param.14) | copy-start | bytes 388
  14.8 1.0 %copy-start = (bf16[512,512]{1,0:T(8,128)(2,1)S(1)}, bf16[512,512]{1,0:T(8,128)(2,1)}, u32[]{:S(2)}) copy-start(bf16[512,512]{1,0:T(8,128)(2,1)} %refs_16_.1) | copy-start | bytes 1572868
  15.8 1.0 %copy-start.1 = (bf16[512,512]{1,0:T(8,128)(2,1)S(1)}, bf16[512,512]{1,0:T(8,128)(2,1)}, u32[]{:S(2)}) copy-start(bf16[512,512]{1,0:T(8,128)(2,1)} %refs_17_.1) | copy-start | bytes 1572868
  16.9 1.0 %copy-start.2 = (bf16[512,512]{1,0:T(8,128)(2,1)S(1)}, bf16[512,512]{1,0:T(8,128)(2,1)}, u32[]{:S(2)}) copy-start(bf16[512,512]{1,0:T(8,128)(2,1)} %refs_18_.1) | copy-start | bytes 1572868
  17.9 0.9 %copy-start.3 = (bf16[512,128]{1,0:T(8,128)(2,1)S(1)}, bf16[512,128]{1,0:T(8,128)(2,1)}, u32[]{:S(2)}) copy-start(bf16[512,128]{1,0:T(8,128)(2,1)} %refs_12_.1) | copy-start | bytes 393220
  18.8 0.9 %copy-start.4 = (bf16[512,128]{1,0:T(8,128)(2,1)S(1)}, bf16[512,128]{1,0:T(8,128)(2,1)}, u32[]{:S(2)}) copy-start(bf16[512,128]{1,0:T(8,128)(2,1)} %refs_13_.1) | copy-start | bytes 393220
  19.7 0.9 %copy-start.5 = (bf16[512,128]{1,0:T(8,128)(2,1)S(1)}, bf16[512,128]{1,0:T(8,128)(2,1)}, u32[]{:S(2)}) copy-start(bf16[512,128]{1,0:T(8,128)(2,1)} %refs_14_.1) | copy-start | bytes 393220
  20.6 0.9 %copy-start.6 = (bf16[128,512]{1,0:T(8,128)(2,1)S(1)}, bf16[128,512]{1,0:T(8,128)(2,1)}, u32[]{:S(2)}) copy-start(bf16[128,512]{1,0:T(8,128)(2,1)} %refs_15_.1) | copy-start | bytes 393220
  24.2 1.2 %collective-permute-start.7 = (f32[24,512]{1,0:T(8,128)S(1)}, f32[24,512]{1,0:T(8,128)S(1)}, u32[]{:S(2)}, u32[]{:S(2)}) collective-permute-start(f32[24,512]{1,0:T(8,128)S(1)} %get-tuple-element.7), channel_id=1, source_target_pairs={{0,1},{1,0},{2,3},{3,2},{4,5},{5,4},{6,7},{7,6},{8,9},{9,8},{10,11... | collective-permute-start | bytes 147464 | tf_op jit(solution)/shard_map/ppermute | solution.py:324
  26.0 3.9 %collective-permute-start.8 = (f32[16,512]{1,0:T(8,128)S(1)}, f32[16,512]{1,0:T(8,128)S(1)}, u32[]{:S(2)}, u32[]{:S(2)}) collective-permute-start(f32[16,512]{1,0:T(8,128)S(1)} %get-tuple-element.10), channel_id=1, source_target_pairs={{0,2},{1,3},{2,0},{3,1},{4,6},{5,7},{6,4},{7,5},{8,10},{9,11},{10,... | collective-permute-start | bytes 98312 | tf_op jit(solution)/shard_map/ppermute | solution.py:364
  30.0 0.6 %copy-start.11 = (f32[16,512]{1,0:T(8,128)}, f32[16,512]{1,0:T(8,128)S(1)}, u32[]{:S(2)}) copy-start(f32[16,512]{1,0:T(8,128)S(1)} %collective-permute-done.8.arrived) | copy-start | bytes 98308

commit v2 on v1

--- a/solution.py
+++ b/solution.py
@@ -10,7 +10,9 @@
 
 HDIM = 64
 SEAM_PAD = 16
-VMEM_LIMIT = 32 * 1024 * 1024
+LANES = 128
+SMALL_LIMIT = 8 * 1024 * 1024
+LAYER_LIMIT = 32 * 1024 * 1024
 
 
 norm_eps = 1e-06
@@ -164,55 +166,112 @@
     return (weights / jnp.sum(weights, axis=-1, keepdims=True)).astype(jnp.bfloat16)
 
 
-def layer_kernel(rounds, cells, slots, *refs):
-    place, blocks, rest = refs[0], refs[1 : 1 + slots], refs[1 + slots :]
-    order, mask_in, gain, w_query, w_key, w_value, w_out, w_gate, w_up, w_down, w_read = rest[:11]
-    send, keep, hidden_all, combined_all, tokens_all = rest[11:]
-    me, model, core = place[0], place[1], place[2]
-    tiles = rounds
-    cell_dev = cells // tiles
+def pack_kernel(tokens, seam_rows, block, landed, padded, arrivals):
+    cells = tokens.shape[1]
+    slots, owners = seam_rows.shape[1:]
+    copies = [
+        pltpu.make_async_copy(seam_rows.at[0], landed, arrivals.at[0]),
+        pltpu.make_async_copy(tokens, block.at[:, :cells], arrivals.at[1]),
+    ]
+    for copy in copies:
+        copy.start()
+    padded[...] = jnp.full(padded.shape, -1.0, jnp.float32)
+    copies[0].wait()
+    padded[:slots, :owners] = landed[...].astype(jnp.float32)
+    block[0, cells:, :LANES] = padded[...].astype(jnp.bfloat16)
+    copies[1].wait()
+
+
+def prepare_kernel(rounds, cells, counts, *refs):
+    copied, order_in, mask_in = refs[:counts], refs[counts], refs[counts + 1]
+    weights, rest = refs[counts + 2 : 2 * counts + 2], refs[2 * counts + 2 :]
+    picks, token_picks, of_tile, place_in_tile, tile_bias, divisor = rest[:6]
+    order, mask, arrivals = rest[6:]
+    copies = [
+        pltpu.make_async_copy(source, target, arrivals.at[k])
+        for k, (source, target) in enumerate(
+            zip((order_in, mask_in, *copied), (order, mask, *weights))
+        )
+    ]
+    for copy in copies:
+        copy.start()
+    me, model = lax.axis_index("round"), lax.axis_index("mp")
+    core, pair = model & 1, lax.shift_right_logical(model, 1)
+    cell_dev = cells // rounds
     tile_rows = rounds * cell_dev
+    share = tile_rows // 4
     total = rounds * cells
+    observables = mask.shape[0]
+
+    def slot_round(slot):
+        return me ^ slot ^ jnp.where(slot >= 2, core, 0)
+
+    for copy in copies[:2]:
+        copy.wait()
+    row = iota((total, 1), 0)
+    placed = order[...] == lax.rem(row, cells)
+    along = iota((1, cells), 1)
+    position = jnp.sum(jnp.where(placed, along, 0), axis=1, keepdims=True)
+    tile = lax.div(position, cell_dev)
+    in_tile = slot_round(lax.div(row, cells)) * cell_dev + lax.rem(position, cell_dev)
+    place_in_tile[...] = jnp.broadcast_to(in_tile.astype(jnp.float32), place_in_tile.shape)
+    of_tile[...] = one_hot(tile == slot_round(iota((1, rounds), 1)))
+    column = iota((1, total), 1)
+    along_rows = jnp.broadcast_to(along.astype(jnp.float32), (8, cells)).astype(jnp.bfloat16)
+    position_row = dot_t(along_rows, one_hot(placed))[:1].astype(jnp.int32)
+    tile_row = lax.div(position_row, cell_dev)
+    in_tile_row = slot_round(lax.div(column, cells)) * cell_dev + lax.rem(position_row, cell_dev)
+    tile_bias[...] = jnp.where(tile == tile_row, 0.0, -1e30)
+
+    index = iota((tile_rows, 1), 0)
+    quarter = lax.div(index, share)
+    target_core = jnp.where(quarter < 2, 1 - core, core)
+    target_pair = jnp.where((quarter & 1) == 0, 1 - pair, pair)
+    target = (target_pair * 2 + target_core) * share + lax.rem(index, share)
+    own = one_hot((tile_row == me) & (in_tile_row == target))
+    mask_bf = mask[...].astype(jnp.float32).astype(jnp.bfloat16)
+    support = dot(mask_bf, one_hot(iota((cells, 1), 0) == lax.rem(column, cells))).astype(
+        jnp.bfloat16
+    )
+    picks[:tile_rows] = own
+    picks[tile_rows:] = support
+    token_picks[:tile_rows] = jnp.where(quarter == 3, own, jnp.zeros_like(own))
+    token_picks[tile_rows:] = jnp.where(model == 0, support, jnp.zeros_like(support))
+    count = rounds * jnp.sum(mask[...].astype(jnp.float32), axis=1, keepdims=True)
+    divisor[...] = jnp.broadcast_to(jnp.sqrt(count), divisor.shape)
+    for copy in copies[2:]:
+        copy.wait()
+
+
+def layer_kernel(cells, slots, *refs):
+    blocks, rest = refs[:slots], refs[slots:]
+    gain, w_read, w_query, w_key, w_value, w_gate, w_up, w_down, w_out = rest[:9]
+    picks, token_picks, of_tile, place_in_tile, tile_bias, divisor, send, keep = rest[9:]
+    total = slots * cells
     width = gain.shape[1]
     head_width = w_query.shape[1]
-    observables = mask_in.shape[0]
-
-    def slot_round(slot):
-        return me ^ slot ^ jnp.where(slot >= 2, core, 0)
-
-    row = iota((total, 1), 0)
-    tile = lax.div(row, tile_rows)
-    row_in_tile = lax.rem(row, tile_rows)
-    place_in_order = tile * cell_dev + lax.rem(row_in_tile, cell_dev)
-    cell = jnp.sum(
-        jnp.where(iota((total, cells), 1) == place_in_order, order[...], 0), axis=1, keepdims=True
-    )
-    source = lax.div(row_in_tile, cell_dev) * cells + cell
-    column = iota((1, total), 1)
-    held = slot_round(lax.div(column, cells)) * cells + lax.rem(column, cells)
-    arrived = jnp.concatenate([block[0, :cells] for block in blocks], axis=0)
-    tokens = dot(one_hot(source == held), arrived).astype(jnp.bfloat16)
-    tokens_all[...] = tokens
-
-    slots_all = 2 * tiles
-    entries = jnp.concatenate([block[0, cells : cells + 1, :slots_all] for block in blocks], axis=0)
-    tile_of_slot = slot_round(iota((1, slots), 1))
-    seam_entries = dot(one_hot(tile == tile_of_slot), entries)
-    matched = seam_entries == row_in_tile.astype(jnp.float32)
-    matched_bf = one_hot(matched)
-    same_owner = one_hot(
-        lax.div(iota((slots_all, slots_all), 0), 2) == lax.div(iota((slots_all, slots_all), 1), 2)
-    )
-    seam_mask = dot_t(dot(matched_bf, same_owner).astype(jnp.bfloat16), matched_bf) > 0.5
-    in_seam = jnp.sum(jnp.where(matched, 1.0, 0.0), axis=1, keepdims=True) > 0.5
-    tile_mask = tile == lax.div(column, tile_rows)
-
+    observables = divisor.shape[0]
+    tile_rows = picks.shape[0] - observables
+
+    tokens = jnp.concatenate([block[0, :cells] for block in blocks], axis=0)
     values = tokens.astype(jnp.float32)
     spread = jnp.mean(values * values, axis=-1, keepdims=True)
     normed = (values * lax.rsqrt(spread + norm_eps) * gain[...]).astype(jnp.bfloat16)
+
+    member = jnp.zeros((total, LANES), jnp.bfloat16)
+    for row in (cells, cells + 1):
+        table = jnp.concatenate([block[0, row : row + 1, :LANES] for block in blocks], axis=0)
+        member = member + one_hot(dot(of_tile[...], table) == place_in_tile[...])
+    seam_bias = jnp.where(dot_t(member, member) > 0.5, 0.0, -1e30)
+    in_seam = jnp.sum(member.astype(jnp.float32), axis=1, keepdims=True) > 0.5
+
     queries = dot(normed, w_query[...]).astype(jnp.bfloat16)
     keys = dot(normed, w_key[...]).astype(jnp.bfloat16)
     vals = dot(normed, w_value[...]).astype(jnp.bfloat16)
+    gate = dot(normed, w_gate[...])
+    up = dot(normed, w_up[...])
+    hidden = (gate / (1.0 + jnp.exp(-gate)) * up).astype(jnp.bfloat16)
+
     scale = 1.0 / math.sqrt(HDIM)
     lane_head = lax.div(iota((1, head_width), 1), HDIM)
     local = jnp.zeros((total, head_width), jnp.float32)
@@ -221,63 +280,39 @@
         mine = lane_head == head
         scores = dot_t(queries, jnp.where(mine, keys, jnp.zeros_like(keys))) * scale
         head_vals = jnp.where(mine, vals, jnp.zeros_like(vals))
-        local = local + dot(softmax(jnp.where(tile_mask, scores, -1e30)), head_vals)
-        seam = seam + dot(softmax(jnp.where(seam_mask, scores, -1e30)), head_vals)
+        local = local + dot(softmax(scores + tile_bias[...]), head_vals)
+        seam = seam + dot(softmax(scores + seam_bias), head_vals)
     seam = seam.astype(jnp.bfloat16).astype(jnp.float32)
     combined = (local + jnp.where(in_seam, seam, 0.0)).astype(jnp.bfloat16)
-    combined_all[...] = combined
-
-    gate = dot(normed, w_gate[...])
-    up = dot(normed, w_up[...])
-    hidden = (gate / (1.0 + jnp.exp(-gate)) * up).astype(jnp.bfloat16)
-    hidden_all[...] = hidden
-
-    mask_bf = mask_in[...].astype(jnp.float32).astype(jnp.bfloat16)
-    support = dot_t(mask_bf, one_hot(iota((total, cells), 1) == cell)).astype(jnp.bfloat16)
-    own = pl.ds(pl.multiple_of(me * tile_rows, tile_rows), tile_rows)
-    hidden_rows = jnp.concatenate([hidden_all[own, :], split_three(dot(support, hidden))], axis=0)
-    combined_rows = jnp.concatenate(
-        [combined_all[own, :], split_three(dot(support, combined))], axis=0
-    )
-    product = dot(hidden_rows, w_down[...]) + dot(combined_rows, w_out[...])
-    first, second, third = (tile_rows + observables * k for k in range(3))
-    pooled = (
-        product[first : first + observables]
-        + product[second : second + observables]
-        + product[third : third + observables]
-        + jnp.where(model == 0, dot(support, tokens), 0.0)
-    )
-    count = rounds * jnp.sum(mask_in[...].astype(jnp.float32), axis=1, keepdims=True)
-    logits = jnp.sum(pooled * w_read[...], axis=1, keepdims=True) / jnp.sqrt(count)
+
+    def last_product(rows, weight):
+        own, sums = rows[:tile_rows].astype(jnp.bfloat16), split_three(rows[tile_rows:])
+        return dot(jnp.concatenate([own, sums], axis=0), weight)
+
+    product = last_product(dot(picks[...], hidden), w_down[...])
+    product = product + last_product(dot(picks[...], combined), w_out[...])
+    token_rows = dot(token_picks[...], tokens)
+    update = product[:tile_rows] + token_rows[:tile_rows]
+    pooled = token_rows[tile_rows:]
+    for k in range(3):
+        first = tile_rows + observables * k
+        pooled = pooled + product[first : first + observables]
+    logits = jnp.sum(pooled * w_read[...], axis=1, keepdims=True) / divisor[:, :1]
     diagonal = iota((observables, width), 0) == iota((observables, width), 1)
     logits_row = jnp.sum(jnp.where(diagonal, logits, 0.0), axis=0, keepdims=True)
-    logits_tile = jnp.broadcast_to(logits_row, (8, width))
-
-    pairs = send.shape[0]
-    share = tile_rows // 4
-    update = product[:tile_rows]
-    own_tokens = tokens_all[own, :].astype(jnp.float32)
-    update = update + jnp.where(lax.div(iota((tile_rows, 1), 0), share) == model, own_tokens, 0.0)
-    pair = lax.shift_right_logical(model, 1)
-    chunks = [update[share * k : share * (k + 1)] for k in range(4)]
-
-    def chunk(pair_index, core_index):
-        low = jnp.where(core_index == 0, chunks[0], chunks[1])
-        high = jnp.where(core_index == 0, chunks[2], chunks[3])
-        return jnp.where(pair_index == 0, low, high)
-
-    for target, core_index in ((send, 1 - core), (keep, core)):
-        target[:share] = chunk(1 - pair, core_index)
-        target[share : share + 8] = logits_tile
-        target[share + 8 :] = chunk(pair, core_index)
-
-
-def finish_kernel(share, own, arrived, tiles_out, logits_out):
-    cell_dev = tiles_out.shape[1]
-    rows = own[8 : 8 + share] + arrived[:share]
-    for k in range(tiles_out.shape[0]):
+    half = tile_rows // 2
+    for target, rows in ((send, update[:half]), (keep, update[half:])):
+        target[:half] = rows
+        target[half:] = jnp.broadcast_to(logits_row, (8, width))
+
+
+def finish_kernel(own, arrived, tiles_out, logits_out):
+    count, cell_dev = tiles_out.shape[:2]
+    share = count * cell_dev
+    rows = own[share : 2 * share] + arrived[:share]
+    for k in range(count):
         tiles_out[k] = rows[k * cell_dev : (k + 1) * cell_dev].astype(tiles_out.dtype)
-    logits = own[:1] + arrived[share : share + 1]
+    logits = own[2 * share : 2 * share + 1] + arrived[2 * share : 2 * share + 1]
     logits_out[...] = logits[:, : logits_out.shape[1]]
 
 
@@ -298,19 +333,30 @@
 ):
     rounds = lax.axis_size("round")
     models = lax.axis_size("mp")
-    me = lax.axis_index("round")
-    model = lax.axis_index("mp")
     cells, width = tokens.shape[1:]
     cell_dev = cells // rounds
     tile_rows = rounds * cell_dev
     share = tile_rows // models
-    core = model & 1
-
-    seam_block = jnp.pad(
-        seam_rows.reshape(1, 1, -1).astype(jnp.bfloat16),
-        ((0, 0), (0, SEAM_PAD - 1), (0, width - seam_rows.size)),
-    )
-    block = jnp.concatenate([tokens, seam_block], axis=1)
+    total = rounds * cells
+    observables = obs_mask.shape[0]
+    vmem = pl.BlockSpec(memory_space=pltpu.VMEM)
+    hbm = pl.BlockSpec(memory_space=pltpu.HBM)
+
+    def stay(arrays, space):
+        return [pltpu.with_memory_space_constraint(array, space) for array in arrays]
+
+    block = pl.pallas_call(
+        pack_kernel,
+        out_shape=pltpu.VMEM((1, cells + SEAM_PAD, width), jnp.bfloat16),
+        in_specs=[hbm, hbm],
+        out_specs=vmem,
+        scratch_shapes=[
+            pltpu.VMEM(seam_rows.shape[:0:-1], jnp.int32),
+            pltpu.VMEM((SEAM_PAD, LANES), jnp.float32),
+            pltpu.SemaphoreType.DMA((2,)),
+        ],
+        compiler_params=pltpu.CompilerParams(vmem_limit_bytes=SMALL_LIMIT),
+    )(*stay([tokens, seam_rows.transpose(0, 2, 1)], pltpu.HBM))
 
     def fetch(even_step, odd_step):
         pairs = [
@@ -323,54 +369,65 @@
     def other_core(array):
         return lax.ppermute(array, "mp", [(m, m ^ 1) for m in range(models)])
 
-    direct = {k: fetch(k, k + 1) for k in range(rounds - 2, 0, -2)}
+    direct = {k: fetch(k, k + 1) for k in range(2, rounds, 2)}
     next_door = fetch(1, 1)
     blocks = [block, next_door]
     for k in range(2, rounds, 2):
         blocks += [direct[k], other_core(direct[k])]
 
-    place = jnp.stack([me, model, core]).astype(jnp.int32)
-    vmem = pl.BlockSpec(memory_space=pltpu.VMEM)
-    smem = pl.BlockSpec(memory_space=pltpu.SMEM)
-    total = rounds * cells
-    part = jax.ShapeDtypeStruct((2 * share + 8, width), jnp.float32)
-    send, keep = pl.pallas_call(
-        functools.partial(layer_kernel, rounds, cells, len(blocks)),
-        out_shape=(part, part),
-        in_specs=[smem] + [vmem] * (len(blocks) + 11),
-        out_specs=(vmem, vmem),
-        scratch_shapes=[
-            pltpu.VMEM((total, w_gate.shape[1]), jnp.bfloat16),
-            pltpu.VMEM((total, w_query.shape[1]), jnp.bfloat16),
-            pltpu.VMEM((total, width), jnp.bfloat16),
-        ],
-        compiler_params=pltpu.CompilerParams(vmem_limit_bytes=VMEM_LIMIT),
-    )(
-        place,
-        *blocks,
-        cell_order.reshape(1, -1),
-        obs_mask,
+    brought = [
         norm_gain.reshape(1, -1),
+        w_read.reshape(1, -1),
         w_query,
         w_key,
         w_value,
-        w_out,
         w_gate,
         w_up,
         w_down,
-        w_read.reshape(1, -1),
-    )
+        w_out,
+    ]
+    prepared = pl.pallas_call(
+        functools.partial(prepare_kernel, rounds, cells, len(brought)),
+        out_shape=[pltpu.VMEM(array.shape, array.dtype) for array in brought]
+        + [
+            pltpu.VMEM((tile_rows + observables, total), jnp.bfloat16),
+            pltpu.VMEM((tile_rows + observables, total), jnp.bfloat16),
+            pltpu.VMEM((total, rounds), jnp.bfloat16),
+            pltpu.VMEM((total, LANES), jnp.float32),
+            pltpu.VMEM((total, total), jnp.float32),
+            pltpu.VMEM((observables, LANES), jnp.float32),
+        ],
+        in_specs=[hbm] * (len(brought) + 2),
+        out_specs=[vmem] * (len(brought) + 6),
+        scratch_shapes=[
+            pltpu.VMEM((1, cells), jnp.int32),
+            pltpu.VMEM(obs_mask.shape, jnp.int32),
+            pltpu.SemaphoreType.DMA((len(brought) + 2,)),
+        ],
+        compiler_params=pltpu.CompilerParams(vmem_limit_bytes=SMALL_LIMIT),
+        cost_estimate=pl.CostEstimate(flops=0, bytes_accessed=8 * 1024 * 1024, transcendentals=0),
+    )(*stay([*brought, cell_order.reshape(1, -1), obs_mask], pltpu.HBM))
+
+    part = pltpu.VMEM((2 * share + 8, width), jnp.float32)
+    send, keep = pl.pallas_call(
+        functools.partial(layer_kernel, cells, len(blocks)),
+        out_shape=(part, part),
+        in_specs=[vmem] * (len(blocks) + len(prepared)),
+        out_specs=(vmem, vmem),
+        compiler_params=pltpu.CompilerParams(vmem_limit_bytes=LAYER_LIMIT),
+    )(*stay([*blocks, *prepared], pltpu.VMEM))
     chip = keep + other_core(send)
-    arrived = lax.ppermute(chip[: share + 8], "mp", [(m, m ^ 2) for m in range(models)])
+    arrived = lax.ppermute(chip, "mp", [(m, m ^ 2) for m in range(models)])
     tiles_out, logits = pl.pallas_call(
-        functools.partial(finish_kernel, share),
+        finish_kernel,
         out_shape=(
             jax.ShapeDtypeStruct((share // cell_dev, cell_dev, width), jnp.bfloat16),
-            jax.ShapeDtypeStruct((1, obs_mask.shape[0]), jnp.float32),
+            jax.ShapeDtypeStruct((1, observables), jnp.float32),
         ),
         in_specs=[vmem, vmem],
         out_specs=(vmem, vmem),
-    )(chip[share:], arrived)
+        compiler_params=pltpu.CompilerParams(vmem_limit_bytes=SMALL_LIMIT),
+    )(*stay([chip, arrived], pltpu.VMEM))
     return tiles_out, logits.reshape(-1)
 
 

time: 32.5 us -> 22.1 us (0.68); the launches traced: 31.9 us -> 21.9 us
  local copies, waits for them, and re-layouts: 8.83 us -> 0 us
  other arithmetic: 1.53 us -> 0.01 us
  waiting for transfers between devices: 7.34 us -> 6.33 us
  Pallas kernels: 4.06 us -> 5 us
  starting transfers between devices: 9.53 us -> 9.87 us
    unnamed x24 -> x0, local copies, waits for them, and re-layouts: 8.04 us -> none
    pallas_call x2 -> x4, Pallas kernels: 4.06 us -> 5 us  [the longest x1 1.87 us: shards_whole(): pl.pallas_call(functools.partial(layer_kernel, cells, len(blocks)), out_s...]
    ppermute x4, waiting for transfers between devices: 1.71 us -> 0.89 us  [other_core(): return lax.ppermute(array, 'mp', [(m, m ^ 1) for m in range(models)])]
    concatenate x1 -> x0, other arithmetic: 0.77 us -> none  [shards_whole(): block = jnp.concatenate([tokens, seam_block], axis=1)]
    convert_element_type x1 -> x0, other arithmetic: 0.68 us -> none  [shards_whole(): seam_rows.reshape(1, 1, -1).astype(jnp.bfloat16)]
    slice x1 -> x0, local copies, waits for them, and re-layouts: 0.61 us -> none  [shards_whole(): chip[:share + 8]]
    ppermute x4, waiting for transfers between devices: 3.21 us -> 2.84 us  [fetch(): return lax.ppermute(block, ('round', 'mp'), pairs)]
  transfers between devices with their start and end apart: 9 -> 9, of which waited for: 7 -> 4; matrix products, arithmetic and copies ran while one was open for 0% -> 0% of each run, Pallas kernels for 0% -> 8%
where the time goes in v2:
time: 22.1 us; the launch traced here: 21.9 us
  starting transfers between devices  9.87 us (45%)
  waiting for transfers between devices  6.33 us (29%)
  Pallas kernels  5 us (23%)
  between operations  0.69 us (3%)
    ppermute x4, starting transfers between devices, fetch(): return lax.ppermute(block, ('round', 'mp'), pairs)  7.42 us
    ppermute x4, waiting for transfers between devices, fetch(): return lax.ppermute(block, ('round', 'mp'), pairs)  2.84 us
    ppermute x1, waiting for transfers between devices, shards_whole(): arrived = lax.ppermute(chip, 'mp', [(m, m ^ 2) for m in range(models)])  2.6 us
    pallas_call x1, Pallas kernels, shards_whole(): pl.pallas_call(functools.partial(layer_kernel, cells, len(blocks)), out_s...  1.87 us
    pallas_call x1, Pallas kernels, shards_whole(): pl.pallas_call(functools.partial(prepare_kernel, rounds, cells, len(broug...  1.72 us
    ppermute x1, starting transfers between devices, shards_whole(): arrived = lax.ppermute(chip, 'mp', [(m, m ^ 2) for m in range(models)])  1.56 us
    ppermute x4, starting transfers between devices, other_core(): return lax.ppermute(array, 'mp', [(m, m ^ 1) for m in range(models)])  0.89 us
    ppermute x4, waiting for transfers between devices, other_core(): return lax.ppermute(array, 'mp', [(m, m ^ 1) for m in range(models)])  0.89 us
  transfers between devices with their start and end apart: 9, of which 4 were waited for; matrix products, arithmetic and copies ran while one was open for 0% of the time, Pallas kernels for 8%

profile of v2, /device:TPU:0, one launch (start us, length us, event | category | flops | bytes accessed | tf_op | source)
XLA Modules:
  0.0 21.9 jit_solution(16037373381722947978)
XLA Ops:
  0.6 0.8 %shard_map.140.refs_0_ = bf16[1,48,512]{2,1,0:T(8,128)(2,1)S(1)} custom-call(bf16[1,32,512]{2,1,0:T(8,128)(2,1)} %tokens.1, s32[1,2,8]{2,1,0:T(2,128)} %bitcast.7), custom_call_target="tpu_custom_call" | custom-call | tf_op jit(solution)/shard_map/pallas_call | solution.py:348
  1.4 5.1 %collective-permute-start.5 = (bf16[1,48,512]{2,1,0:T(8,128)(2,1)S(1)}, bf16[1,48,512]{2,1,0:T(8,128)(2,1)S(1)}, u32[]{:S(2)}, u32[]{:S(2)}) collective-permute-start(bf16[1,48,512]{2,1,0:T(8,128)(2,1)S(1)} %shard_map.140.refs_0_), channel_id=1, source_target_pairs={{0,24},{1,29},{2,26},{3,31},{4,28},{5,25},{6,30},{7,27},{8,16},{9,... | collective-permute-start | bytes 147464 | tf_op jit(solution)/shard_map/ppermute | solution.py:367
  6.5 0.0 collective-permute-start.3
  6.5 0.6 %collective-permute-start.1 = (bf16[1,48,512]{2,1,0:T(8,128)(2,1)S(1)}, bf16[1,48,512]{2,1,0:T(8,128)(2,1)S(1)}, u32[]{:S(2)}, u32[]{:S(2)}) collective-permute-start(bf16[1,48,512]{2,1,0:T(8,128)(2,1)S(1)} %shard_map.140.refs_0_), channel_id=1, source_target_pairs={{0,8},{1,13},{2,10},{3,15},{4,12},{5,9},{6,14},{7,11},{8,0},{9,5},... | collective-permute-start | bytes 147464 | tf_op jit(solution)/shard_map/ppermute | solution.py:367
  7.2 1.7 %collective-permute-start = (bf16[1,48,512]{2,1,0:T(8,128)(2,1)S(1)}, bf16[1,48,512]{2,1,0:T(8,128)(2,1)S(1)}, u32[]{:S(2)}, u32[]{:S(2)}) collective-permute-start(bf16[1,48,512]{2,1,0:T(8,128)(2,1)S(1)} %shard_map.140.refs_0_), channel_id=1, source_target_pairs={{0,4},{1,5},{2,6},{3,7},{4,0},{5,1},{6,2},{7,3},{8,12},{9,13},{10,... | collective-permute-start | bytes 147464 | tf_op jit(solution)/shard_map/ppermute | solution.py:367
  8.9 0.4 %collective-permute-done.5.refs_6_ = bf16[1,48,512]{2,1,0:T(8,128)(2,1)S(1)} collective-permute-done((bf16[1,48,512]{2,1,0:T(8,128)(2,1)S(1)}, bf16[1,48,512]{2,1,0:T(8,128)(2,1)S(1)}, u32[]{:S(2)}, u32[]{:S(2)}) %collective-permute-start.5) | collective-permute-done | bytes 49184 | tf_op jit(solution)/shard_map/ppermute | solution.py:367
  9.2 0.0 collective-permute-start.6
  9.2 2.5 %collective-permute-done.3.refs_4_ = bf16[1,48,512]{2,1,0:T(8,128)(2,1)S(1)} collective-permute-done((bf16[1,48,512]{2,1,0:T(8,128)(2,1)S(1)}, bf16[1,48,512]{2,1,0:T(8,128)(2,1)S(1)}, u32[]{:S(2)}, u32[]{:S(2)}) %collective-permute-start.3) | collective-permute-done | bytes 49184 | tf_op jit(solution)/shard_map/ppermute | solution.py:367
  11.7 0.4 %collective-permute-start.4 = (bf16[1,48,512]{2,1,0:T(8,128)(2,1)S(1)}, bf16[1,48,512]{2,1,0:T(8,128)(2,1)S(1)}, u32[]{:S(2)}, u32[]{:S(2)}) collective-permute-start(bf16[1,48,512]{2,1,0:T(8,128)(2,1)S(1)} %collective-permute-done.3.refs_4_), channel_id=1, source_target_pairs={{0,1},{1,0},{2,3},{3,2},{4,5},{5,4},{6,7},{7,6},{8,9},{9,8},{10,11... | collective-permute-start | bytes 147464 | tf_op jit(solution)/shard_map/ppermute | solution.py:370
  12.1 0.0 collective-permute-done.1.refs_2_
  12.1 0.1 collective-permute-start.2
  12.2 1.7 %shard_map.141 = (f32[1,512]{1,0:T(1,128)S(1)}, f32[1,512]{1,0:T(1,128)S(1)}, bf16[512,128]{1,0:T(8,128)(2,1)S(1)}, bf16[512,128]{1,0:T(8,128)(2,1)S(1)}, bf16[5...) custom-call(f32[1,512]{1,0:T(1,128)} %bitcast.5, ...), custom_call_target="tpu_custom_call" | custom-call | bytes 8388608 | tf_op jit(solution)/shard_map/pallas_call | solution.py:389
  13.9 0.0 collective-permute-done.refs_1_
  13.9 0.0 collective-permute-done.6.refs_7_
  14.0 0.0 collective-permute-done.4.refs_5_
  14.0 0.0 collective-permute-done.2.refs_3_
  14.0 1.9 %shard_map.142 = (f32[24,512]{1,0:T(8,128)S(1)}, f32[24,512]{1,0:T(8,128)S(1)}) custom-call(bf16[1,48,512]{2,1,0:T(8,128)(2,1)S(1)} %shard_map.140.refs_0_, bf16[1,48,512]{2,1,0:T(8,128)(2,1)S(1)} %collective-permute-done.refs_1_, bf16[1,48,512]{2,1,0:T(8,128)(2,1)S(1)} %collective-permute-done.1.refs_2_, ...), custom_call_target="tpu_custom_call" | custom-call | tf_op jit(solution)/shard_map/pallas_call | solution.py:412
  15.9 0.4 %collective-permute-start.7 = (f32[24,512]{1,0:T(8,128)S(1)}, f32[24,512]{1,0:T(8,128)S(1)}, u32[]{:S(2)}, u32[]{:S(2)}) collective-permute-start(f32[24,512]{1,0:T(8,128)S(1)} %get-tuple-element.37), channel_id=1, source_target_pairs={{0,1},{1,0},{2,3},{3,2},{4,5},{5,4},{6,7},{7,6},{8,9},{9,8},{10,11... | collective-permute-start | bytes 147464 | tf_op jit(solution)/shard_map/ppermute | solution.py:370
  16.2 0.9 %collective-permute-done.7 = f32[24,512]{1,0:T(8,128)S(1)} collective-permute-done((f32[24,512]{1,0:T(8,128)S(1)}, f32[24,512]{1,0:T(8,128)S(1)}, u32[]{:S(2)}, u32[]{:S(2)}) %collective-permute-start.7) | collective-permute-done | bytes 49184 | tf_op jit(solution)/shard_map/ppermute | solution.py:370
  17.1 1.6 %collective-permute-start.8 = (f32[24,512]{1,0:T(8,128)S(1)}, f32[24,512]{1,0:T(8,128)S(1)}, u32[]{:S(2)}, u32[]{:S(2)}) collective-permute-start(f32[24,512]{1,0:T(8,128)S(1)} %add.3.own), channel_id=1, source_target_pairs={{0,2},{1,3},{2,0},{3,1},{4,6},{5,7},{6,4},{7,5},{8,10},{9,11},{10,... | collective-permute-start | bytes 147464 | tf_op jit(solution)/shard_map/ppermute | solution.py:420
  18.7 2.6 %collective-permute-done.8.arrived = f32[24,512]{1,0:T(8,128)S(1)} collective-permute-done((f32[24,512]{1,0:T(8,128)S(1)}, f32[24,512]{1,0:T(8,128)S(1)}, u32[]{:S(2)}, u32[]{:S(2)}) %collective-permute-start.8) | collective-permute-done | bytes 49184 | tf_op jit(solution)/shard_map/ppermute | solution.py:420
  21.3 0.6 %shard_map.143 = (bf16[2,4,512]{2,1,0:T(4,128)(2,1)}, f32[1,16]{1,0:T(1,128)}) custom-call(f32[24,512]{1,0:T(8,128)S(1)} %add.3.own, f32[24,512]{1,0:T(8,128)S(1)} %collective-permute-done.8.arrived), custom_call_target="tpu_custom_call" | custom-call | tf_op jit(solution)/shard_map/pallas_call | solution.py:421
  (1 shorter events, 0.0 us)
Async XLA Ops:
  1.4 7.8 %collective-permute-start.5 = (bf16[1,48,512]{2,1,0:T(8,128)(2,1)S(1)}, bf16[1,48,512]{2,1,0:T(8,128)(2,1)S(1)}, u32[]{:S(2)}, u32[]{:S(2)}) collective-permute-start(bf16[1,48,512]{2,1,0:T(8,128)(2,1)S(1)} %shard_map.140.refs_0_), channel_id=1, source_target_pairs={{0,24},{1,29},{2,26},{3,31},{4,28},{5,25},{6,30},{7,27},{8,16},{9,... | collective-permute-start | bytes 147464 | tf_op jit(solution)/shard_map/ppermute | solution.py:367
  6.5 5.1 %collective-permute-start.3 = (bf16[1,48,512]{2,1,0:T(8,128)(2,1)S(1)}, bf16[1,48,512]{2,1,0:T(8,128)(2,1)S(1)}, u32[]{:S(2)}, u32[]{:S(2)}) collective-permute-start(bf16[1,48,512]{2,1,0:T(8,128)(2,1)S(1)} %shard_map.140.refs_0_), channel_id=1, source_target_pairs={{0,16},{1,21},{2,18},{3,23},{4,20},{5,17},{6,22},{7,19},{8,24},{9,... | collective-permute-start | bytes 147464 | tf_op jit(solution)/shard_map/ppermute | solution.py:367
  6.5 5.5 %collective-permute-start.1 = (bf16[1,48,512]{2,1,0:T(8,128)(2,1)S(1)}, bf16[1,48,512]{2,1,0:T(8,128)(2,1)S(1)}, u32[]{:S(2)}, u32[]{:S(2)}) collective-permute-start(bf16[1,48,512]{2,1,0:T(8,128)(2,1)S(1)} %shard_map.140.refs_0_), channel_id=1, source_target_pairs={{0,8},{1,13},{2,10},{3,15},{4,12},{5,9},{6,14},{7,11},{8,0},{9,5},... | collective-permute-start | bytes 147464 | tf_op jit(solution)/shard_map/ppermute | solution.py:367
  7.2 6.8 %collective-permute-start = (bf16[1,48,512]{2,1,0:T(8,128)(2,1)S(1)}, bf16[1,48,512]{2,1,0:T(8,128)(2,1)S(1)}, u32[]{:S(2)}, u32[]{:S(2)}) collective-permute-start(bf16[1,48,512]{2,1,0:T(8,128)(2,1)S(1)} %shard_map.140.refs_0_), channel_id=1, source_target_pairs={{0,4},{1,5},{2,6},{3,7},{4,0},{5,1},{6,2},{7,3},{8,12},{9,13},{10,... | collective-permute-start | bytes 147464 | tf_op jit(solution)/shard_map/ppermute | solution.py:367
  9.2 4.7 %collective-permute-start.6 = (bf16[1,48,512]{2,1,0:T(8,128)(2,1)S(1)}, bf16[1,48,512]{2,1,0:T(8,128)(2,1)S(1)}, u32[]{:S(2)}, u32[]{:S(2)}) collective-permute-start(bf16[1,48,512]{2,1,0:T(8,128)(2,1)S(1)} %collective-permute-done.5.refs_6_), channel_id=1, source_target_pairs={{0,1},{1,0},{2,3},{3,2},{4,5},{5,4},{6,7},{7,6},{8,9},{9,8},{10,11... | collective-permute-start | bytes 147464 | tf_op jit(solution)/shard_map/ppermute | solution.py:370
  11.7 2.3 %collective-permute-start.4 = (bf16[1,48,512]{2,1,0:T(8,128)(2,1)S(1)}, bf16[1,48,512]{2,1,0:T(8,128)(2,1)S(1)}, u32[]{:S(2)}, u32[]{:S(2)}) collective-permute-start(bf16[1,48,512]{2,1,0:T(8,128)(2,1)S(1)} %collective-permute-done.3.refs_4_), channel_id=1, source_target_pairs={{0,1},{1,0},{2,3},{3,2},{4,5},{5,4},{6,7},{7,6},{8,9},{9,8},{10,11... | collective-permute-start | bytes 147464 | tf_op jit(solution)/shard_map/ppermute | solution.py:370
  12.1 1.9 %collective-permute-start.2 = (bf16[1,48,512]{2,1,0:T(8,128)(2,1)S(1)}, bf16[1,48,512]{2,1,0:T(8,128)(2,1)S(1)}, u32[]{:S(2)}, u32[]{:S(2)}) collective-permute-start(bf16[1,48,512]{2,1,0:T(8,128)(2,1)S(1)} %collective-permute-done.1.refs_2_), channel_id=1, source_target_pairs={{0,1},{1,0},{2,3},{3,2},{4,5},{5,4},{6,7},{7,6},{8,9},{9,8},{10,11... | collective-permute-start | bytes 147464 | tf_op jit(solution)/shard_map/ppermute | solution.py:370
  15.9 1.3 %collective-permute-start.7 = (f32[24,512]{1,0:T(8,128)S(1)}, f32[24,512]{1,0:T(8,128)S(1)}, u32[]{:S(2)}, u32[]{:S(2)}) collective-permute-start(f32[24,512]{1,0:T(8,128)S(1)} %get-tuple-element.37), channel_id=1, source_target_pairs={{0,1},{1,0},{2,3},{3,2},{4,5},{5,4},{6,7},{7,6},{8,9},{9,8},{10,11... | collective-permute-start | bytes 147464 | tf_op jit(solution)/shard_map/ppermute | solution.py:370
  17.1 4.2 %collective-permute-start.8 = (f32[24,512]{1,0:T(8,128)S(1)}, f32[24,512]{1,0:T(8,128)S(1)}, u32[]{:S(2)}, u32[]{:S(2)}) collective-permute-start(f32[24,512]{1,0:T(8,128)S(1)} %add.3.own), channel_id=1, source_target_pairs={{0,2},{1,3},{2,0},{3,1},{4,6},{5,7},{6,4},{7,5},{8,10},{9,11},{10,... | collective-permute-start | bytes 147464 | tf_op jit(solution)/shard_map/ppermute | solution.py:420

commit v3 on v2

--- a/solution.py
+++ b/solution.py
@@ -9,9 +9,9 @@
 from jax.sharding import PartitionSpec as P
 
 HDIM = 64
-SEAM_PAD = 16
 LANES = 128
 SMALL_LIMIT = 8 * 1024 * 1024
+TIED = 0
 LAYER_LIMIT = 32 * 1024 * 1024
 
 
@@ -162,36 +162,64 @@
 
 
 def softmax(scores):
-    weights = jnp.exp(scores - jnp.max(scores, axis=-1, keepdims=True))
-    return (weights / jnp.sum(weights, axis=-1, keepdims=True)).astype(jnp.bfloat16)
-
-
-def pack_kernel(tokens, seam_rows, block, landed, padded, arrivals):
-    cells = tokens.shape[1]
+    weights = jnp.exp(scores - jnp.max(scores, axis=0, keepdims=True))
+    return (weights / jnp.sum(weights, axis=0, keepdims=True)).astype(jnp.bfloat16)
+
+
+def fetch_steps(rounds):
+    shifts = [2, *range(rounds - 2, 2, -2)]
+    return [((k, 0), (k, 1)) for k in shifts] + [((0, 1), (0, 1))]
+
+
+def slot_steps(rounds):
+    steps = [((0, 0), (0, 0))]
+    for even, odd in fetch_steps(rounds):
+        steps += [(even, odd)] if even == odd else [(even, odd), (odd, even)]
+    return steps
+
+
+def pack_kernel(prepare, given, made, tokens, seam_rows, *refs):
+    block, (landed, padded, arrivals) = refs[given], refs[-3:]
+    width = tokens.shape[2]
     slots, owners = seam_rows.shape[1:]
     copies = [
         pltpu.make_async_copy(seam_rows.at[0], landed, arrivals.at[0]),
-        pltpu.make_async_copy(tokens, block.at[:, :cells], arrivals.at[1]),
+        pltpu.make_async_copy(tokens, block.at[:, :, :width], arrivals.at[1]),
     ]
     for copy in copies:
         copy.start()
-    padded[...] = jnp.full(padded.shape, -1.0, jnp.float32)
+    padded[...] = jnp.zeros(padded.shape, jnp.float32)
     copies[0].wait()
-    padded[:slots, :owners] = landed[...].astype(jnp.float32)
-    block[0, cells:, :LANES] = padded[...].astype(jnp.bfloat16)
+    row = iota((tokens.shape[1], owners), 0)
+    held = row == landed[:1]
+    for slot in range(1, slots):
+        held = held | (row == landed[slot : slot + 1])
+    padded[:, :owners] = jnp.where(held, 1.0, 0.0)
+    block[0, :, width:] = padded[...].astype(jnp.bfloat16)
     copies[1].wait()
 
-
-def prepare_kernel(rounds, cells, counts, *refs):
-    copied, order_in, mask_in = refs[:counts], refs[counts], refs[counts + 1]
-    weights, rest = refs[counts + 2 : 2 * counts + 2], refs[2 * counts + 2 :]
-    picks, token_picks, of_tile, place_in_tile, tile_bias, divisor = rest[:6]
-    order, mask, arrivals = rest[6:]
+    @pl.when(lax.axis_index("round") == 0)
+    def _():
+        prepare(*refs[:given], *refs[given + 1 : given + 1 + made], *refs[given + 1 + made : -3])
+
+
+def late_kernel(prepare, given, made, *refs):
+    @pl.when(lax.axis_index("round") != 0)
+    def _():
+        prepare(*refs[:given], *refs[given + made :])
+
+
+def prepare(rounds, cells, counts, *refs):
+    order_in, mask_in, *copied = refs[: counts + 2]
+    rest = refs[counts + 2 :]
+    gain, w_read, w_query, w_key, w_gate, w_up, w_down, w_out = rest[:8]
+    w_value_t, read_down, read_out = rest[8:11]
+    picks, token_picks, place, tile_bias, divisor = rest[11:16]
+    order, mask, w_value, arrivals = rest[16:]
+    targets = (order, mask, gain, w_read, w_value, w_query, w_key, w_gate, w_up, w_down, w_out)
     copies = [
         pltpu.make_async_copy(source, target, arrivals.at[k])
-        for k, (source, target) in enumerate(
-            zip((order_in, mask_in, *copied), (order, mask, *weights))
-        )
+        for k, (source, target) in enumerate(zip((order_in, mask_in, *copied), targets))
     ]
     for copy in copies:
         copy.start()
@@ -204,7 +232,11 @@
     observables = mask.shape[0]
 
     def slot_round(slot):
-        return me ^ slot ^ jnp.where(slot >= 2, core, 0)
+        shift, flip = jnp.zeros_like(slot), jnp.zeros_like(slot)
+        for k, (even, odd) in enumerate(slot_steps(rounds)):
+            shift = jnp.where(slot == k, jnp.where(core == 0, even[0], odd[0]), shift)
+            flip = jnp.where(slot == k, jnp.where(core == 0, even[1], odd[1]), flip)
+        return ((me + rounds - shift) & (rounds - 1)) ^ flip
 
     for copy in copies[:2]:
         copy.wait()
@@ -214,9 +246,9 @@
     position = jnp.sum(jnp.where(placed, along, 0), axis=1, keepdims=True)
     tile = lax.div(position, cell_dev)
     in_tile = slot_round(lax.div(row, cells)) * cell_dev + lax.rem(position, cell_dev)
-    place_in_tile[...] = jnp.broadcast_to(in_tile.astype(jnp.float32), place_in_tile.shape)
-    of_tile[...] = one_hot(tile == slot_round(iota((1, rounds), 1)))
     column = iota((1, total), 1)
+    slot_start = slot_round(lax.div(column, cells)) * tile_rows
+    place[...] = one_hot(tile * tile_rows + in_tile == slot_start + lax.rem(column, cells))
     along_rows = jnp.broadcast_to(along.astype(jnp.float32), (8, cells)).astype(jnp.bfloat16)
     position_row = dot_t(along_rows, one_hot(placed))[:1].astype(jnp.int32)
     tile_row = lax.div(position_row, cell_dev)
@@ -239,80 +271,99 @@
     token_picks[tile_rows:] = jnp.where(model == 0, support, jnp.zeros_like(support))
     count = rounds * jnp.sum(mask[...].astype(jnp.float32), axis=1, keepdims=True)
     divisor[...] = jnp.broadcast_to(jnp.sqrt(count), divisor.shape)
-    for copy in copies[2:]:
+
+    for copy in copies[2:5]:
         copy.wait()
+    head_width = w_value.shape[1]
+    identity = one_hot(iota((head_width, 1), 0) == iota((1, head_width), 1))
+    w_value_t[...] = dot_t(identity, w_value[...]).astype(jnp.bfloat16)
+    read_parts = split_three(jnp.broadcast_to(w_read[...], (8, w_read.shape[1])))
+    for copy in copies[5:]:
+        copy.wait()
+    for weight, read in ((w_down, read_down), (w_out, read_out)):
+        parts = dot_t(read_parts, weight[...])
+        read[...] = parts[:1] + parts[8:9] + parts[16:17]
 
 
 def layer_kernel(cells, slots, *refs):
     blocks, rest = refs[:slots], refs[slots:]
-    gain, w_read, w_query, w_key, w_value, w_gate, w_up, w_down, w_out = rest[:9]
-    picks, token_picks, of_tile, place_in_tile, tile_bias, divisor, send, keep = rest[9:]
+    gain, w_read, w_query, w_key, w_gate, w_up, w_down, w_out = rest[:8]
+    w_value_t, read_down, read_out = rest[8:11]
+    picks, token_picks, place, tile_bias, divisor = rest[11:16]
+    outs = rest[16:]
     total = slots * cells
     width = gain.shape[1]
     head_width = w_query.shape[1]
     observables = divisor.shape[0]
     tile_rows = picks.shape[0] - observables
 
-    tokens = jnp.concatenate([block[0, :cells] for block in blocks], axis=0)
+    tokens = jnp.concatenate([block[0, :, :width] for block in blocks], axis=0)
     values = tokens.astype(jnp.float32)
     spread = jnp.mean(values * values, axis=-1, keepdims=True)
     normed = (values * lax.rsqrt(spread + norm_eps) * gain[...]).astype(jnp.bfloat16)
 
-    member = jnp.zeros((total, LANES), jnp.bfloat16)
-    for row in (cells, cells + 1):
-        table = jnp.concatenate([block[0, row : row + 1, :LANES] for block in blocks], axis=0)
-        member = member + one_hot(dot(of_tile[...], table) == place_in_tile[...])
+    members = jnp.concatenate([block[0, :, width:] for block in blocks], axis=0)
+    member = dot(place[...], members).astype(jnp.bfloat16)
     seam_bias = jnp.where(dot_t(member, member) > 0.5, 0.0, -1e30)
-    in_seam = jnp.sum(member.astype(jnp.float32), axis=1, keepdims=True) > 0.5
-
-    queries = dot(normed, w_query[...]).astype(jnp.bfloat16)
-    keys = dot(normed, w_key[...]).astype(jnp.bfloat16)
-    vals = dot(normed, w_value[...]).astype(jnp.bfloat16)
+    in_seam = dot_t(jnp.ones((8, LANES), jnp.bfloat16), member)[:1] > 0.5
+
     gate = dot(normed, w_gate[...])
     up = dot(normed, w_up[...])
     hidden = (gate / (1.0 + jnp.exp(-gate)) * up).astype(jnp.bfloat16)
 
-    scale = 1.0 / math.sqrt(HDIM)
+    queries = (dot(normed, w_query[...]) * (1.0 / math.sqrt(HDIM))).astype(jnp.bfloat16)
+    keys = dot(normed, w_key[...]).astype(jnp.bfloat16)
+    vals = dot_t(w_value_t[...], normed).astype(jnp.bfloat16)
     lane_head = lax.div(iota((1, head_width), 1), HDIM)
-    local = jnp.zeros((total, head_width), jnp.float32)
-    seam = jnp.zeros((total, head_width), jnp.float32)
+    heads = []
     for head in range(head_width // HDIM):
-        mine = lane_head == head
-        scores = dot_t(queries, jnp.where(mine, keys, jnp.zeros_like(keys))) * scale
-        head_vals = jnp.where(mine, vals, jnp.zeros_like(vals))
-        local = local + dot(softmax(scores + tile_bias[...]), head_vals)
-        seam = seam + dot(softmax(scores + seam_bias), head_vals)
-    seam = seam.astype(jnp.bfloat16).astype(jnp.float32)
-    combined = (local + jnp.where(in_seam, seam, 0.0)).astype(jnp.bfloat16)
-
-    def last_product(rows, weight):
-        own, sums = rows[:tile_rows].astype(jnp.bfloat16), split_three(rows[tile_rows:])
-        return dot(jnp.concatenate([own, sums], axis=0), weight)
-
-    product = last_product(dot(picks[...], hidden), w_down[...])
-    product = product + last_product(dot(picks[...], combined), w_out[...])
+        head_keys = jnp.where(lane_head == head, keys, jnp.zeros_like(keys))
+        head_vals = vals[head * HDIM : (head + 1) * HDIM]
+        parts = []
+        for first in range(0, total, LANES):
+            some = slice(first, first + LANES)
+            scores = dot_t(head_keys, queries[some])
+            local = dot(head_vals, softmax(scores + tile_bias[:, some]))
+            seam = dot(head_vals, softmax(scores + seam_bias[:, some]))
+            seam = seam.astype(jnp.bfloat16).astype(jnp.float32)
+            parts.append((local + jnp.where(in_seam[:, some], seam, 0.0)).astype(jnp.bfloat16))
+        heads.append(jnp.concatenate(parts, axis=1))
+    combined = jnp.concatenate(heads, axis=0)
+
+    hidden_rows = dot(picks[...], hidden)
+    combined_rows = dot_t(picks[...], combined)
     token_rows = dot(token_picks[...], tokens)
-    update = product[:tile_rows] + token_rows[:tile_rows]
-    pooled = token_rows[tile_rows:]
-    for k in range(3):
-        first = tile_rows + observables * k
-        pooled = pooled + product[first : first + observables]
-    logits = jnp.sum(pooled * w_read[...], axis=1, keepdims=True) / divisor[:, :1]
-    diagonal = iota((observables, width), 0) == iota((observables, width), 1)
+    update = (
+        token_rows[:tile_rows]
+        + dot(hidden_rows[:tile_rows].astype(jnp.bfloat16), w_down[...])
+        + dot(combined_rows[:tile_rows].astype(jnp.bfloat16), w_out[...])
+    )
+    logits = sum(
+        jnp.sum(sums[tile_rows:] * read[...], axis=1, keepdims=True)
+        for sums, read in (
+            (hidden_rows, read_down),
+            (combined_rows, read_out),
+            (token_rows, w_read),
+        )
+    )
+    logits = logits / divisor[:, :1]
+    diagonal = iota((observables, LANES), 0) == iota((observables, LANES), 1)
     logits_row = jnp.sum(jnp.where(diagonal, logits, 0.0), axis=0, keepdims=True)
-    half = tile_rows // 2
-    for target, rows in ((send, update[:half]), (keep, update[half:])):
-        target[:half] = rows
-        target[half:] = jnp.broadcast_to(logits_row, (8, width))
-
-
-def finish_kernel(own, arrived, tiles_out, logits_out):
+    share = tile_rows // 4
+    send_over, send_stay, keep_over, keep_stay = outs
+    for k, (over, stay) in enumerate(((send_over, send_stay), (keep_over, keep_stay))):
+        over[:, :width] = update[2 * k * share : (2 * k + 1) * share]
+        over[:, width:] = jnp.broadcast_to(logits_row, (share, LANES))
+        stay[...] = update[(2 * k + 1) * share : (2 * k + 2) * share]
+
+
+def finish_kernel(over, arrived, stay, other_stay, tiles_out, logits_out):
     count, cell_dev = tiles_out.shape[:2]
-    share = count * cell_dev
-    rows = own[share : 2 * share] + arrived[:share]
+    width = stay.shape[1]
+    rows = stay[...] + other_stay[...] + arrived[:, :width]
     for k in range(count):
         tiles_out[k] = rows[k * cell_dev : (k + 1) * cell_dev].astype(tiles_out.dtype)
-    logits = own[2 * share : 2 * share + 1] + arrived[2 * share : 2 * share + 1]
+    logits = over[:1, width:] + arrived[:1, width:]
     logits_out[...] = logits[:, : logits_out.shape[1]]
 
 
@@ -342,92 +393,103 @@
     vmem = pl.BlockSpec(memory_space=pltpu.VMEM)
     hbm = pl.BlockSpec(memory_space=pltpu.HBM)
 
-    def stay(arrays, space):
+    def pin(arrays, space):
         return [pltpu.with_memory_space_constraint(array, space) for array in arrays]
-
-    block = pl.pallas_call(
-        pack_kernel,
-        out_shape=pltpu.VMEM((1, cells + SEAM_PAD, width), jnp.bfloat16),
-        in_specs=[hbm, hbm],
-        out_specs=vmem,
-        scratch_shapes=[
-            pltpu.VMEM(seam_rows.shape[:0:-1], jnp.int32),
-            pltpu.VMEM((SEAM_PAD, LANES), jnp.float32),
-            pltpu.SemaphoreType.DMA((2,)),
-        ],
-        compiler_params=pltpu.CompilerParams(vmem_limit_bytes=SMALL_LIMIT),
-    )(*stay([tokens, seam_rows.transpose(0, 2, 1)], pltpu.HBM))
-
-    def fetch(even_step, odd_step):
-        pairs = [
-            (r * models + m, (r ^ (odd_step if m & 1 else even_step)) * models + m)
-            for r in range(rounds)
-            for m in range(models)
-        ]
-        return lax.ppermute(block, ("round", "mp"), pairs)
-
-    def other_core(array):
-        return lax.ppermute(array, "mp", [(m, m ^ 1) for m in range(models)])
-
-    direct = {k: fetch(k, k + 1) for k in range(2, rounds, 2)}
-    next_door = fetch(1, 1)
-    blocks = [block, next_door]
-    for k in range(2, rounds, 2):
-        blocks += [direct[k], other_core(direct[k])]
 
     brought = [
         norm_gain.reshape(1, -1),
         w_read.reshape(1, -1),
+        w_value,
         w_query,
         w_key,
-        w_value,
         w_gate,
         w_up,
         w_down,
         w_out,
     ]
+    sources = pin([cell_order.reshape(1, -1), obs_mask, *brought], pltpu.HBM)
+    made = [pltpu.VMEM(array.shape, array.dtype) for k, array in enumerate(brought) if k != 2] + [
+        pltpu.VMEM(w_value.shape[::-1], w_value.dtype),
+        pltpu.VMEM((1, w_down.shape[0]), jnp.float32),
+        pltpu.VMEM((1, w_out.shape[0]), jnp.float32),
+        pltpu.VMEM((tile_rows + observables, total), jnp.bfloat16),
+        pltpu.VMEM((tile_rows + observables, total), jnp.bfloat16),
+        pltpu.VMEM((total, total), jnp.bfloat16),
+        pltpu.VMEM((total, total), jnp.float32),
+        pltpu.VMEM((observables, LANES), jnp.float32),
+    ]
+    scratch = [
+        pltpu.VMEM((1, cells), jnp.int32),
+        pltpu.VMEM(obs_mask.shape, jnp.int32),
+        pltpu.VMEM(w_value.shape, w_value.dtype),
+        pltpu.SemaphoreType.DMA((len(sources),)),
+    ]
+    small = pltpu.CompilerParams(vmem_limit_bytes=SMALL_LIMIT)
+    preparation = functools.partial(prepare, rounds, cells, len(brought))
+    block, *prepared = pl.pallas_call(
+        functools.partial(pack_kernel, preparation, len(sources), len(made)),
+        out_shape=[pltpu.VMEM((1, cells, width + LANES), jnp.bfloat16), *made],
+        in_specs=[hbm] * (len(sources) + 2),
+        out_specs=[vmem] * (len(made) + 1),
+        scratch_shapes=[
+            *scratch,
+            pltpu.VMEM(seam_rows.shape[:0:-1], jnp.int32),
+            pltpu.VMEM((cells, LANES), jnp.float32),
+            pltpu.SemaphoreType.DMA((2,)),
+        ],
+        compiler_params=small,
+    )(*pin([tokens, seam_rows.transpose(0, 2, 1)], pltpu.HBM), *sources)
+
+    def fetch(even, odd):
+        pairs = []
+        for r in range(rounds):
+            for m in range(models):
+                shift, flip = odd if m & 1 else even
+                pairs.append(((((r - shift) % rounds) ^ flip) * models + m, r * models + m))
+        return lax.ppermute(block, ("round", "mp"), pairs)
+
+    def other_core(array):
+        return lax.ppermute(array, "mp", [(m, m ^ 1) for m in range(models)])
+
+    direct = [fetch(even, odd) for even, odd in fetch_steps(rounds)]
     prepared = pl.pallas_call(
-        functools.partial(prepare_kernel, rounds, cells, len(brought)),
-        out_shape=[pltpu.VMEM(array.shape, array.dtype) for array in brought]
-        + [
-            pltpu.VMEM((tile_rows + observables, total), jnp.bfloat16),
-            pltpu.VMEM((tile_rows + observables, total), jnp.bfloat16),
-            pltpu.VMEM((total, rounds), jnp.bfloat16),
-            pltpu.VMEM((total, LANES), jnp.float32),
-            pltpu.VMEM((total, total), jnp.float32),
-            pltpu.VMEM((observables, LANES), jnp.float32),
-        ],
-        in_specs=[hbm] * (len(brought) + 2),
-        out_specs=[vmem] * (len(brought) + 6),
-        scratch_shapes=[
-            pltpu.VMEM((1, cells), jnp.int32),
-            pltpu.VMEM(obs_mask.shape, jnp.int32),
-            pltpu.SemaphoreType.DMA((len(brought) + 2,)),
-        ],
-        compiler_params=pltpu.CompilerParams(vmem_limit_bytes=SMALL_LIMIT),
+        functools.partial(late_kernel, preparation, len(sources), len(made)),
+        out_shape=made,
+        in_specs=[hbm] * len(sources) + [vmem] * len(made),
+        out_specs=[vmem] * len(made),
+        input_output_aliases={len(sources) + k: k for k in range(len(made))},
+        scratch_shapes=scratch,
+        compiler_params=small,
         cost_estimate=pl.CostEstimate(flops=0, bytes_accessed=8 * 1024 * 1024, transcendentals=0),
-    )(*stay([*brought, cell_order.reshape(1, -1), obs_mask], pltpu.HBM))
-
-    part = pltpu.VMEM((2 * share + 8, width), jnp.float32)
-    send, keep = pl.pallas_call(
+    )(*sources, *pin(prepared, pltpu.VMEM))
+
+    direct[TIED], prepared = lax.optimization_barrier((direct[TIED], prepared))
+    blocks = [block]
+    for (even, odd), fetched in zip(fetch_steps(rounds), direct):
+        blocks += [fetched] if even == odd else [fetched, other_core(fetched)]
+
+    over = pltpu.VMEM((share, width + LANES), jnp.float32)
+    stay = pltpu.VMEM((share, width), jnp.float32)
+    send_over, send_stay, keep_over, keep_stay = pl.pallas_call(
         functools.partial(layer_kernel, cells, len(blocks)),
-        out_shape=(part, part),
+        out_shape=(over, stay, over, stay),
         in_specs=[vmem] * (len(blocks) + len(prepared)),
-        out_specs=(vmem, vmem),
+        out_specs=(vmem,) * 4,
         compiler_params=pltpu.CompilerParams(vmem_limit_bytes=LAYER_LIMIT),
-    )(*stay([*blocks, *prepared], pltpu.VMEM))
-    chip = keep + other_core(send)
-    arrived = lax.ppermute(chip, "mp", [(m, m ^ 2) for m in range(models)])
+    )(*pin([*blocks, *prepared], pltpu.VMEM))
+    over = keep_over + other_core(send_over)
+    arrived = lax.ppermute(over, "mp", [(m, m ^ 2) for m in range(models)])
+    other_stay = other_core(send_stay)
     tiles_out, logits = pl.pallas_call(
         finish_kernel,
         out_shape=(
             jax.ShapeDtypeStruct((share // cell_dev, cell_dev, width), jnp.bfloat16),
             jax.ShapeDtypeStruct((1, observables), jnp.float32),
         ),
-        in_specs=[vmem, vmem],
+        in_specs=[vmem] * 4,
         out_specs=(vmem, vmem),
         compiler_params=pltpu.CompilerParams(vmem_limit_bytes=SMALL_LIMIT),
-    )(*stay([chip, arrived], pltpu.VMEM))
+    )(*pin([over, arrived, keep_stay, other_stay], pltpu.VMEM))
     return tiles_out, logits.reshape(-1)
 
 
@@ -441,6 +503,7 @@
         and rounds & (rounds - 1) == 0
         and rounds > 2
         and total <= 512
+        and total % LANES == 0
         and total // rounds <= 256
         and share % 8 == 0
         and tokens.shape[1] % 16 == 0

time: 22.1 us -> 20.9 us (0.946)
  waiting for transfers between devices: 6.33 us -> 4.82 us
  Pallas kernels: 5 us -> 5.57 us
    ppermute x1, waiting for transfers between devices: 2.6 us -> 1.03 us  [shards_whole(): arrived = lax.ppermute(over, 'mp', [(m, m ^ 2) for m in range(models)])]
    ppermute x4 -> x5, waiting for transfers between devices: 0.89 us -> 2.21 us  [other_core(): return lax.ppermute(array, 'mp', [(m, m ^ 1) for m in range(models)])]
    ppermute x4, waiting for transfers between devices: 2.84 us -> 1.58 us  [fetch(): return lax.ppermute(block, ('round', 'mp'), pairs)]
    ppermute x4, starting transfers between devices: 7.42 us -> 6.57 us  [fetch(): return lax.ppermute(block, ('round', 'mp'), pairs)]
    ppermute x4 -> x5, starting transfers between devices: 0.89 us -> 1.53 us  [other_core(): return lax.ppermute(array, 'mp', [(m, m ^ 1) for m in range(models)])]
    pallas_call x2, Pallas kernels: 2.52 us -> 3.02 us  [the longest x1 2.92 us: shards_whole(): pl.pallas_call(functools.partial(pack_kernel, preparation, len(sources),...]
  transfers between devices with their start and end apart: 9 -> 10, of which waited for: 4 -> 7; matrix products, arithmetic and copies ran while one was open for 0% -> 0% of each run, Pallas kernels for 8% -> 0%
where the time goes in v3:
time: 20.9 us; the launch traced here: 20.7 us
  starting transfers between devices  9.66 us (46%)
  Pallas kernels  5.57 us (27%)
  waiting for transfers between devices  4.82 us (23%)
  between operations  0.66 us (3%)
    ppermute x4, starting transfers between devices, fetch(): return lax.ppermute(block, ('round', 'mp'), pairs)  6.57 us
    pallas_call x1, Pallas kernels, shards_whole(): pl.pallas_call(functools.partial(pack_kernel, preparation, len(sources),...  2.92 us
    ppermute x5, waiting for transfers between devices, other_core(): return lax.ppermute(array, 'mp', [(m, m ^ 1) for m in range(models)])  2.21 us
    pallas_call x1, Pallas kernels, shards_whole(): pl.pallas_call(functools.partial(layer_kernel, cells, len(blocks)), out_s...  1.95 us
    ppermute x4, waiting for transfers between devices, fetch(): return lax.ppermute(block, ('round', 'mp'), pairs)  1.58 us
    ppermute x1, starting transfers between devices, shards_whole(): arrived = lax.ppermute(over, 'mp', [(m, m ^ 2) for m in range(models)])  1.56 us
    ppermute x5, starting transfers between devices, other_core(): return lax.ppermute(array, 'mp', [(m, m ^ 1) for m in range(models)])  1.53 us
    ppermute x1, waiting for transfers between devices, shards_whole(): arrived = lax.ppermute(over, 'mp', [(m, m ^ 2) for m in range(models)])  1.03 us
  transfers between devices with their start and end apart: 10, of which 7 were waited for; matrix products, arithmetic and copies ran while one was open for 0% of the time, Pallas kernels for 0%

profile of v3, /device:TPU:0, one launch (start us, length us, event | category | flops | bytes accessed | tf_op | source)
XLA Modules:
  0.0 20.7 jit_solution(2298063652666938454)
XLA Ops:
  0.6 2.9 %shard_map.140 = (bf16[1,32,640]{2,1,0:T(8,128)(2,1)S(1)}, f32[1,512]{1,0:T(1,128)S(1)}, f32[1,512]{1,0:T(1,128)S(1)}, bf16[512,128]{1,0:T(8,128)(2,1)S(1)}, bf1...) custom-call(bf16[1,32,512]{2,1,0:T(8,128)(2,1)} %tokens.1, ...), custom_call_target="tpu_custom_call" | custom-call | tf_op jit(solution)/shard_map/pallas_call | solution.py:429
  3.6 1.1 %collective-permute-start = (bf16[1,32,640]{2,1,0:T(8,128)(2,1)S(1)}, bf16[1,32,640]{2,1,0:T(8,128)(2,1)S(1)}, u32[]{:S(2)}, u32[]{:S(2)}) collective-permute-start(bf16[1,32,640]{2,1,0:T(8,128)(2,1)S(1)} %get-tuple-element.58.refs_0_), channel_id=1, source_target_pairs={{24,0},{29,1},{26,2},{31,3},{28,4},{25,5},{30,6},{27,7},{0,8},{5,9... | collective-permute-start | bytes 122888 | tf_op jit(solution)/shard_map/ppermute | solution.py:449
  4.7 2.6 %collective-permute-start.4 = (bf16[1,32,640]{2,1,0:T(8,128)(2,1)S(1)}, bf16[1,32,640]{2,1,0:T(8,128)(2,1)S(1)}, u32[]{:S(2)}, u32[]{:S(2)}) collective-permute-start(bf16[1,32,640]{2,1,0:T(8,128)(2,1)S(1)} %get-tuple-element.58.refs_0_), channel_id=1, source_target_pairs={{16,0},{21,1},{18,2},{23,3},{20,4},{17,5},{22,6},{19,7},{24,8},{29... | collective-permute-start | bytes 122888 | tf_op jit(solution)/shard_map/ppermute | solution.py:449
  7.3 1.3 %collective-permute-start.2 = (bf16[1,32,640]{2,1,0:T(8,128)(2,1)S(1)}, bf16[1,32,640]{2,1,0:T(8,128)(2,1)S(1)}, u32[]{:S(2)}, u32[]{:S(2)}) collective-permute-start(bf16[1,32,640]{2,1,0:T(8,128)(2,1)S(1)} %get-tuple-element.58.refs_0_), channel_id=1, source_target_pairs={{8,0},{13,1},{10,2},{15,3},{12,4},{9,5},{14,6},{11,7},{16,8},{21,9... | collective-permute-start | bytes 122888 | tf_op jit(solution)/shard_map/ppermute | solution.py:449
  8.6 1.5 %collective-permute-start.6 = (bf16[1,32,640]{2,1,0:T(8,128)(2,1)S(1)}, bf16[1,32,640]{2,1,0:T(8,128)(2,1)S(1)}, u32[]{:S(2)}, u32[]{:S(2)}) collective-permute-start(bf16[1,32,640]{2,1,0:T(8,128)(2,1)S(1)} %get-tuple-element.58.refs_0_), channel_id=1, source_target_pairs={{4,0},{5,1},{6,2},{7,3},{0,4},{1,5},{2,6},{3,7},{12,8},{13,9},{14,... | collective-permute-start | bytes 122888 | tf_op jit(solution)/shard_map/ppermute | solution.py:449
  10.1 0.1 shard_map.141
  10.2 0.0 collective-permute-done.refs_1_
  10.2 0.9 %collective-permute-done.4.refs_5_ = bf16[1,32,640]{2,1,0:T(8,128)(2,1)S(1)} collective-permute-done((bf16[1,32,640]{2,1,0:T(8,128)(2,1)S(1)}, bf16[1,32,640]{2,1,0:T(8,128)(2,1)S(1)}, u32[]{:S(2)}, u32[]{:S(2)}) %collective-permute-start.4) | collective-permute-done | bytes 40992 | tf_op jit(solution)/shard_map/ppermute | solution.py:449
  11.2 0.6 %collective-permute-start.5 = (bf16[1,32,640]{2,1,0:T(8,128)(2,1)S(1)}, bf16[1,32,640]{2,1,0:T(8,128)(2,1)S(1)}, u32[]{:S(2)}, u32[]{:S(2)}) collective-permute-start(bf16[1,32,640]{2,1,0:T(8,128)(2,1)S(1)} %collective-permute-done.4.refs_5_), channel_id=1, source_target_pairs={{0,1},{1,0},{2,3},{3,2},{4,5},{5,4},{6,7},{7,6},{8,9},{9,8},{10,11... | collective-permute-start | bytes 122888 | tf_op jit(solution)/shard_map/ppermute | solution.py:452
  11.8 0.0 collective-permute-done.2.refs_3_
  11.8 0.0 collective-permute-start.3
  11.8 0.5 %collective-permute-start.1 = (bf16[1,32,640]{2,1,0:T(8,128)(2,1)S(1)}, bf16[1,32,640]{2,1,0:T(8,128)(2,1)S(1)}, u32[]{:S(2)}, u32[]{:S(2)}) collective-permute-start(bf16[1,32,640]{2,1,0:T(8,128)(2,1)S(1)} %collective-permute-done.refs_1_), channel_id=1, source_target_pairs={{0,1},{1,0},{2,3},{3,2},{4,5},{5,4},{6,7},{7,6},{8,9},{9,8},{10,11... | collective-permute-start | bytes 122888 | tf_op jit(solution)/shard_map/ppermute | solution.py:452
  12.3 0.6 %collective-permute-done.6.refs_7_ = bf16[1,32,640]{2,1,0:T(8,128)(2,1)S(1)} collective-permute-done((bf16[1,32,640]{2,1,0:T(8,128)(2,1)S(1)}, bf16[1,32,640]{2,1,0:T(8,128)(2,1)S(1)}, u32[]{:S(2)}, u32[]{:S(2)}) %collective-permute-start.6) | collective-permute-done | bytes 40992 | tf_op jit(solution)/shard_map/ppermute | solution.py:449
  12.9 0.0 collective-permute-done.5.refs_6_
  12.9 0.1 collective-permute-done.3.refs_4_
  13.0 0.2 collective-permute-done.1.refs_2_
  13.2 1.9 %shard_map.142 = (f32[8,640]{1,0:T(8,128)S(1)}, f32[8,512]{1,0:T(8,128)S(1)}, f32[8,640]{1,0:T(8,128)S(1)}, f32[8,512]{1,0:T(8,128)S(1)}) custom-call(bf16[1,32,640]{2,1,0:T(8,128)(2,1)S(1)} %get-tuple-element.58.refs_0_, bf16[1,32,640]{2,1,0:T(8,128)(2,1)S(1)} %collective-permute-done.refs_1_, bf16[1,32,640]{2,1,0:T(8,128)(2,1)S(1)} %collective-permute-done.1.refs_2_, ...), custom_call_target="tpu_custom_call" | custom-call | tf_op jit(solution)/shard_map/pallas_call | solution.py:473
  15.1 0.4 %collective-permute-start.7 = (f32[8,640]{1,0:T(8,128)S(1)}, f32[8,640]{1,0:T(8,128)S(1)}, u32[]{:S(2)}, u32[]{:S(2)}) collective-permute-start(f32[8,640]{1,0:T(8,128)S(1)} %get-tuple-element.109), channel_id=1, source_target_pairs={{0,1},{1,0},{2,3},{3,2},{4,5},{5,4},{6,7},{7,6},{8,9},{9,8},{10,11... | collective-permute-start | bytes 61448 | tf_op jit(solution)/shard_map/ppermute | solution.py:452
  15.5 0.8 %collective-permute-done.7 = f32[8,640]{1,0:T(8,128)S(1)} collective-permute-done((f32[8,640]{1,0:T(8,128)S(1)}, f32[8,640]{1,0:T(8,128)S(1)}, u32[]{:S(2)}, u32[]{:S(2)}) %collective-permute-start.7) | collective-permute-done | bytes 20512 | tf_op jit(solution)/shard_map/ppermute | solution.py:452
  16.3 1.6 %collective-permute-start.8 = (f32[8,640]{1,0:T(8,128)S(1)}, f32[8,640]{1,0:T(8,128)S(1)}, u32[]{:S(2)}, u32[]{:S(2)}) collective-permute-start(f32[8,640]{1,0:T(8,128)S(1)} %add.3.over), channel_id=1, source_target_pairs={{0,2},{1,3},{2,0},{3,1},{4,6},{5,7},{6,4},{7,5},{8,10},{9,11},{10,... | collective-permute-start | bytes 61448 | tf_op jit(solution)/shard_map/ppermute | solution.py:481
  17.9 0.1 collective-permute-start.9
  18.0 1.1 %collective-permute-done.9.other_stay = f32[8,512]{1,0:T(8,128)S(1)} collective-permute-done((f32[8,512]{1,0:T(8,128)S(1)}, f32[8,512]{1,0:T(8,128)S(1)}, u32[]{:S(2)}, u32[]{:S(2)}) %collective-permute-start.9) | collective-permute-done | bytes 16416 | tf_op jit(solution)/shard_map/ppermute | solution.py:452
  19.1 1.0 %collective-permute-done.8.arrived = f32[8,640]{1,0:T(8,128)S(1)} collective-permute-done((f32[8,640]{1,0:T(8,128)S(1)}, f32[8,640]{1,0:T(8,128)S(1)}, u32[]{:S(2)}, u32[]{:S(2)}) %collective-permute-start.8) | collective-permute-done | bytes 20512 | tf_op jit(solution)/shard_map/ppermute | solution.py:481
  20.1 0.6 %shard_map.143 = (bf16[2,4,512]{2,1,0:T(4,128)(2,1)}, f32[1,16]{1,0:T(1,128)}) custom-call(f32[8,640]{1,0:T(8,128)S(1)} %add.3.over, f32[8,640]{1,0:T(8,128)S(1)} %collective-permute-done.8.arrived, f32[8,512]{1,0:T(8,128)S(1)} %get-tuple-element.110.stay, f32[8,512]{1,0:T(8,128)S(1)} %collective-permute-done.9.other_stay), custom_call_target="tpu_custom_call" | custom-call | tf_op jit(solution)/shard_map/pallas_call | solution.py:483
  (1 shorter events, 0.0 us)
Async XLA Ops:
  3.6 6.7 %collective-permute-start = (bf16[1,32,640]{2,1,0:T(8,128)(2,1)S(1)}, bf16[1,32,640]{2,1,0:T(8,128)(2,1)S(1)}, u32[]{:S(2)}, u32[]{:S(2)}) collective-permute-start(bf16[1,32,640]{2,1,0:T(8,128)(2,1)S(1)} %get-tuple-element.58.refs_0_), channel_id=1, source_target_pairs={{24,0},{29,1},{26,2},{31,3},{28,4},{25,5},{30,6},{27,7},{0,8},{5,9... | collective-permute-start | bytes 122888 | tf_op jit(solution)/shard_map/ppermute | solution.py:449
  4.7 6.5 %collective-permute-start.4 = (bf16[1,32,640]{2,1,0:T(8,128)(2,1)S(1)}, bf16[1,32,640]{2,1,0:T(8,128)(2,1)S(1)}, u32[]{:S(2)}, u32[]{:S(2)}) collective-permute-start(bf16[1,32,640]{2,1,0:T(8,128)(2,1)S(1)} %get-tuple-element.58.refs_0_), channel_id=1, source_target_pairs={{16,0},{21,1},{18,2},{23,3},{20,4},{17,5},{22,6},{19,7},{24,8},{29... | collective-permute-start | bytes 122888 | tf_op jit(solution)/shard_map/ppermute | solution.py:449
  7.3 4.5 %collective-permute-start.2 = (bf16[1,32,640]{2,1,0:T(8,128)(2,1)S(1)}, bf16[1,32,640]{2,1,0:T(8,128)(2,1)S(1)}, u32[]{:S(2)}, u32[]{:S(2)}) collective-permute-start(bf16[1,32,640]{2,1,0:T(8,128)(2,1)S(1)} %get-tuple-element.58.refs_0_), channel_id=1, source_target_pairs={{8,0},{13,1},{10,2},{15,3},{12,4},{9,5},{14,6},{11,7},{16,8},{21,9... | collective-permute-start | bytes 122888 | tf_op jit(solution)/shard_map/ppermute | solution.py:449
  8.6 4.3 %collective-permute-start.6 = (bf16[1,32,640]{2,1,0:T(8,128)(2,1)S(1)}, bf16[1,32,640]{2,1,0:T(8,128)(2,1)S(1)}, u32[]{:S(2)}, u32[]{:S(2)}) collective-permute-start(bf16[1,32,640]{2,1,0:T(8,128)(2,1)S(1)} %get-tuple-element.58.refs_0_), channel_id=1, source_target_pairs={{4,0},{5,1},{6,2},{7,3},{0,4},{1,5},{2,6},{3,7},{12,8},{13,9},{14,... | collective-permute-start | bytes 122888 | tf_op jit(solution)/shard_map/ppermute | solution.py:449
  11.2 1.8 %collective-permute-start.5 = (bf16[1,32,640]{2,1,0:T(8,128)(2,1)S(1)}, bf16[1,32,640]{2,1,0:T(8,128)(2,1)S(1)}, u32[]{:S(2)}, u32[]{:S(2)}) collective-permute-start(bf16[1,32,640]{2,1,0:T(8,128)(2,1)S(1)} %collective-permute-done.4.refs_5_), channel_id=1, source_target_pairs={{0,1},{1,0},{2,3},{3,2},{4,5},{5,4},{6,7},{7,6},{8,9},{9,8},{10,11... | collective-permute-start | bytes 122888 | tf_op jit(solution)/shard_map/ppermute | solution.py:452
  11.8 1.2 %collective-permute-start.3 = (bf16[1,32,640]{2,1,0:T(8,128)(2,1)S(1)}, bf16[1,32,640]{2,1,0:T(8,128)(2,1)S(1)}, u32[]{:S(2)}, u32[]{:S(2)}) collective-permute-start(bf16[1,32,640]{2,1,0:T(8,128)(2,1)S(1)} %collective-permute-done.2.refs_3_), channel_id=1, source_target_pairs={{0,1},{1,0},{2,3},{3,2},{4,5},{5,4},{6,7},{7,6},{8,9},{9,8},{10,11... | collective-permute-start | bytes 122888 | tf_op jit(solution)/shard_map/ppermute | solution.py:452
  11.8 1.4 %collective-permute-start.1 = (bf16[1,32,640]{2,1,0:T(8,128)(2,1)S(1)}, bf16[1,32,640]{2,1,0:T(8,128)(2,1)S(1)}, u32[]{:S(2)}, u32[]{:S(2)}) collective-permute-start(bf16[1,32,640]{2,1,0:T(8,128)(2,1)S(1)} %collective-permute-done.refs_1_), channel_id=1, source_target_pairs={{0,1},{1,0},{2,3},{3,2},{4,5},{5,4},{6,7},{7,6},{8,9},{9,8},{10,11... | collective-permute-start | bytes 122888 | tf_op jit(solution)/shard_map/ppermute | solution.py:452
  15.1 1.2 %collective-permute-start.7 = (f32[8,640]{1,0:T(8,128)S(1)}, f32[8,640]{1,0:T(8,128)S(1)}, u32[]{:S(2)}, u32[]{:S(2)}) collective-permute-start(f32[8,640]{1,0:T(8,128)S(1)} %get-tuple-element.109), channel_id=1, source_target_pairs={{0,1},{1,0},{2,3},{3,2},{4,5},{5,4},{6,7},{7,6},{8,9},{9,8},{10,11... | collective-permute-start | bytes 61448 | tf_op jit(solution)/shard_map/ppermute | solution.py:452
  16.3 3.8 %collective-permute-start.8 = (f32[8,640]{1,0:T(8,128)S(1)}, f32[8,640]{1,0:T(8,128)S(1)}, u32[]{:S(2)}, u32[]{:S(2)}) collective-permute-start(f32[8,640]{1,0:T(8,128)S(1)} %add.3.over), channel_id=1, source_target_pairs={{0,2},{1,3},{2,0},{3,1},{4,6},{5,7},{6,4},{7,5},{8,10},{9,11},{10,... | collective-permute-start | bytes 61448 | tf_op jit(solution)/shard_map/ppermute | solution.py:481
  17.9 1.2 %collective-permute-start.9 = (f32[8,512]{1,0:T(8,128)S(1)}, f32[8,512]{1,0:T(8,128)S(1)}, u32[]{:S(2)}, u32[]{:S(2)}) collective-permute-start(f32[8,512]{1,0:T(8,128)S(1)} %get-tuple-element.111), channel_id=1, source_target_pairs={{0,1},{1,0},{2,3},{3,2},{4,5},{5,4},{6,7},{7,6},{8,9},{9,8},{10,11... | collective-permute-start | bytes 49160 | tf_op jit(solution)/shard_map/ppermute | solution.py:452

commit v4 on v3

--- a/solution.py
+++ b/solution.py
@@ -161,9 +161,10 @@
     return jnp.concatenate([high, middle, low], axis=0)
 
 
-def softmax(scores):
+def attend_by_keys(head_vals, scores):
     weights = jnp.exp(scores - jnp.max(scores, axis=0, keepdims=True))
-    return (weights / jnp.sum(weights, axis=0, keepdims=True)).astype(jnp.bfloat16)
+    probabilities = (weights / jnp.sum(weights, axis=0, keepdims=True)).astype(jnp.bfloat16)
+    return dot(head_vals, probabilities)
 
 
 def fetch_steps(rounds):
@@ -298,41 +299,43 @@
     tile_rows = picks.shape[0] - observables
 
     tokens = jnp.concatenate([block[0, :, :width] for block in blocks], axis=0)
+    token_rows = dot(token_picks[...], tokens)
+
+    members = jnp.concatenate([block[0, :, width:] for block in blocks], axis=0)
+    member = dot(place[...], members).astype(jnp.bfloat16)
+
     values = tokens.astype(jnp.float32)
     spread = jnp.mean(values * values, axis=-1, keepdims=True)
     normed = (values * lax.rsqrt(spread + norm_eps) * gain[...]).astype(jnp.bfloat16)
 
-    members = jnp.concatenate([block[0, :, width:] for block in blocks], axis=0)
-    member = dot(place[...], members).astype(jnp.bfloat16)
-    seam_bias = jnp.where(dot_t(member, member) > 0.5, 0.0, -1e30)
-    in_seam = dot_t(jnp.ones((8, LANES), jnp.bfloat16), member)[:1] > 0.5
+    queries = (dot(normed, w_query[...]) * (1.0 / math.sqrt(HDIM))).astype(jnp.bfloat16)
+    keys = dot(normed, w_key[...]).astype(jnp.bfloat16)
+    vals = dot_t(w_value_t[...], normed).astype(jnp.bfloat16)
 
     gate = dot(normed, w_gate[...])
     up = dot(normed, w_up[...])
     hidden = (gate / (1.0 + jnp.exp(-gate)) * up).astype(jnp.bfloat16)
 
-    queries = (dot(normed, w_query[...]) * (1.0 / math.sqrt(HDIM))).astype(jnp.bfloat16)
-    keys = dot(normed, w_key[...]).astype(jnp.bfloat16)
-    vals = dot_t(w_value_t[...], normed).astype(jnp.bfloat16)
+    seam_bias = jnp.where(dot_t(member, member) > 0.5, 0.0, -1e30)
+    in_seam = dot_t(jnp.ones((8, LANES), jnp.bfloat16), member)[:1] > 0.5
     lane_head = lax.div(iota((1, head_width), 1), HDIM)
-    heads = []
-    for head in range(head_width // HDIM):
-        head_keys = jnp.where(lane_head == head, keys, jnp.zeros_like(keys))
-        head_vals = vals[head * HDIM : (head + 1) * HDIM]
-        parts = []
-        for first in range(0, total, LANES):
-            some = slice(first, first + LANES)
+    parts = []
+    for first in range(0, total, LANES):
+        some = slice(first, first + LANES)
+        mixed = []
+        for head in range(head_width // HDIM):
+            head_keys = jnp.where(lane_head == head, keys, jnp.zeros_like(keys))
+            head_vals = vals[head * HDIM : (head + 1) * HDIM]
             scores = dot_t(head_keys, queries[some])
-            local = dot(head_vals, softmax(scores + tile_bias[:, some]))
-            seam = dot(head_vals, softmax(scores + seam_bias[:, some]))
+            local = attend_by_keys(head_vals, scores + tile_bias[:, some])
+            seam = attend_by_keys(head_vals, scores + seam_bias[:, some])
             seam = seam.astype(jnp.bfloat16).astype(jnp.float32)
-            parts.append((local + jnp.where(in_seam[:, some], seam, 0.0)).astype(jnp.bfloat16))
-        heads.append(jnp.concatenate(parts, axis=1))
-    combined = jnp.concatenate(heads, axis=0)
+            mixed.append((local + jnp.where(in_seam[:, some], seam, 0.0)).astype(jnp.bfloat16))
+        parts.append(jnp.concatenate(mixed, axis=0))
+    combined = jnp.concatenate(parts, axis=1)
 
     hidden_rows = dot(picks[...], hidden)
     combined_rows = dot_t(picks[...], combined)
-    token_rows = dot(token_picks[...], tokens)
     update = (
         token_rows[:tile_rows]
         + dot(hidden_rows[:tile_rows].astype(jnp.bfloat16), w_down[...])

time: 20.9 us -> 20.5 us (0.981)
  Pallas kernels: 5.57 us -> 5.14 us
    pallas_call x1, Pallas kernels: 1.95 us -> 1.51 us  [shards_whole(): pl.pallas_call(functools.partial(layer_kernel, cells, len(blocks)), out_s...]
where the time goes in v4:
time: 20.5 us; the launch traced here: 20.3 us
  starting transfers between devices  9.69 us (47%)
  Pallas kernels  5.14 us (25%)
  waiting for transfers between devices  4.82 us (24%)
  between operations  0.66 us (3%)
    ppermute x4, starting transfers between devices, fetch(): return lax.ppermute(block, ('round', 'mp'), pairs)  6.57 us
    pallas_call x1, Pallas kernels, shards_whole(): pl.pallas_call(functools.partial(pack_kernel, preparation, len(sources),...  2.92 us
    ppermute x5, waiting for transfers between devices, other_core(): return lax.ppermute(array, 'mp', [(m, m ^ 1) for m in range(models)])  2.2 us
    ppermute x4, waiting for transfers between devices, fetch(): return lax.ppermute(block, ('round', 'mp'), pairs)  1.58 us
    ppermute x1, starting transfers between devices, shards_whole(): arrived = lax.ppermute(over, 'mp', [(m, m ^ 2) for m in range(models)])  1.56 us
    ppermute x5, starting transfers between devices, other_core(): return lax.ppermute(array, 'mp', [(m, m ^ 1) for m in range(models)])  1.56 us
    pallas_call x1, Pallas kernels, shards_whole(): pl.pallas_call(functools.partial(layer_kernel, cells, len(blocks)), out_s...  1.51 us
    ppermute x1, waiting for transfers between devices, shards_whole(): arrived = lax.ppermute(over, 'mp', [(m, m ^ 2) for m in range(models)])  1.04 us
  transfers between devices with their start and end apart: 10, of which 7 were waited for; matrix products, arithmetic and copies ran while one was open for 0% of the time, Pallas kernels for 0%

profile of v4, /device:TPU:0, one launch (start us, length us, event | category | flops | bytes accessed | tf_op | source)
XLA Modules:
  0.0 20.3 jit_solution(8354838012226022587)
XLA Ops:
  0.6 2.9 %shard_map.140 = (bf16[1,32,640]{2,1,0:T(8,128)(2,1)S(1)}, f32[1,512]{1,0:T(1,128)S(1)}, f32[1,512]{1,0:T(1,128)S(1)}, bf16[512,128]{1,0:T(8,128)(2,1)S(1)}, bf1...) custom-call(bf16[1,32,512]{2,1,0:T(8,128)(2,1)} %tokens.1, ...), custom_call_target="tpu_custom_call" | custom-call | tf_op jit(solution)/shard_map/pallas_call | solution.py:432
  3.6 1.1 %collective-permute-start = (bf16[1,32,640]{2,1,0:T(8,128)(2,1)S(1)}, bf16[1,32,640]{2,1,0:T(8,128)(2,1)S(1)}, u32[]{:S(2)}, u32[]{:S(2)}) collective-permute-start(bf16[1,32,640]{2,1,0:T(8,128)(2,1)S(1)} %get-tuple-element.58.refs_0_), channel_id=1, source_target_pairs={{24,0},{29,1},{26,2},{31,3},{28,4},{25,5},{30,6},{27,7},{0,8},{5,9... | collective-permute-start | bytes 122888 | tf_op jit(solution)/shard_map/ppermute | solution.py:452
  4.7 2.6 %collective-permute-start.4 = (bf16[1,32,640]{2,1,0:T(8,128)(2,1)S(1)}, bf16[1,32,640]{2,1,0:T(8,128)(2,1)S(1)}, u32[]{:S(2)}, u32[]{:S(2)}) collective-permute-start(bf16[1,32,640]{2,1,0:T(8,128)(2,1)S(1)} %get-tuple-element.58.refs_0_), channel_id=1, source_target_pairs={{16,0},{21,1},{18,2},{23,3},{20,4},{17,5},{22,6},{19,7},{24,8},{29... | collective-permute-start | bytes 122888 | tf_op jit(solution)/shard_map/ppermute | solution.py:452
  7.3 1.3 %collective-permute-start.2 = (bf16[1,32,640]{2,1,0:T(8,128)(2,1)S(1)}, bf16[1,32,640]{2,1,0:T(8,128)(2,1)S(1)}, u32[]{:S(2)}, u32[]{:S(2)}) collective-permute-start(bf16[1,32,640]{2,1,0:T(8,128)(2,1)S(1)} %get-tuple-element.58.refs_0_), channel_id=1, source_target_pairs={{8,0},{13,1},{10,2},{15,3},{12,4},{9,5},{14,6},{11,7},{16,8},{21,9... | collective-permute-start | bytes 122888 | tf_op jit(solution)/shard_map/ppermute | solution.py:452
  8.6 1.5 %collective-permute-start.6 = (bf16[1,32,640]{2,1,0:T(8,128)(2,1)S(1)}, bf16[1,32,640]{2,1,0:T(8,128)(2,1)S(1)}, u32[]{:S(2)}, u32[]{:S(2)}) collective-permute-start(bf16[1,32,640]{2,1,0:T(8,128)(2,1)S(1)} %get-tuple-element.58.refs_0_), channel_id=1, source_target_pairs={{4,0},{5,1},{6,2},{7,3},{0,4},{1,5},{2,6},{3,7},{12,8},{13,9},{14,... | collective-permute-start | bytes 122888 | tf_op jit(solution)/shard_map/ppermute | solution.py:452
  10.1 0.1 shard_map.141
  10.2 0.0 collective-permute-done.refs_1_
  10.2 0.9 %collective-permute-done.4.refs_5_ = bf16[1,32,640]{2,1,0:T(8,128)(2,1)S(1)} collective-permute-done((bf16[1,32,640]{2,1,0:T(8,128)(2,1)S(1)}, bf16[1,32,640]{2,1,0:T(8,128)(2,1)S(1)}, u32[]{:S(2)}, u32[]{:S(2)}) %collective-permute-start.4) | collective-permute-done | bytes 40992 | tf_op jit(solution)/shard_map/ppermute | solution.py:452
  11.2 0.6 %collective-permute-start.5 = (bf16[1,32,640]{2,1,0:T(8,128)(2,1)S(1)}, bf16[1,32,640]{2,1,0:T(8,128)(2,1)S(1)}, u32[]{:S(2)}, u32[]{:S(2)}) collective-permute-start(bf16[1,32,640]{2,1,0:T(8,128)(2,1)S(1)} %collective-permute-done.4.refs_5_), channel_id=1, source_target_pairs={{0,1},{1,0},{2,3},{3,2},{4,5},{5,4},{6,7},{7,6},{8,9},{9,8},{10,11... | collective-permute-start | bytes 122888 | tf_op jit(solution)/shard_map/ppermute | solution.py:455
  11.8 0.0 collective-permute-done.2.refs_3_
  11.8 0.0 collective-permute-start.3
  11.8 0.5 %collective-permute-start.1 = (bf16[1,32,640]{2,1,0:T(8,128)(2,1)S(1)}, bf16[1,32,640]{2,1,0:T(8,128)(2,1)S(1)}, u32[]{:S(2)}, u32[]{:S(2)}) collective-permute-start(bf16[1,32,640]{2,1,0:T(8,128)(2,1)S(1)} %collective-permute-done.refs_1_), channel_id=1, source_target_pairs={{0,1},{1,0},{2,3},{3,2},{4,5},{5,4},{6,7},{7,6},{8,9},{9,8},{10,11... | collective-permute-start | bytes 122888 | tf_op jit(solution)/shard_map/ppermute | solution.py:455
  12.3 0.6 %collective-permute-done.6.refs_7_ = bf16[1,32,640]{2,1,0:T(8,128)(2,1)S(1)} collective-permute-done((bf16[1,32,640]{2,1,0:T(8,128)(2,1)S(1)}, bf16[1,32,640]{2,1,0:T(8,128)(2,1)S(1)}, u32[]{:S(2)}, u32[]{:S(2)}) %collective-permute-start.6) | collective-permute-done | bytes 40992 | tf_op jit(solution)/shard_map/ppermute | solution.py:452
  12.9 0.0 collective-permute-done.5.refs_6_
  12.9 0.1 collective-permute-done.3.refs_4_
  13.0 0.2 collective-permute-done.1.refs_2_
  13.2 1.5 %shard_map.142 = (f32[8,640]{1,0:T(8,128)S(1)}, f32[8,512]{1,0:T(8,128)S(1)}, f32[8,640]{1,0:T(8,128)S(1)}, f32[8,512]{1,0:T(8,128)S(1)}) custom-call(bf16[1,32,640]{2,1,0:T(8,128)(2,1)S(1)} %get-tuple-element.58.refs_0_, bf16[1,32,640]{2,1,0:T(8,128)(2,1)S(1)} %collective-permute-done.refs_1_, bf16[1,32,640]{2,1,0:T(8,128)(2,1)S(1)} %collective-permute-done.1.refs_2_, ...), custom_call_target="tpu_custom_call" | custom-call | tf_op jit(solution)/shard_map/pallas_call | solution.py:476
  14.7 0.4 %collective-permute-start.7 = (f32[8,640]{1,0:T(8,128)S(1)}, f32[8,640]{1,0:T(8,128)S(1)}, u32[]{:S(2)}, u32[]{:S(2)}) collective-permute-start(f32[8,640]{1,0:T(8,128)S(1)} %get-tuple-element.109), channel_id=1, source_target_pairs={{0,1},{1,0},{2,3},{3,2},{4,5},{5,4},{6,7},{7,6},{8,9},{9,8},{10,11... | collective-permute-start | bytes 61448 | tf_op jit(solution)/shard_map/ppermute | solution.py:455
  15.1 0.8 %collective-permute-done.7 = f32[8,640]{1,0:T(8,128)S(1)} collective-permute-done((f32[8,640]{1,0:T(8,128)S(1)}, f32[8,640]{1,0:T(8,128)S(1)}, u32[]{:S(2)}, u32[]{:S(2)}) %collective-permute-start.7) | collective-permute-done | bytes 20512 | tf_op jit(solution)/shard_map/ppermute | solution.py:455
  15.9 1.6 %collective-permute-start.8 = (f32[8,640]{1,0:T(8,128)S(1)}, f32[8,640]{1,0:T(8,128)S(1)}, u32[]{:S(2)}, u32[]{:S(2)}) collective-permute-start(f32[8,640]{1,0:T(8,128)S(1)} %add.3.over), channel_id=1, source_target_pairs={{0,2},{1,3},{2,0},{3,1},{4,6},{5,7},{6,4},{7,5},{8,10},{9,11},{10,... | collective-permute-start | bytes 61448 | tf_op jit(solution)/shard_map/ppermute | solution.py:484
  17.5 0.1 collective-permute-start.9
  17.6 1.1 %collective-permute-done.9.other_stay = f32[8,512]{1,0:T(8,128)S(1)} collective-permute-done((f32[8,512]{1,0:T(8,128)S(1)}, f32[8,512]{1,0:T(8,128)S(1)}, u32[]{:S(2)}, u32[]{:S(2)}) %collective-permute-start.9) | collective-permute-done | bytes 16416 | tf_op jit(solution)/shard_map/ppermute | solution.py:455
  18.7 1.0 %collective-permute-done.8.arrived = f32[8,640]{1,0:T(8,128)S(1)} collective-permute-done((f32[8,640]{1,0:T(8,128)S(1)}, f32[8,640]{1,0:T(8,128)S(1)}, u32[]{:S(2)}, u32[]{:S(2)}) %collective-permute-start.8) | collective-permute-done | bytes 20512 | tf_op jit(solution)/shard_map/ppermute | solution.py:484
  19.7 0.6 %shard_map.143 = (bf16[2,4,512]{2,1,0:T(4,128)(2,1)}, f32[1,16]{1,0:T(1,128)}) custom-call(f32[8,640]{1,0:T(8,128)S(1)} %add.3.over, f32[8,640]{1,0:T(8,128)S(1)} %collective-permute-done.8.arrived, f32[8,512]{1,0:T(8,128)S(1)} %get-tuple-element.110.stay, f32[8,512]{1,0:T(8,128)S(1)} %collective-permute-done.9.other_stay), custom_call_target="tpu_custom_call" | custom-call | tf_op jit(solution)/shard_map/pallas_call | solution.py:486
  (1 shorter events, 0.0 us)
Async XLA Ops:
  3.6 6.7 %collective-permute-start = (bf16[1,32,640]{2,1,0:T(8,128)(2,1)S(1)}, bf16[1,32,640]{2,1,0:T(8,128)(2,1)S(1)}, u32[]{:S(2)}, u32[]{:S(2)}) collective-permute-start(bf16[1,32,640]{2,1,0:T(8,128)(2,1)S(1)} %get-tuple-element.58.refs_0_), channel_id=1, source_target_pairs={{24,0},{29,1},{26,2},{31,3},{28,4},{25,5},{30,6},{27,7},{0,8},{5,9... | collective-permute-start | bytes 122888 | tf_op jit(solution)/shard_map/ppermute | solution.py:452
  4.7 6.5 %collective-permute-start.4 = (bf16[1,32,640]{2,1,0:T(8,128)(2,1)S(1)}, bf16[1,32,640]{2,1,0:T(8,128)(2,1)S(1)}, u32[]{:S(2)}, u32[]{:S(2)}) collective-permute-start(bf16[1,32,640]{2,1,0:T(8,128)(2,1)S(1)} %get-tuple-element.58.refs_0_), channel_id=1, source_target_pairs={{16,0},{21,1},{18,2},{23,3},{20,4},{17,5},{22,6},{19,7},{24,8},{29... | collective-permute-start | bytes 122888 | tf_op jit(solution)/shard_map/ppermute | solution.py:452
  7.3 4.5 %collective-permute-start.2 = (bf16[1,32,640]{2,1,0:T(8,128)(2,1)S(1)}, bf16[1,32,640]{2,1,0:T(8,128)(2,1)S(1)}, u32[]{:S(2)}, u32[]{:S(2)}) collective-permute-start(bf16[1,32,640]{2,1,0:T(8,128)(2,1)S(1)} %get-tuple-element.58.refs_0_), channel_id=1, source_target_pairs={{8,0},{13,1},{10,2},{15,3},{12,4},{9,5},{14,6},{11,7},{16,8},{21,9... | collective-permute-start | bytes 122888 | tf_op jit(solution)/shard_map/ppermute | solution.py:452
  8.6 4.3 %collective-permute-start.6 = (bf16[1,32,640]{2,1,0:T(8,128)(2,1)S(1)}, bf16[1,32,640]{2,1,0:T(8,128)(2,1)S(1)}, u32[]{:S(2)}, u32[]{:S(2)}) collective-permute-start(bf16[1,32,640]{2,1,0:T(8,128)(2,1)S(1)} %get-tuple-element.58.refs_0_), channel_id=1, source_target_pairs={{4,0},{5,1},{6,2},{7,3},{0,4},{1,5},{2,6},{3,7},{12,8},{13,9},{14,... | collective-permute-start | bytes 122888 | tf_op jit(solution)/shard_map/ppermute | solution.py:452
  11.2 1.8 %collective-permute-start.5 = (bf16[1,32,640]{2,1,0:T(8,128)(2,1)S(1)}, bf16[1,32,640]{2,1,0:T(8,128)(2,1)S(1)}, u32[]{:S(2)}, u32[]{:S(2)}) collective-permute-start(bf16[1,32,640]{2,1,0:T(8,128)(2,1)S(1)} %collective-permute-done.4.refs_5_), channel_id=1, source_target_pairs={{0,1},{1,0},{2,3},{3,2},{4,5},{5,4},{6,7},{7,6},{8,9},{9,8},{10,11... | collective-permute-start | bytes 122888 | tf_op jit(solution)/shard_map/ppermute | solution.py:455
  11.8 1.2 %collective-permute-start.3 = (bf16[1,32,640]{2,1,0:T(8,128)(2,1)S(1)}, bf16[1,32,640]{2,1,0:T(8,128)(2,1)S(1)}, u32[]{:S(2)}, u32[]{:S(2)}) collective-permute-start(bf16[1,32,640]{2,1,0:T(8,128)(2,1)S(1)} %collective-permute-done.2.refs_3_), channel_id=1, source_target_pairs={{0,1},{1,0},{2,3},{3,2},{4,5},{5,4},{6,7},{7,6},{8,9},{9,8},{10,11... | collective-permute-start | bytes 122888 | tf_op jit(solution)/shard_map/ppermute | solution.py:455
  11.8 1.4 %collective-permute-start.1 = (bf16[1,32,640]{2,1,0:T(8,128)(2,1)S(1)}, bf16[1,32,640]{2,1,0:T(8,128)(2,1)S(1)}, u32[]{:S(2)}, u32[]{:S(2)}) collective-permute-start(bf16[1,32,640]{2,1,0:T(8,128)(2,1)S(1)} %collective-permute-done.refs_1_), channel_id=1, source_target_pairs={{0,1},{1,0},{2,3},{3,2},{4,5},{5,4},{6,7},{7,6},{8,9},{9,8},{10,11... | collective-permute-start | bytes 122888 | tf_op jit(solution)/shard_map/ppermute | solution.py:455
  14.7 1.2 %collective-permute-start.7 = (f32[8,640]{1,0:T(8,128)S(1)}, f32[8,640]{1,0:T(8,128)S(1)}, u32[]{:S(2)}, u32[]{:S(2)}) collective-permute-start(f32[8,640]{1,0:T(8,128)S(1)} %get-tuple-element.109), channel_id=1, source_target_pairs={{0,1},{1,0},{2,3},{3,2},{4,5},{5,4},{6,7},{7,6},{8,9},{9,8},{10,11... | collective-permute-start | bytes 61448 | tf_op jit(solution)/shard_map/ppermute | solution.py:455
  15.9 3.8 %collective-permute-start.8 = (f32[8,640]{1,0:T(8,128)S(1)}, f32[8,640]{1,0:T(8,128)S(1)}, u32[]{:S(2)}, u32[]{:S(2)}) collective-permute-start(f32[8,640]{1,0:T(8,128)S(1)} %add.3.over), channel_id=1, source_target_pairs={{0,2},{1,3},{2,0},{3,1},{4,6},{5,7},{6,4},{7,5},{8,10},{9,11},{10,... | collective-permute-start | bytes 61448 | tf_op jit(solution)/shard_map/ppermute | solution.py:484
  17.5 1.2 %collective-permute-start.9 = (f32[8,512]{1,0:T(8,128)S(1)}, f32[8,512]{1,0:T(8,128)S(1)}, u32[]{:S(2)}, u32[]{:S(2)}) collective-permute-start(f32[8,512]{1,0:T(8,128)S(1)} %get-tuple-element.111), channel_id=1, source_target_pairs={{0,1},{1,0},{2,3},{3,2},{4,5},{5,4},{6,7},{7,6},{8,9},{9,8},{10,11... | collective-permute-start | bytes 49160 | tf_op jit(solution)/shard_map/ppermute | solution.py:455

commit v5 on v4

--- a/solution.py
+++ b/solution.py
@@ -179,8 +179,7 @@
     return steps
 
 
-def pack_kernel(prepare, given, made, tokens, seam_rows, *refs):
-    block, (landed, padded, arrivals) = refs[given], refs[-3:]
+def pack_kernel(tokens, seam_rows, block, landed, padded, arrivals):
     width = tokens.shape[2]
     slots, owners = seam_rows.shape[1:]
     copies = [
@@ -199,9 +198,11 @@
     block[0, :, width:] = padded[...].astype(jnp.bfloat16)
     copies[1].wait()
 
+
+def early_kernel(prepare, *refs):
     @pl.when(lax.axis_index("round") == 0)
     def _():
-        prepare(*refs[:given], *refs[given + 1 : given + 1 + made], *refs[given + 1 + made : -3])
+        prepare(*refs)
 
 
 def late_kernel(prepare, given, made, *refs):
@@ -213,11 +214,11 @@
 def prepare(rounds, cells, counts, *refs):
     order_in, mask_in, *copied = refs[: counts + 2]
     rest = refs[counts + 2 :]
-    gain, w_read, w_query, w_key, w_gate, w_up, w_down, w_out = rest[:8]
+    w_read, w_down, w_out, gain, w_query, w_key, w_gate, w_up = rest[:8]
     w_value_t, read_down, read_out = rest[8:11]
     picks, token_picks, place, tile_bias, divisor = rest[11:16]
     order, mask, w_value, arrivals = rest[16:]
-    targets = (order, mask, gain, w_read, w_value, w_query, w_key, w_gate, w_up, w_down, w_out)
+    targets = (order, mask, w_read, w_value, w_down, w_out, gain, w_query, w_key, w_gate, w_up)
     copies = [
         pltpu.make_async_copy(source, target, arrivals.at[k])
         for k, (source, target) in enumerate(zip((order_in, mask_in, *copied), targets))
@@ -225,7 +226,7 @@
     for copy in copies:
         copy.start()
     me, model = lax.axis_index("round"), lax.axis_index("mp")
-    core, pair = model & 1, lax.shift_right_logical(model, 1)
+    core = model & 1
     cell_dev = cells // rounds
     tile_rows = rounds * cell_dev
     share = tile_rows // 4
@@ -258,9 +259,8 @@
 
     index = iota((tile_rows, 1), 0)
     quarter = lax.div(index, share)
-    target_core = jnp.where(quarter < 2, 1 - core, core)
-    target_pair = jnp.where((quarter & 1) == 0, 1 - pair, pair)
-    target = (target_pair * 2 + target_core) * share + lax.rem(index, share)
+    target_model = jnp.where(quarter < 2, model ^ 1, model) ^ jnp.where((quarter & 1) == 0, 3, 0)
+    target = target_model * share + lax.rem(index, share)
     own = one_hot((tile_row == me) & (in_tile_row == target))
     mask_bf = mask[...].astype(jnp.float32).astype(jnp.bfloat16)
     support = dot(mask_bf, one_hot(iota((cells, 1), 0) == lax.rem(column, cells))).astype(
@@ -273,22 +273,22 @@
     count = rounds * jnp.sum(mask[...].astype(jnp.float32), axis=1, keepdims=True)
     divisor[...] = jnp.broadcast_to(jnp.sqrt(count), divisor.shape)
 
-    for copy in copies[2:5]:
+    for copy in copies[2:6]:
         copy.wait()
     head_width = w_value.shape[1]
     identity = one_hot(iota((head_width, 1), 0) == iota((1, head_width), 1))
     w_value_t[...] = dot_t(identity, w_value[...]).astype(jnp.bfloat16)
     read_parts = split_three(jnp.broadcast_to(w_read[...], (8, w_read.shape[1])))
-    for copy in copies[5:]:
-        copy.wait()
     for weight, read in ((w_down, read_down), (w_out, read_out)):
         parts = dot_t(read_parts, weight[...])
         read[...] = parts[:1] + parts[8:9] + parts[16:17]
+    for copy in copies[6:]:
+        copy.wait()
 
 
 def layer_kernel(cells, slots, *refs):
     blocks, rest = refs[:slots], refs[slots:]
-    gain, w_read, w_query, w_key, w_gate, w_up, w_down, w_out = rest[:8]
+    w_read, w_down, w_out, gain, w_query, w_key, w_gate, w_up = rest[:8]
     w_value_t, read_down, read_out = rest[8:11]
     picks, token_picks, place, tile_bias, divisor = rest[11:16]
     outs = rest[16:]
@@ -400,18 +400,18 @@
         return [pltpu.with_memory_space_constraint(array, space) for array in arrays]
 
     brought = [
-        norm_gain.reshape(1, -1),
         w_read.reshape(1, -1),
         w_value,
+        w_down,
+        w_out,
+        norm_gain.reshape(1, -1),
         w_query,
         w_key,
         w_gate,
         w_up,
-        w_down,
-        w_out,
     ]
     sources = pin([cell_order.reshape(1, -1), obs_mask, *brought], pltpu.HBM)
-    made = [pltpu.VMEM(array.shape, array.dtype) for k, array in enumerate(brought) if k != 2] + [
+    made = [pltpu.VMEM(array.shape, array.dtype) for array in brought if array is not w_value] + [
         pltpu.VMEM(w_value.shape[::-1], w_value.dtype),
         pltpu.VMEM((1, w_down.shape[0]), jnp.float32),
         pltpu.VMEM((1, w_out.shape[0]), jnp.float32),
@@ -429,19 +429,27 @@
     ]
     small = pltpu.CompilerParams(vmem_limit_bytes=SMALL_LIMIT)
     preparation = functools.partial(prepare, rounds, cells, len(brought))
-    block, *prepared = pl.pallas_call(
-        functools.partial(pack_kernel, preparation, len(sources), len(made)),
-        out_shape=[pltpu.VMEM((1, cells, width + LANES), jnp.bfloat16), *made],
-        in_specs=[hbm] * (len(sources) + 2),
-        out_specs=[vmem] * (len(made) + 1),
+    block = pl.pallas_call(
+        pack_kernel,
+        out_shape=pltpu.VMEM((1, cells, width + LANES), jnp.bfloat16),
+        in_specs=[hbm, hbm],
+        out_specs=vmem,
         scratch_shapes=[
-            *scratch,
             pltpu.VMEM(seam_rows.shape[:0:-1], jnp.int32),
             pltpu.VMEM((cells, LANES), jnp.float32),
             pltpu.SemaphoreType.DMA((2,)),
         ],
         compiler_params=small,
-    )(*pin([tokens, seam_rows.transpose(0, 2, 1)], pltpu.HBM), *sources)
+    )(*pin([tokens, seam_rows.transpose(0, 2, 1)], pltpu.HBM))
+    prepared = pl.pallas_call(
+        functools.partial(early_kernel, preparation),
+        out_shape=made,
+        in_specs=[hbm] * len(sources),
+        out_specs=[vmem] * len(made),
+        scratch_shapes=scratch,
+        compiler_params=small,
+    )(*sources)
+    block, prepared = lax.optimization_barrier((block, prepared))
 
     def fetch(even, odd):
         pairs = []
@@ -481,7 +489,7 @@
         compiler_params=pltpu.CompilerParams(vmem_limit_bytes=LAYER_LIMIT),
     )(*pin([*blocks, *prepared], pltpu.VMEM))
     over = keep_over + other_core(send_over)
-    arrived = lax.ppermute(over, "mp", [(m, m ^ 2) for m in range(models)])
+    arrived = lax.ppermute(over, "mp", [(m, m ^ 3) for m in range(models)])
     other_stay = other_core(send_stay)
     tiles_out, logits = pl.pallas_call(
         finish_kernel,

time: 20.5 us -> 19.9 us (0.971)
  Pallas kernels: 5.14 us -> 4.75 us
    ppermute x4, waiting for transfers between devices: 1.58 us -> 2.17 us  [fetch(): return lax.ppermute(block, ('round', 'mp'), pairs)]
    ppermute x1, waiting for transfers between devices: 1.04 us -> 0.46 us  [shards_whole(): arrived = lax.ppermute(over, 'mp', [(m, m ^ 3) for m in range(models)])]
    ppermute x5, starting transfers between devices: 1.56 us -> 1.07 us  [other_core(): return lax.ppermute(array, 'mp', [(m, m ^ 1) for m in range(models)])]
    pallas_call x1 -> x2, Pallas kernels: 2.92 us -> 2.52 us  [the longest x1 1.73 us: shards_whole(): pl.pallas_call(functools.partial(early_kernel, preparation), out_shape=ma...]
    ppermute x4, starting transfers between devices: 6.57 us -> 6.93 us  [fetch(): return lax.ppermute(block, ('round', 'mp'), pairs)]
  transfers between devices with their start and end apart: 10 -> 10, of which waited for: 7 -> 7; matrix products, arithmetic and copies ran while one was open for 0% -> 0% of each run, Pallas kernels for 0% -> 1%
where the time goes in v5:
time: 19.9 us; the launch traced here: 19.6 us
  starting transfers between devices  9.56 us (48%)
  Pallas kernels  4.75 us (24%)
  waiting for transfers between devices  4.66 us (23%)
  between operations  0.67 us (3%)
    ppermute x4, starting transfers between devices, fetch(): return lax.ppermute(block, ('round', 'mp'), pairs)  6.93 us
    ppermute x4, waiting for transfers between devices, fetch(): return lax.ppermute(block, ('round', 'mp'), pairs)  2.17 us
    ppermute x5, waiting for transfers between devices, other_core(): return lax.ppermute(array, 'mp', [(m, m ^ 1) for m in range(models)])  2.02 us
    pallas_call x1, Pallas kernels, shards_whole(): pl.pallas_call(functools.partial(early_kernel, preparation), out_shape=ma...  1.73 us
    ppermute x1, starting transfers between devices, shards_whole(): arrived = lax.ppermute(over, 'mp', [(m, m ^ 3) for m in range(models)])  1.56 us
    pallas_call x1, Pallas kernels, shards_whole(): pl.pallas_call(functools.partial(layer_kernel, cells, len(blocks)), out_s...  1.52 us
    ppermute x5, starting transfers between devices, other_core(): return lax.ppermute(array, 'mp', [(m, m ^ 1) for m in range(models)])  1.07 us
    pallas_call x1, Pallas kernels, shards_whole(): pl.pallas_call(pack_kernel, out_shape=pltpu.VMEM((1, cells, width + LANES...  0.79 us
  transfers between devices with their start and end apart: 10, of which 7 were waited for; matrix products, arithmetic and copies ran while one was open for 0% of the time, Pallas kernels for 1%

profile of v5, /device:TPU:0, one launch (start us, length us, event | category | flops | bytes accessed | tf_op | source)
XLA Modules:
  0.0 19.6 jit_solution(5499869969225430593)
XLA Ops:
  0.6 0.8 %shard_map.140.refs_0_ = bf16[1,32,640]{2,1,0:T(8,128)(2,1)S(1)} custom-call(bf16[1,32,512]{2,1,0:T(8,128)(2,1)} %tokens.1, s32[1,2,8]{2,1,0:T(2,128)} %bitcast.11), custom_call_target="tpu_custom_call" | custom-call | tf_op jit(solution)/shard_map/pallas_call | solution.py:432
  1.4 1.7 %shard_map.141 = (f32[1,512]{1,0:T(1,128)S(1)}, bf16[512,512]{1,0:T(8,128)(2,1)S(1)}, bf16[128,512]{1,0:T(8,128)(2,1)S(1)}, f32[1,512]{1,0:T(1,128)S(1)}, bf16[5...) custom-call(s32[1,32]{1,0:T(1,128)} %bitcast.9, ...), custom_call_target="tpu_custom_call" | custom-call | tf_op jit(solution)/shard_map/pallas_call | solution.py:444
  3.2 1.5 %collective-permute-start = (bf16[1,32,640]{2,1,0:T(8,128)(2,1)S(1)}, bf16[1,32,640]{2,1,0:T(8,128)(2,1)S(1)}, u32[]{:S(2)}, u32[]{:S(2)}) collective-permute-start(bf16[1,32,640]{2,1,0:T(8,128)(2,1)S(1)} %shard_map.140.refs_0_), channel_id=1, source_target_pairs={{24,0},{29,1},{26,2},{31,3},{28,4},{25,5},{30,6},{27,7},{0,8},{5,9... | collective-permute-start | bytes 122888 | tf_op jit(solution)/shard_map/ppermute | solution.py:460
  4.6 2.6 %collective-permute-start.4 = (bf16[1,32,640]{2,1,0:T(8,128)(2,1)S(1)}, bf16[1,32,640]{2,1,0:T(8,128)(2,1)S(1)}, u32[]{:S(2)}, u32[]{:S(2)}) collective-permute-start(bf16[1,32,640]{2,1,0:T(8,128)(2,1)S(1)} %shard_map.140.refs_0_), channel_id=1, source_target_pairs={{16,0},{21,1},{18,2},{23,3},{20,4},{17,5},{22,6},{19,7},{24,8},{29... | collective-permute-start | bytes 122888 | tf_op jit(solution)/shard_map/ppermute | solution.py:460
  7.2 1.3 %collective-permute-start.2 = (bf16[1,32,640]{2,1,0:T(8,128)(2,1)S(1)}, bf16[1,32,640]{2,1,0:T(8,128)(2,1)S(1)}, u32[]{:S(2)}, u32[]{:S(2)}) collective-permute-start(bf16[1,32,640]{2,1,0:T(8,128)(2,1)S(1)} %shard_map.140.refs_0_), channel_id=1, source_target_pairs={{8,0},{13,1},{10,2},{15,3},{12,4},{9,5},{14,6},{11,7},{16,8},{21,9... | collective-permute-start | bytes 122888 | tf_op jit(solution)/shard_map/ppermute | solution.py:460
  8.6 1.5 %collective-permute-start.6 = (bf16[1,32,640]{2,1,0:T(8,128)(2,1)S(1)}, bf16[1,32,640]{2,1,0:T(8,128)(2,1)S(1)}, u32[]{:S(2)}, u32[]{:S(2)}) collective-permute-start(bf16[1,32,640]{2,1,0:T(8,128)(2,1)S(1)} %shard_map.140.refs_0_), channel_id=1, source_target_pairs={{4,0},{5,1},{6,2},{7,3},{0,4},{1,5},{2,6},{3,7},{12,8},{13,9},{14,... | collective-permute-start | bytes 122888 | tf_op jit(solution)/shard_map/ppermute | solution.py:460
  10.1 0.1 shard_map.142
  10.2 0.0 collective-permute-done.refs_1_
  10.2 0.7 %collective-permute-done.4.refs_5_ = bf16[1,32,640]{2,1,0:T(8,128)(2,1)S(1)} collective-permute-done((bf16[1,32,640]{2,1,0:T(8,128)(2,1)S(1)}, bf16[1,32,640]{2,1,0:T(8,128)(2,1)S(1)}, u32[]{:S(2)}, u32[]{:S(2)}) %collective-permute-start.4) | collective-permute-done | bytes 40992 | tf_op jit(solution)/shard_map/ppermute | solution.py:460
  10.9 0.0 collective-permute-start.5
  10.9 0.8 %collective-permute-done.2.refs_3_ = bf16[1,32,640]{2,1,0:T(8,128)(2,1)S(1)} collective-permute-done((bf16[1,32,640]{2,1,0:T(8,128)(2,1)S(1)}, bf16[1,32,640]{2,1,0:T(8,128)(2,1)S(1)}, u32[]{:S(2)}, u32[]{:S(2)}) %collective-permute-start.2) | collective-permute-done | bytes 40992 | tf_op jit(solution)/shard_map/ppermute | solution.py:460
  11.7 0.5 %collective-permute-start.1 = (bf16[1,32,640]{2,1,0:T(8,128)(2,1)S(1)}, bf16[1,32,640]{2,1,0:T(8,128)(2,1)S(1)}, u32[]{:S(2)}, u32[]{:S(2)}) collective-permute-start(bf16[1,32,640]{2,1,0:T(8,128)(2,1)S(1)} %collective-permute-done.refs_1_), channel_id=1, source_target_pairs={{0,1},{1,0},{2,3},{3,2},{4,5},{5,4},{6,7},{7,6},{8,9},{9,8},{10,11... | collective-permute-start | bytes 122888 | tf_op jit(solution)/shard_map/ppermute | solution.py:463
  12.2 0.7 %collective-permute-done.6.refs_7_ = bf16[1,32,640]{2,1,0:T(8,128)(2,1)S(1)} collective-permute-done((bf16[1,32,640]{2,1,0:T(8,128)(2,1)S(1)}, bf16[1,32,640]{2,1,0:T(8,128)(2,1)S(1)}, u32[]{:S(2)}, u32[]{:S(2)}) %collective-permute-start.6) | collective-permute-done | bytes 40992 | tf_op jit(solution)/shard_map/ppermute | solution.py:460
  12.9 0.0 collective-permute-done.5.refs_6_
  12.9 0.0 collective-permute-done.3.refs_4_
  12.9 0.2 collective-permute-done.1.refs_2_
  13.1 1.5 %shard_map.143 = (f32[8,640]{1,0:T(8,128)S(1)}, f32[8,512]{1,0:T(8,128)S(1)}, f32[8,640]{1,0:T(8,128)S(1)}, f32[8,512]{1,0:T(8,128)S(1)}) custom-call(bf16[1,32,640]{2,1,0:T(8,128)(2,1)S(1)} %shard_map.140.refs_0_, bf16[1,32,640]{2,1,0:T(8,128)(2,1)S(1)} %collective-permute-done.refs_1_, bf16[1,32,640]{2,1,0:T(8,128)(2,1)S(1)} %collective-permute-done.1.refs_2_, ...), custom_call_target="tpu_custom_call" | custom-call | tf_op jit(solution)/shard_map/pallas_call | solution.py:484
  14.6 0.4 %collective-permute-start.7 = (f32[8,640]{1,0:T(8,128)S(1)}, f32[8,640]{1,0:T(8,128)S(1)}, u32[]{:S(2)}, u32[]{:S(2)}) collective-permute-start(f32[8,640]{1,0:T(8,128)S(1)} %get-tuple-element.141), channel_id=1, source_target_pairs={{0,1},{1,0},{2,3},{3,2},{4,5},{5,4},{6,7},{7,6},{8,9},{9,8},{10,11... | collective-permute-start | bytes 61448 | tf_op jit(solution)/shard_map/ppermute | solution.py:463
  15.0 0.8 %collective-permute-done.7 = f32[8,640]{1,0:T(8,128)S(1)} collective-permute-done((f32[8,640]{1,0:T(8,128)S(1)}, f32[8,640]{1,0:T(8,128)S(1)}, u32[]{:S(2)}, u32[]{:S(2)}) %collective-permute-start.7) | collective-permute-done | bytes 20512 | tf_op jit(solution)/shard_map/ppermute | solution.py:463
  15.8 1.6 %collective-permute-start.8 = (f32[8,640]{1,0:T(8,128)S(1)}, f32[8,640]{1,0:T(8,128)S(1)}, u32[]{:S(2)}, u32[]{:S(2)}) collective-permute-start(f32[8,640]{1,0:T(8,128)S(1)} %add.3.over), channel_id=1, source_target_pairs={{0,3},{1,2},{2,1},{3,0},{4,7},{5,6},{6,5},{7,4},{8,11},{9,10},{10,... | collective-permute-start | bytes 61448 | tf_op jit(solution)/shard_map/ppermute | solution.py:492
  17.4 0.2 collective-permute-start.9
  17.6 1.0 %collective-permute-done.9.other_stay = f32[8,512]{1,0:T(8,128)S(1)} collective-permute-done((f32[8,512]{1,0:T(8,128)S(1)}, f32[8,512]{1,0:T(8,128)S(1)}, u32[]{:S(2)}, u32[]{:S(2)}) %collective-permute-start.9) | collective-permute-done | bytes 16416 | tf_op jit(solution)/shard_map/ppermute | solution.py:463
  18.6 0.5 %collective-permute-done.8.arrived = f32[8,640]{1,0:T(8,128)S(1)} collective-permute-done((f32[8,640]{1,0:T(8,128)S(1)}, f32[8,640]{1,0:T(8,128)S(1)}, u32[]{:S(2)}, u32[]{:S(2)}) %collective-permute-start.8) | collective-permute-done | bytes 20512 | tf_op jit(solution)/shard_map/ppermute | solution.py:492
  19.0 0.6 %shard_map.144 = (bf16[2,4,512]{2,1,0:T(4,128)(2,1)}, f32[1,16]{1,0:T(1,128)}) custom-call(f32[8,640]{1,0:T(8,128)S(1)} %add.3.over, f32[8,640]{1,0:T(8,128)S(1)} %collective-permute-done.8.arrived, f32[8,512]{1,0:T(8,128)S(1)} %get-tuple-element.142.stay, f32[8,512]{1,0:T(8,128)S(1)} %collective-permute-done.9.other_stay), custom_call_target="tpu_custom_call" | custom-call | tf_op jit(solution)/shard_map/pallas_call | solution.py:494
  (2 shorter events, 0.0 us)
Async XLA Ops:
  3.2 7.0 %collective-permute-start = (bf16[1,32,640]{2,1,0:T(8,128)(2,1)S(1)}, bf16[1,32,640]{2,1,0:T(8,128)(2,1)S(1)}, u32[]{:S(2)}, u32[]{:S(2)}) collective-permute-start(bf16[1,32,640]{2,1,0:T(8,128)(2,1)S(1)} %shard_map.140.refs_0_), channel_id=1, source_target_pairs={{24,0},{29,1},{26,2},{31,3},{28,4},{25,5},{30,6},{27,7},{0,8},{5,9... | collective-permute-start | bytes 122888 | tf_op jit(solution)/shard_map/ppermute | solution.py:460
  4.6 6.3 %collective-permute-start.4 = (bf16[1,32,640]{2,1,0:T(8,128)(2,1)S(1)}, bf16[1,32,640]{2,1,0:T(8,128)(2,1)S(1)}, u32[]{:S(2)}, u32[]{:S(2)}) collective-permute-start(bf16[1,32,640]{2,1,0:T(8,128)(2,1)S(1)} %shard_map.140.refs_0_), channel_id=1, source_target_pairs={{16,0},{21,1},{18,2},{23,3},{20,4},{17,5},{22,6},{19,7},{24,8},{29... | collective-permute-start | bytes 122888 | tf_op jit(solution)/shard_map/ppermute | solution.py:460
  7.2 4.5 %collective-permute-start.2 = (bf16[1,32,640]{2,1,0:T(8,128)(2,1)S(1)}, bf16[1,32,640]{2,1,0:T(8,128)(2,1)S(1)}, u32[]{:S(2)}, u32[]{:S(2)}) collective-permute-start(bf16[1,32,640]{2,1,0:T(8,128)(2,1)S(1)} %shard_map.140.refs_0_), channel_id=1, source_target_pairs={{8,0},{13,1},{10,2},{15,3},{12,4},{9,5},{14,6},{11,7},{16,8},{21,9... | collective-permute-start | bytes 122888 | tf_op jit(solution)/shard_map/ppermute | solution.py:460
  8.6 4.3 %collective-permute-start.6 = (bf16[1,32,640]{2,1,0:T(8,128)(2,1)S(1)}, bf16[1,32,640]{2,1,0:T(8,128)(2,1)S(1)}, u32[]{:S(2)}, u32[]{:S(2)}) collective-permute-start(bf16[1,32,640]{2,1,0:T(8,128)(2,1)S(1)} %shard_map.140.refs_0_), channel_id=1, source_target_pairs={{4,0},{5,1},{6,2},{7,3},{0,4},{1,5},{2,6},{3,7},{12,8},{13,9},{14,... | collective-permute-start | bytes 122888 | tf_op jit(solution)/shard_map/ppermute | solution.py:460
  10.9 2.0 %collective-permute-start.5 = (bf16[1,32,640]{2,1,0:T(8,128)(2,1)S(1)}, bf16[1,32,640]{2,1,0:T(8,128)(2,1)S(1)}, u32[]{:S(2)}, u32[]{:S(2)}) collective-permute-start(bf16[1,32,640]{2,1,0:T(8,128)(2,1)S(1)} %collective-permute-done.4.refs_5_), channel_id=1, source_target_pairs={{0,1},{1,0},{2,3},{3,2},{4,5},{5,4},{6,7},{7,6},{8,9},{9,8},{10,11... | collective-permute-start | bytes 122888 | tf_op jit(solution)/shard_map/ppermute | solution.py:463
  11.7 1.2 %collective-permute-start.3 = (bf16[1,32,640]{2,1,0:T(8,128)(2,1)S(1)}, bf16[1,32,640]{2,1,0:T(8,128)(2,1)S(1)}, u32[]{:S(2)}, u32[]{:S(2)}) collective-permute-start(bf16[1,32,640]{2,1,0:T(8,128)(2,1)S(1)} %collective-permute-done.2.refs_3_), channel_id=1, source_target_pairs={{0,1},{1,0},{2,3},{3,2},{4,5},{5,4},{6,7},{7,6},{8,9},{9,8},{10,11... | collective-permute-start | bytes 122888 | tf_op jit(solution)/shard_map/ppermute | solution.py:463
  11.7 1.4 %collective-permute-start.1 = (bf16[1,32,640]{2,1,0:T(8,128)(2,1)S(1)}, bf16[1,32,640]{2,1,0:T(8,128)(2,1)S(1)}, u32[]{:S(2)}, u32[]{:S(2)}) collective-permute-start(bf16[1,32,640]{2,1,0:T(8,128)(2,1)S(1)} %collective-permute-done.refs_1_), channel_id=1, source_target_pairs={{0,1},{1,0},{2,3},{3,2},{4,5},{5,4},{6,7},{7,6},{8,9},{9,8},{10,11... | collective-permute-start | bytes 122888 | tf_op jit(solution)/shard_map/ppermute | solution.py:463
  14.6 1.2 %collective-permute-start.7 = (f32[8,640]{1,0:T(8,128)S(1)}, f32[8,640]{1,0:T(8,128)S(1)}, u32[]{:S(2)}, u32[]{:S(2)}) collective-permute-start(f32[8,640]{1,0:T(8,128)S(1)} %get-tuple-element.141), channel_id=1, source_target_pairs={{0,1},{1,0},{2,3},{3,2},{4,5},{5,4},{6,7},{7,6},{8,9},{9,8},{10,11... | collective-permute-start | bytes 61448 | tf_op jit(solution)/shard_map/ppermute | solution.py:463
  15.8 3.2 %collective-permute-start.8 = (f32[8,640]{1,0:T(8,128)S(1)}, f32[8,640]{1,0:T(8,128)S(1)}, u32[]{:S(2)}, u32[]{:S(2)}) collective-permute-start(f32[8,640]{1,0:T(8,128)S(1)} %add.3.over), channel_id=1, source_target_pairs={{0,3},{1,2},{2,1},{3,0},{4,7},{5,6},{6,5},{7,4},{8,11},{9,10},{10,... | collective-permute-start | bytes 61448 | tf_op jit(solution)/shard_map/ppermute | solution.py:492
  17.4 1.2 %collective-permute-start.9 = (f32[8,512]{1,0:T(8,128)S(1)}, f32[8,512]{1,0:T(8,128)S(1)}, u32[]{:S(2)}, u32[]{:S(2)}) collective-permute-start(f32[8,512]{1,0:T(8,128)S(1)} %get-tuple-element.143), channel_id=1, source_target_pairs={{0,1},{1,0},{2,3},{3,2},{4,5},{5,4},{6,7},{7,6},{8,9},{9,8},{10,11... | collective-permute-start | bytes 49160 | tf_op jit(solution)/shard_map/ppermute | solution.py:463

commit v6 on v5

--- a/solution.py
+++ b/solution.py
@@ -11,7 +11,6 @@
 HDIM = 64
 LANES = 128
 SMALL_LIMIT = 8 * 1024 * 1024
-TIED = 0
 LAYER_LIMIT = 32 * 1024 * 1024
 
 
@@ -168,8 +167,7 @@
 
 
 def fetch_steps(rounds):
-    shifts = [2, *range(rounds - 2, 2, -2)]
-    return [((k, 0), (k, 1)) for k in shifts] + [((0, 1), (0, 1))]
+    return [((k, 0), (k, 1)) for k in range(rounds - 2, 0, -2)] + [((0, 1), (0, 1))]
 
 
 def slot_steps(rounds):
@@ -452,11 +450,13 @@
     block, prepared = lax.optimization_barrier((block, prepared))
 
     def fetch(even, odd):
+        across = 1 if even == odd else 0
         pairs = []
         for r in range(rounds):
             for m in range(models):
                 shift, flip = odd if m & 1 else even
-                pairs.append(((((r - shift) % rounds) ^ flip) * models + m, r * models + m))
+                source = ((r - shift) % rounds) ^ flip
+                pairs.append((source * models + (m ^ across), r * models + m))
         return lax.ppermute(block, ("round", "mp"), pairs)
 
     def other_core(array):
@@ -474,7 +474,7 @@
         cost_estimate=pl.CostEstimate(flops=0, bytes_accessed=8 * 1024 * 1024, transcendentals=0),
     )(*sources, *pin(prepared, pltpu.VMEM))
 
-    direct[TIED], prepared = lax.optimization_barrier((direct[TIED], prepared))
+    direct[-2], prepared = lax.optimization_barrier((direct[-2], prepared))
     blocks = [block]
     for (even, odd), fetched in zip(fetch_steps(rounds), direct):
         blocks += [fetched] if even == odd else [fetched, other_core(fetched)]

time: 19.9 us -> 19.7 us (0.990)
  starting transfers between devices: 9.56 us -> 9.04 us
  waiting for transfers between devices: 4.66 us -> 5.01 us
    ppermute x5, waiting for transfers between devices: 2.02 us -> 2.76 us  [other_core(): return lax.ppermute(array, 'mp', [(m, m ^ 1) for m in range(models)])]
    ppermute x4, waiting for transfers between devices: 2.17 us -> 1.6 us  [fetch(): return lax.ppermute(block, ('round', 'mp'), pairs)]
    ppermute x4, starting transfers between devices: 6.93 us -> 6.37 us  [fetch(): return lax.ppermute(block, ('round', 'mp'), pairs)]
    ppermute x5, starting transfers between devices: 1.07 us -> 1.29 us  [other_core(): return lax.ppermute(array, 'mp', [(m, m ^ 1) for m in range(models)])]
  transfers between devices with their start and end apart: 10 -> 10, of which waited for: 7 -> 8; matrix products, arithmetic and copies ran while one was open for 0% -> 0% of each run, Pallas kernels for 1% -> 1%
where the time goes in v6:
time: 19.7 us; the launch traced here: 19.5 us
  starting transfers between devices  9.04 us (46%)
  waiting for transfers between devices  5.01 us (25%)
  Pallas kernels  4.76 us (24%)
  between operations  0.67 us (3%)
    ppermute x4, starting transfers between devices, fetch(): return lax.ppermute(block, ('round', 'mp'), pairs)  6.37 us
    ppermute x5, waiting for transfers between devices, other_core(): return lax.ppermute(array, 'mp', [(m, m ^ 1) for m in range(models)])  2.76 us
    pallas_call x1, Pallas kernels, shards_whole(): pl.pallas_call(functools.partial(early_kernel, preparation), out_shape=ma...  1.73 us
    ppermute x4, waiting for transfers between devices, fetch(): return lax.ppermute(block, ('round', 'mp'), pairs)  1.6 us
    pallas_call x1, Pallas kernels, shards_whole(): pl.pallas_call(functools.partial(layer_kernel, cells, len(blocks)), out_s...  1.53 us
    ppermute x1, starting transfers between devices, shards_whole(): arrived = lax.ppermute(over, 'mp', [(m, m ^ 3) for m in range(models)])  1.38 us
    ppermute x5, starting transfers between devices, other_core(): return lax.ppermute(array, 'mp', [(m, m ^ 1) for m in range(models)])  1.29 us
    pallas_call x1, Pallas kernels, shards_whole(): pl.pallas_call(pack_kernel, out_shape=pltpu.VMEM((1, cells, width + LANES...  0.79 us
  transfers between devices with their start and end apart: 10, of which 8 were waited for; matrix products, arithmetic and copies ran while one was open for 0% of the time, Pallas kernels for 1%

profile of v6, /device:TPU:0, one launch (start us, length us, event | category | flops | bytes accessed | tf_op | source)
XLA Modules:
  0.0 19.5 jit_solution(15780474098218556603)
XLA Ops:
  0.6 0.8 %shard_map.140.refs_0_ = bf16[1,32,640]{2,1,0:T(8,128)(2,1)S(1)} custom-call(bf16[1,32,512]{2,1,0:T(8,128)(2,1)} %tokens.1, s32[1,2,8]{2,1,0:T(2,128)} %bitcast.11), custom_call_target="tpu_custom_call" | custom-call | tf_op jit(solution)/shard_map/pallas_call | solution.py:430
  1.4 1.7 %shard_map.141 = (f32[1,512]{1,0:T(1,128)S(1)}, bf16[512,512]{1,0:T(8,128)(2,1)S(1)}, bf16[128,512]{1,0:T(8,128)(2,1)S(1)}, f32[1,512]{1,0:T(1,128)S(1)}, bf16[5...) custom-call(s32[1,32]{1,0:T(1,128)} %bitcast.9, ...), custom_call_target="tpu_custom_call" | custom-call | tf_op jit(solution)/shard_map/pallas_call | solution.py:442
  3.2 1.5 %collective-permute-start.4 = (bf16[1,32,640]{2,1,0:T(8,128)(2,1)S(1)}, bf16[1,32,640]{2,1,0:T(8,128)(2,1)S(1)}, u32[]{:S(2)}, u32[]{:S(2)}) collective-permute-start(bf16[1,32,640]{2,1,0:T(8,128)(2,1)S(1)} %shard_map.140.refs_0_), channel_id=1, source_target_pairs={{24,0},{29,1},{26,2},{31,3},{28,4},{25,5},{30,6},{27,7},{0,8},{5,9... | collective-permute-start | bytes 122888 | tf_op jit(solution)/shard_map/ppermute | solution.py:460
  4.6 2.6 %collective-permute-start.2 = (bf16[1,32,640]{2,1,0:T(8,128)(2,1)S(1)}, bf16[1,32,640]{2,1,0:T(8,128)(2,1)S(1)}, u32[]{:S(2)}, u32[]{:S(2)}) collective-permute-start(bf16[1,32,640]{2,1,0:T(8,128)(2,1)S(1)} %shard_map.140.refs_0_), channel_id=1, source_target_pairs={{16,0},{21,1},{18,2},{23,3},{20,4},{17,5},{22,6},{19,7},{24,8},{29... | collective-permute-start | bytes 122888 | tf_op jit(solution)/shard_map/ppermute | solution.py:460
  7.2 1.3 %collective-permute-start = (bf16[1,32,640]{2,1,0:T(8,128)(2,1)S(1)}, bf16[1,32,640]{2,1,0:T(8,128)(2,1)S(1)}, u32[]{:S(2)}, u32[]{:S(2)}) collective-permute-start(bf16[1,32,640]{2,1,0:T(8,128)(2,1)S(1)} %shard_map.140.refs_0_), channel_id=1, source_target_pairs={{8,0},{13,1},{10,2},{15,3},{12,4},{9,5},{14,6},{11,7},{16,8},{21,9... | collective-permute-start | bytes 122888 | tf_op jit(solution)/shard_map/ppermute | solution.py:460
  8.6 1.0 %collective-permute-start.6 = (bf16[1,32,640]{2,1,0:T(8,128)(2,1)S(1)}, bf16[1,32,640]{2,1,0:T(8,128)(2,1)S(1)}, u32[]{:S(2)}, u32[]{:S(2)}) collective-permute-start(bf16[1,32,640]{2,1,0:T(8,128)(2,1)S(1)} %shard_map.140.refs_0_), channel_id=1, source_target_pairs={{5,0},{4,1},{7,2},{6,3},{1,4},{0,5},{3,6},{2,7},{13,8},{12,9},{15,... | collective-permute-start | bytes 122888 | tf_op jit(solution)/shard_map/ppermute | solution.py:460
  9.5 0.1 shard_map.142
  9.6 0.0 collective-permute-done.4.refs_5_
  9.7 0.7 %collective-permute-start.5 = (bf16[1,32,640]{2,1,0:T(8,128)(2,1)S(1)}, bf16[1,32,640]{2,1,0:T(8,128)(2,1)S(1)}, u32[]{:S(2)}, u32[]{:S(2)}) collective-permute-start(bf16[1,32,640]{2,1,0:T(8,128)(2,1)S(1)} %collective-permute-done.4.refs_5_), channel_id=1, source_target_pairs={{0,1},{1,0},{2,3},{3,2},{4,5},{5,4},{6,7},{7,6},{8,9},{9,8},{10,11... | collective-permute-start | bytes 122888 | tf_op jit(solution)/shard_map/ppermute | solution.py:463
  10.4 0.5 %collective-permute-done.2.refs_3_ = bf16[1,32,640]{2,1,0:T(8,128)(2,1)S(1)} collective-permute-done((bf16[1,32,640]{2,1,0:T(8,128)(2,1)S(1)}, bf16[1,32,640]{2,1,0:T(8,128)(2,1)S(1)}, u32[]{:S(2)}, u32[]{:S(2)}) %collective-permute-start.2) | collective-permute-done | bytes 40992 | tf_op jit(solution)/shard_map/ppermute | solution.py:460
  10.9 0.0 collective-permute-start.3
  10.9 0.8 %collective-permute-done.refs_1_ = bf16[1,32,640]{2,1,0:T(8,128)(2,1)S(1)} collective-permute-done((bf16[1,32,640]{2,1,0:T(8,128)(2,1)S(1)}, bf16[1,32,640]{2,1,0:T(8,128)(2,1)S(1)}, u32[]{:S(2)}, u32[]{:S(2)}) %collective-permute-start) | collective-permute-done | bytes 40992 | tf_op jit(solution)/shard_map/ppermute | solution.py:460
  11.7 0.0 collective-permute-start.1
  11.7 0.3 %collective-permute-done.6.refs_7_ = bf16[1,32,640]{2,1,0:T(8,128)(2,1)S(1)} collective-permute-done((bf16[1,32,640]{2,1,0:T(8,128)(2,1)S(1)}, bf16[1,32,640]{2,1,0:T(8,128)(2,1)S(1)}, u32[]{:S(2)}, u32[]{:S(2)}) %collective-permute-start.6) | collective-permute-done | bytes 40992 | tf_op jit(solution)/shard_map/ppermute | solution.py:460
  12.0 0.1 collective-permute-done.3.refs_4_
  12.1 0.8 %collective-permute-done.1.refs_2_ = bf16[1,32,640]{2,1,0:T(8,128)(2,1)S(1)} collective-permute-done((bf16[1,32,640]{2,1,0:T(8,128)(2,1)S(1)}, bf16[1,32,640]{2,1,0:T(8,128)(2,1)S(1)}, u32[]{:S(2)}, u32[]{:S(2)}) %collective-permute-start.1) | collective-permute-done | bytes 40992 | tf_op jit(solution)/shard_map/ppermute | solution.py:463
  12.9 1.5 %shard_map.143 = (f32[8,640]{1,0:T(8,128)S(1)}, f32[8,512]{1,0:T(8,128)S(1)}, f32[8,640]{1,0:T(8,128)S(1)}, f32[8,512]{1,0:T(8,128)S(1)}) custom-call(bf16[1,32,640]{2,1,0:T(8,128)(2,1)S(1)} %shard_map.140.refs_0_, bf16[1,32,640]{2,1,0:T(8,128)(2,1)S(1)} %collective-permute-done.refs_1_, bf16[1,32,640]{2,1,0:T(8,128)(2,1)S(1)} %collective-permute-done.1.refs_2_, ...), custom_call_target="tpu_custom_call" | custom-call | tf_op jit(solution)/shard_map/pallas_call | solution.py:484
  14.4 0.2 %collective-permute-start.7 = (f32[8,640]{1,0:T(8,128)S(1)}, f32[8,640]{1,0:T(8,128)S(1)}, u32[]{:S(2)}, u32[]{:S(2)}) collective-permute-start(f32[8,640]{1,0:T(8,128)S(1)} %get-tuple-element.141), channel_id=1, source_target_pairs={{0,1},{1,0},{2,3},{3,2},{4,5},{5,4},{6,7},{7,6},{8,9},{9,8},{10,11... | collective-permute-start | bytes 61448 | tf_op jit(solution)/shard_map/ppermute | solution.py:463
  14.6 1.0 %collective-permute-done.7 = f32[8,640]{1,0:T(8,128)S(1)} collective-permute-done((f32[8,640]{1,0:T(8,128)S(1)}, f32[8,640]{1,0:T(8,128)S(1)}, u32[]{:S(2)}, u32[]{:S(2)}) %collective-permute-start.7) | collective-permute-done | bytes 20512 | tf_op jit(solution)/shard_map/ppermute | solution.py:463
  15.7 1.4 %collective-permute-start.8 = (f32[8,640]{1,0:T(8,128)S(1)}, f32[8,640]{1,0:T(8,128)S(1)}, u32[]{:S(2)}, u32[]{:S(2)}) collective-permute-start(f32[8,640]{1,0:T(8,128)S(1)} %add.3.over), channel_id=1, source_target_pairs={{0,3},{1,2},{2,1},{3,0},{4,7},{5,6},{6,5},{7,4},{8,11},{9,10},{10,... | collective-permute-start | bytes 61448 | tf_op jit(solution)/shard_map/ppermute | solution.py:492
  17.0 0.3 %collective-permute-start.9 = (f32[8,512]{1,0:T(8,128)S(1)}, f32[8,512]{1,0:T(8,128)S(1)}, u32[]{:S(2)}, u32[]{:S(2)}) collective-permute-start(f32[8,512]{1,0:T(8,128)S(1)} %get-tuple-element.143), channel_id=1, source_target_pairs={{0,1},{1,0},{2,3},{3,2},{4,5},{5,4},{6,7},{7,6},{8,9},{9,8},{10,11... | collective-permute-start | bytes 49160 | tf_op jit(solution)/shard_map/ppermute | solution.py:463
  17.4 0.8 %collective-permute-done.9.other_stay = f32[8,512]{1,0:T(8,128)S(1)} collective-permute-done((f32[8,512]{1,0:T(8,128)S(1)}, f32[8,512]{1,0:T(8,128)S(1)}, u32[]{:S(2)}, u32[]{:S(2)}) %collective-permute-start.9) | collective-permute-done | bytes 16416 | tf_op jit(solution)/shard_map/ppermute | solution.py:463
  18.2 0.6 %collective-permute-done.8.arrived = f32[8,640]{1,0:T(8,128)S(1)} collective-permute-done((f32[8,640]{1,0:T(8,128)S(1)}, f32[8,640]{1,0:T(8,128)S(1)}, u32[]{:S(2)}, u32[]{:S(2)}) %collective-permute-start.8) | collective-permute-done | bytes 20512 | tf_op jit(solution)/shard_map/ppermute | solution.py:492
  18.9 0.6 %shard_map.144 = (bf16[2,4,512]{2,1,0:T(4,128)(2,1)}, f32[1,16]{1,0:T(1,128)}) custom-call(f32[8,640]{1,0:T(8,128)S(1)} %add.3.over, f32[8,640]{1,0:T(8,128)S(1)} %collective-permute-done.8.arrived, f32[8,512]{1,0:T(8,128)S(1)} %get-tuple-element.142.stay, f32[8,512]{1,0:T(8,128)S(1)} %collective-permute-done.9.other_stay), custom_call_target="tpu_custom_call" | custom-call | tf_op jit(solution)/shard_map/pallas_call | solution.py:494
  (2 shorter events, 0.0 us)
Async XLA Ops:
  3.2 6.5 %collective-permute-start.4 = (bf16[1,32,640]{2,1,0:T(8,128)(2,1)S(1)}, bf16[1,32,640]{2,1,0:T(8,128)(2,1)S(1)}, u32[]{:S(2)}, u32[]{:S(2)}) collective-permute-start(bf16[1,32,640]{2,1,0:T(8,128)(2,1)S(1)} %shard_map.140.refs_0_), channel_id=1, source_target_pairs={{24,0},{29,1},{26,2},{31,3},{28,4},{25,5},{30,6},{27,7},{0,8},{5,9... | collective-permute-start | bytes 122888 | tf_op jit(solution)/shard_map/ppermute | solution.py:460
  4.6 6.3 %collective-permute-start.2 = (bf16[1,32,640]{2,1,0:T(8,128)(2,1)S(1)}, bf16[1,32,640]{2,1,0:T(8,128)(2,1)S(1)}, u32[]{:S(2)}, u32[]{:S(2)}) collective-permute-start(bf16[1,32,640]{2,1,0:T(8,128)(2,1)S(1)} %shard_map.140.refs_0_), channel_id=1, source_target_pairs={{16,0},{21,1},{18,2},{23,3},{20,4},{17,5},{22,6},{19,7},{24,8},{29... | collective-permute-start | bytes 122888 | tf_op jit(solution)/shard_map/ppermute | solution.py:460
  7.2 4.5 %collective-permute-start = (bf16[1,32,640]{2,1,0:T(8,128)(2,1)S(1)}, bf16[1,32,640]{2,1,0:T(8,128)(2,1)S(1)}, u32[]{:S(2)}, u32[]{:S(2)}) collective-permute-start(bf16[1,32,640]{2,1,0:T(8,128)(2,1)S(1)} %shard_map.140.refs_0_), channel_id=1, source_target_pairs={{8,0},{13,1},{10,2},{15,3},{12,4},{9,5},{14,6},{11,7},{16,8},{21,9... | collective-permute-start | bytes 122888 | tf_op jit(solution)/shard_map/ppermute | solution.py:460
  8.6 3.4 %collective-permute-start.6 = (bf16[1,32,640]{2,1,0:T(8,128)(2,1)S(1)}, bf16[1,32,640]{2,1,0:T(8,128)(2,1)S(1)}, u32[]{:S(2)}, u32[]{:S(2)}) collective-permute-start(bf16[1,32,640]{2,1,0:T(8,128)(2,1)S(1)} %shard_map.140.refs_0_), channel_id=1, source_target_pairs={{5,0},{4,1},{7,2},{6,3},{1,4},{0,5},{3,6},{2,7},{13,8},{12,9},{15,... | collective-permute-start | bytes 122888 | tf_op jit(solution)/shard_map/ppermute | solution.py:460
  9.7 2.4 %collective-permute-start.5 = (bf16[1,32,640]{2,1,0:T(8,128)(2,1)S(1)}, bf16[1,32,640]{2,1,0:T(8,128)(2,1)S(1)}, u32[]{:S(2)}, u32[]{:S(2)}) collective-permute-start(bf16[1,32,640]{2,1,0:T(8,128)(2,1)S(1)} %collective-permute-done.4.refs_5_), channel_id=1, source_target_pairs={{0,1},{1,0},{2,3},{3,2},{4,5},{5,4},{6,7},{7,6},{8,9},{9,8},{10,11... | collective-permute-start | bytes 122888 | tf_op jit(solution)/shard_map/ppermute | solution.py:463
  10.9 1.2 %collective-permute-start.3 = (bf16[1,32,640]{2,1,0:T(8,128)(2,1)S(1)}, bf16[1,32,640]{2,1,0:T(8,128)(2,1)S(1)}, u32[]{:S(2)}, u32[]{:S(2)}) collective-permute-start(bf16[1,32,640]{2,1,0:T(8,128)(2,1)S(1)} %collective-permute-done.2.refs_3_), channel_id=1, source_target_pairs={{0,1},{1,0},{2,3},{3,2},{4,5},{5,4},{6,7},{7,6},{8,9},{9,8},{10,11... | collective-permute-start | bytes 122888 | tf_op jit(solution)/shard_map/ppermute | solution.py:463
  11.7 1.2 %collective-permute-start.1 = (bf16[1,32,640]{2,1,0:T(8,128)(2,1)S(1)}, bf16[1,32,640]{2,1,0:T(8,128)(2,1)S(1)}, u32[]{:S(2)}, u32[]{:S(2)}) collective-permute-start(bf16[1,32,640]{2,1,0:T(8,128)(2,1)S(1)} %collective-permute-done.refs_1_), channel_id=1, source_target_pairs={{0,1},{1,0},{2,3},{3,2},{4,5},{5,4},{6,7},{7,6},{8,9},{9,8},{10,11... | collective-permute-start | bytes 122888 | tf_op jit(solution)/shard_map/ppermute | solution.py:463
  14.4 1.2 %collective-permute-start.7 = (f32[8,640]{1,0:T(8,128)S(1)}, f32[8,640]{1,0:T(8,128)S(1)}, u32[]{:S(2)}, u32[]{:S(2)}) collective-permute-start(f32[8,640]{1,0:T(8,128)S(1)} %get-tuple-element.141), channel_id=1, source_target_pairs={{0,1},{1,0},{2,3},{3,2},{4,5},{5,4},{6,7},{7,6},{8,9},{9,8},{10,11... | collective-permute-start | bytes 61448 | tf_op jit(solution)/shard_map/ppermute | solution.py:463
  15.7 3.2 %collective-permute-start.8 = (f32[8,640]{1,0:T(8,128)S(1)}, f32[8,640]{1,0:T(8,128)S(1)}, u32[]{:S(2)}, u32[]{:S(2)}) collective-permute-start(f32[8,640]{1,0:T(8,128)S(1)} %add.3.over), channel_id=1, source_target_pairs={{0,3},{1,2},{2,1},{3,0},{4,7},{5,6},{6,5},{7,4},{8,11},{9,10},{10,... | collective-permute-start | bytes 61448 | tf_op jit(solution)/shard_map/ppermute | solution.py:492
  17.0 1.2 %collective-permute-start.9 = (f32[8,512]{1,0:T(8,128)S(1)}, f32[8,512]{1,0:T(8,128)S(1)}, u32[]{:S(2)}, u32[]{:S(2)}) collective-permute-start(f32[8,512]{1,0:T(8,128)S(1)} %get-tuple-element.143), channel_id=1, source_target_pairs={{0,1},{1,0},{2,3},{3,2},{4,5},{5,4},{6,7},{7,6},{8,9},{9,8},{10,11... | collective-permute-start | bytes 49160 | tf_op jit(solution)/shard_map/ppermute | solution.py:463

commit v7 on v6

--- a/solution.py
+++ b/solution.py
@@ -212,10 +212,12 @@
 def prepare(rounds, cells, counts, *refs):
     order_in, mask_in, *copied = refs[: counts + 2]
     rest = refs[counts + 2 :]
-    w_read, w_down, w_out, gain, w_query, w_key, w_gate, w_up = rest[:8]
-    w_value_t, read_down, read_out = rest[8:11]
-    picks, token_picks, place, tile_bias, divisor = rest[11:16]
-    order, mask, w_value, arrivals = rest[16:]
+    w_read, w_down, w_out, gain, w_gate, w_up, w_query_key = rest[:7]
+    w_value_t, read_down, read_out = rest[7:10]
+    picks, token_picks, place, tile_bias, divisor = rest[10:15]
+    order, mask, w_value, arrivals = rest[15:]
+    half = w_query_key.shape[1] // 2
+    w_query, w_key = w_query_key.at[:, :half], w_query_key.at[:, half:]
     targets = (order, mask, w_read, w_value, w_down, w_out, gain, w_query, w_key, w_gate, w_up)
     copies = [
         pltpu.make_async_copy(source, target, arrivals.at[k])
@@ -286,13 +288,13 @@
 
 def layer_kernel(cells, slots, *refs):
     blocks, rest = refs[:slots], refs[slots:]
-    w_read, w_down, w_out, gain, w_query, w_key, w_gate, w_up = rest[:8]
-    w_value_t, read_down, read_out = rest[8:11]
-    picks, token_picks, place, tile_bias, divisor = rest[11:16]
-    outs = rest[16:]
+    w_read, w_down, w_out, gain, w_gate, w_up, w_query_key = rest[:7]
+    w_value_t, read_down, read_out = rest[7:10]
+    picks, token_picks, place, tile_bias, divisor = rest[10:15]
+    outs = rest[15:]
     total = slots * cells
     width = gain.shape[1]
-    head_width = w_query.shape[1]
+    head_width = w_query_key.shape[1] // 2
     observables = divisor.shape[0]
     tile_rows = picks.shape[0] - observables
 
@@ -306,9 +308,10 @@
     spread = jnp.mean(values * values, axis=-1, keepdims=True)
     normed = (values * lax.rsqrt(spread + norm_eps) * gain[...]).astype(jnp.bfloat16)
 
-    queries = (dot(normed, w_query[...]) * (1.0 / math.sqrt(HDIM))).astype(jnp.bfloat16)
-    keys = dot(normed, w_key[...]).astype(jnp.bfloat16)
     vals = dot_t(w_value_t[...], normed).astype(jnp.bfloat16)
+    query_key = dot(normed, w_query_key[...])
+    keys = query_key[:, head_width:].astype(jnp.bfloat16)
+    queries = (query_key[:, :head_width] * (1.0 / math.sqrt(HDIM))).astype(jnp.bfloat16)
 
     gate = dot(normed, w_gate[...])
     up = dot(normed, w_up[...])
@@ -409,7 +412,8 @@
         w_up,
     ]
     sources = pin([cell_order.reshape(1, -1), obs_mask, *brought], pltpu.HBM)
-    made = [pltpu.VMEM(array.shape, array.dtype) for array in brought if array is not w_value] + [
+    made = [pltpu.VMEM(array.shape, array.dtype) for array in brought if not any(array is w for w in (w_value, w_query, w_key))] + [
+        pltpu.VMEM((width, 2 * w_query.shape[1]), w_query.dtype),
         pltpu.VMEM(w_value.shape[::-1], w_value.dtype),
         pltpu.VMEM((1, w_down.shape[0]), jnp.float32),
         pltpu.VMEM((1, w_out.shape[0]), jnp.float32),

time: 19.7 us -> 19.7 us (level)
  no operation moved by 1% of the time
where the time goes in v7:
time: 19.7 us; the launch traced here: 19.5 us
  starting transfers between devices  9.07 us (46%)
  waiting for transfers between devices  5 us (25%)
  Pallas kernels  4.74 us (24%)
  between operations  0.68 us (3%)
    ppermute x4, starting transfers between devices, fetch(): return lax.ppermute(block, ('round', 'mp'), pairs)  6.37 us
    ppermute x5, waiting for transfers between devices, other_core(): return lax.ppermute(array, 'mp', [(m, m ^ 1) for m in range(models)])  2.76 us
    pallas_call x1, Pallas kernels, shards_whole(): pl.pallas_call(functools.partial(early_kernel, preparation), out_shape=ma...  1.73 us
    ppermute x4, waiting for transfers between devices, fetch(): return lax.ppermute(block, ('round', 'mp'), pairs)  1.6 us
    pallas_call x1, Pallas kernels, shards_whole(): pl.pallas_call(functools.partial(layer_kernel, cells, len(blocks)), out_s...  1.51 us
    ppermute x1, starting transfers between devices, shards_whole(): arrived = lax.ppermute(over, 'mp', [(m, m ^ 3) for m in range(models)])  1.38 us
    ppermute x5, starting transfers between devices, other_core(): return lax.ppermute(array, 'mp', [(m, m ^ 1) for m in range(models)])  1.32 us
    pallas_call x1, Pallas kernels, shards_whole(): pl.pallas_call(pack_kernel, out_shape=pltpu.VMEM((1, cells, width + LANES...  0.79 us
  transfers between devices with their start and end apart: 10, of which 8 were waited for; matrix products, arithmetic and copies ran while one was open for 0% of the time, Pallas kernels for 1%

profile of v7, /device:TPU:0, one launch (start us, length us, event | category | flops | bytes accessed | tf_op | source)
XLA Modules:
  0.0 19.5 jit_solution(13525384225548583162)
XLA Ops:
  0.6 0.8 %shard_map.140.refs_0_ = bf16[1,32,640]{2,1,0:T(8,128)(2,1)S(1)} custom-call(bf16[1,32,512]{2,1,0:T(8,128)(2,1)} %tokens.1, s32[1,2,8]{2,1,0:T(2,128)} %bitcast.11), custom_call_target="tpu_custom_call" | custom-call | tf_op jit(solution)/shard_map/pallas_call | solution.py:434
  1.4 1.7 %shard_map.141 = (f32[1,512]{1,0:T(1,128)S(1)}, bf16[512,512]{1,0:T(8,128)(2,1)S(1)}, bf16[128,512]{1,0:T(8,128)(2,1)S(1)}, f32[1,512]{1,0:T(1,128)S(1)}, bf16[5...) custom-call(s32[1,32]{1,0:T(1,128)} %bitcast.9, ...), custom_call_target="tpu_custom_call" | custom-call | tf_op jit(solution)/shard_map/pallas_call | solution.py:446
  3.2 1.5 %collective-permute-start.4 = (bf16[1,32,640]{2,1,0:T(8,128)(2,1)S(1)}, bf16[1,32,640]{2,1,0:T(8,128)(2,1)S(1)}, u32[]{:S(2)}, u32[]{:S(2)}) collective-permute-start(bf16[1,32,640]{2,1,0:T(8,128)(2,1)S(1)} %shard_map.140.refs_0_), channel_id=1, source_target_pairs={{24,0},{29,1},{26,2},{31,3},{28,4},{25,5},{30,6},{27,7},{0,8},{5,9... | collective-permute-start | bytes 122888 | tf_op jit(solution)/shard_map/ppermute | solution.py:464
  4.6 2.6 %collective-permute-start.2 = (bf16[1,32,640]{2,1,0:T(8,128)(2,1)S(1)}, bf16[1,32,640]{2,1,0:T(8,128)(2,1)S(1)}, u32[]{:S(2)}, u32[]{:S(2)}) collective-permute-start(bf16[1,32,640]{2,1,0:T(8,128)(2,1)S(1)} %shard_map.140.refs_0_), channel_id=1, source_target_pairs={{16,0},{21,1},{18,2},{23,3},{20,4},{17,5},{22,6},{19,7},{24,8},{29... | collective-permute-start | bytes 122888 | tf_op jit(solution)/shard_map/ppermute | solution.py:464
  7.2 1.3 %collective-permute-start = (bf16[1,32,640]{2,1,0:T(8,128)(2,1)S(1)}, bf16[1,32,640]{2,1,0:T(8,128)(2,1)S(1)}, u32[]{:S(2)}, u32[]{:S(2)}) collective-permute-start(bf16[1,32,640]{2,1,0:T(8,128)(2,1)S(1)} %shard_map.140.refs_0_), channel_id=1, source_target_pairs={{8,0},{13,1},{10,2},{15,3},{12,4},{9,5},{14,6},{11,7},{16,8},{21,9... | collective-permute-start | bytes 122888 | tf_op jit(solution)/shard_map/ppermute | solution.py:464
  8.6 1.0 %collective-permute-start.6 = (bf16[1,32,640]{2,1,0:T(8,128)(2,1)S(1)}, bf16[1,32,640]{2,1,0:T(8,128)(2,1)S(1)}, u32[]{:S(2)}, u32[]{:S(2)}) collective-permute-start(bf16[1,32,640]{2,1,0:T(8,128)(2,1)S(1)} %shard_map.140.refs_0_), channel_id=1, source_target_pairs={{5,0},{4,1},{7,2},{6,3},{1,4},{0,5},{3,6},{2,7},{13,8},{12,9},{15,... | collective-permute-start | bytes 122888 | tf_op jit(solution)/shard_map/ppermute | solution.py:464
  9.5 0.1 shard_map.142
  9.6 0.0 collective-permute-done.4.refs_5_
  9.7 0.7 %collective-permute-start.5 = (bf16[1,32,640]{2,1,0:T(8,128)(2,1)S(1)}, bf16[1,32,640]{2,1,0:T(8,128)(2,1)S(1)}, u32[]{:S(2)}, u32[]{:S(2)}) collective-permute-start(bf16[1,32,640]{2,1,0:T(8,128)(2,1)S(1)} %collective-permute-done.4.refs_5_), channel_id=1, source_target_pairs={{0,1},{1,0},{2,3},{3,2},{4,5},{5,4},{6,7},{7,6},{8,9},{9,8},{10,11... | collective-permute-start | bytes 122888 | tf_op jit(solution)/shard_map/ppermute | solution.py:467
  10.4 0.5 %collective-permute-done.2.refs_3_ = bf16[1,32,640]{2,1,0:T(8,128)(2,1)S(1)} collective-permute-done((bf16[1,32,640]{2,1,0:T(8,128)(2,1)S(1)}, bf16[1,32,640]{2,1,0:T(8,128)(2,1)S(1)}, u32[]{:S(2)}, u32[]{:S(2)}) %collective-permute-start.2) | collective-permute-done | bytes 40992 | tf_op jit(solution)/shard_map/ppermute | solution.py:464
  10.9 0.0 collective-permute-start.3
  10.9 0.8 %collective-permute-done.refs_1_ = bf16[1,32,640]{2,1,0:T(8,128)(2,1)S(1)} collective-permute-done((bf16[1,32,640]{2,1,0:T(8,128)(2,1)S(1)}, bf16[1,32,640]{2,1,0:T(8,128)(2,1)S(1)}, u32[]{:S(2)}, u32[]{:S(2)}) %collective-permute-start) | collective-permute-done | bytes 40992 | tf_op jit(solution)/shard_map/ppermute | solution.py:464
  11.7 0.0 collective-permute-start.1
  11.7 0.3 %collective-permute-done.6.refs_7_ = bf16[1,32,640]{2,1,0:T(8,128)(2,1)S(1)} collective-permute-done((bf16[1,32,640]{2,1,0:T(8,128)(2,1)S(1)}, bf16[1,32,640]{2,1,0:T(8,128)(2,1)S(1)}, u32[]{:S(2)}, u32[]{:S(2)}) %collective-permute-start.6) | collective-permute-done | bytes 40992 | tf_op jit(solution)/shard_map/ppermute | solution.py:464
  12.0 0.1 collective-permute-done.3.refs_4_
  12.1 0.8 %collective-permute-done.1.refs_2_ = bf16[1,32,640]{2,1,0:T(8,128)(2,1)S(1)} collective-permute-done((bf16[1,32,640]{2,1,0:T(8,128)(2,1)S(1)}, bf16[1,32,640]{2,1,0:T(8,128)(2,1)S(1)}, u32[]{:S(2)}, u32[]{:S(2)}) %collective-permute-start.1) | collective-permute-done | bytes 40992 | tf_op jit(solution)/shard_map/ppermute | solution.py:467
  12.9 1.5 %shard_map.143 = (f32[8,640]{1,0:T(8,128)S(1)}, f32[8,512]{1,0:T(8,128)S(1)}, f32[8,640]{1,0:T(8,128)S(1)}, f32[8,512]{1,0:T(8,128)S(1)}) custom-call(bf16[1,32,640]{2,1,0:T(8,128)(2,1)S(1)} %shard_map.140.refs_0_, bf16[1,32,640]{2,1,0:T(8,128)(2,1)S(1)} %collective-permute-done.refs_1_, bf16[1,32,640]{2,1,0:T(8,128)(2,1)S(1)} %collective-permute-done.1.refs_2_, ...), custom_call_target="tpu_custom_call" | custom-call | tf_op jit(solution)/shard_map/pallas_call | solution.py:488
  14.4 0.2 %collective-permute-start.7 = (f32[8,640]{1,0:T(8,128)S(1)}, f32[8,640]{1,0:T(8,128)S(1)}, u32[]{:S(2)}, u32[]{:S(2)}) collective-permute-start(f32[8,640]{1,0:T(8,128)S(1)} %get-tuple-element.133), channel_id=1, source_target_pairs={{0,1},{1,0},{2,3},{3,2},{4,5},{5,4},{6,7},{7,6},{8,9},{9,8},{10,11... | collective-permute-start | bytes 61448 | tf_op jit(solution)/shard_map/ppermute | solution.py:467
  14.6 1.0 %collective-permute-done.7 = f32[8,640]{1,0:T(8,128)S(1)} collective-permute-done((f32[8,640]{1,0:T(8,128)S(1)}, f32[8,640]{1,0:T(8,128)S(1)}, u32[]{:S(2)}, u32[]{:S(2)}) %collective-permute-start.7) | collective-permute-done | bytes 20512 | tf_op jit(solution)/shard_map/ppermute | solution.py:467
  15.7 1.4 %collective-permute-start.8 = (f32[8,640]{1,0:T(8,128)S(1)}, f32[8,640]{1,0:T(8,128)S(1)}, u32[]{:S(2)}, u32[]{:S(2)}) collective-permute-start(f32[8,640]{1,0:T(8,128)S(1)} %add.3.over), channel_id=1, source_target_pairs={{0,3},{1,2},{2,1},{3,0},{4,7},{5,6},{6,5},{7,4},{8,11},{9,10},{10,... | collective-permute-start | bytes 61448 | tf_op jit(solution)/shard_map/ppermute | solution.py:496
  17.1 0.3 %collective-permute-start.9 = (f32[8,512]{1,0:T(8,128)S(1)}, f32[8,512]{1,0:T(8,128)S(1)}, u32[]{:S(2)}, u32[]{:S(2)}) collective-permute-start(f32[8,512]{1,0:T(8,128)S(1)} %get-tuple-element.135), channel_id=1, source_target_pairs={{0,1},{1,0},{2,3},{3,2},{4,5},{5,4},{6,7},{7,6},{8,9},{9,8},{10,11... | collective-permute-start | bytes 49160 | tf_op jit(solution)/shard_map/ppermute | solution.py:467
  17.4 0.8 %collective-permute-done.9.other_stay = f32[8,512]{1,0:T(8,128)S(1)} collective-permute-done((f32[8,512]{1,0:T(8,128)S(1)}, f32[8,512]{1,0:T(8,128)S(1)}, u32[]{:S(2)}, u32[]{:S(2)}) %collective-permute-start.9) | collective-permute-done | bytes 16416 | tf_op jit(solution)/shard_map/ppermute | solution.py:467
  18.2 0.6 %collective-permute-done.8.arrived = f32[8,640]{1,0:T(8,128)S(1)} collective-permute-done((f32[8,640]{1,0:T(8,128)S(1)}, f32[8,640]{1,0:T(8,128)S(1)}, u32[]{:S(2)}, u32[]{:S(2)}) %collective-permute-start.8) | collective-permute-done | bytes 20512 | tf_op jit(solution)/shard_map/ppermute | solution.py:496
  18.9 0.6 %shard_map.144 = (bf16[2,4,512]{2,1,0:T(4,128)(2,1)}, f32[1,16]{1,0:T(1,128)}) custom-call(f32[8,640]{1,0:T(8,128)S(1)} %add.3.over, f32[8,640]{1,0:T(8,128)S(1)} %collective-permute-done.8.arrived, f32[8,512]{1,0:T(8,128)S(1)} %get-tuple-element.134.stay, f32[8,512]{1,0:T(8,128)S(1)} %collective-permute-done.9.other_stay), custom_call_target="tpu_custom_call" | custom-call | tf_op jit(solution)/shard_map/pallas_call | solution.py:498
  (2 shorter events, 0.0 us)
Async XLA Ops:
  3.2 6.5 %collective-permute-start.4 = (bf16[1,32,640]{2,1,0:T(8,128)(2,1)S(1)}, bf16[1,32,640]{2,1,0:T(8,128)(2,1)S(1)}, u32[]{:S(2)}, u32[]{:S(2)}) collective-permute-start(bf16[1,32,640]{2,1,0:T(8,128)(2,1)S(1)} %shard_map.140.refs_0_), channel_id=1, source_target_pairs={{24,0},{29,1},{26,2},{31,3},{28,4},{25,5},{30,6},{27,7},{0,8},{5,9... | collective-permute-start | bytes 122888 | tf_op jit(solution)/shard_map/ppermute | solution.py:464
  4.6 6.3 %collective-permute-start.2 = (bf16[1,32,640]{2,1,0:T(8,128)(2,1)S(1)}, bf16[1,32,640]{2,1,0:T(8,128)(2,1)S(1)}, u32[]{:S(2)}, u32[]{:S(2)}) collective-permute-start(bf16[1,32,640]{2,1,0:T(8,128)(2,1)S(1)} %shard_map.140.refs_0_), channel_id=1, source_target_pairs={{16,0},{21,1},{18,2},{23,3},{20,4},{17,5},{22,6},{19,7},{24,8},{29... | collective-permute-start | bytes 122888 | tf_op jit(solution)/shard_map/ppermute | solution.py:464
  7.2 4.5 %collective-permute-start = (bf16[1,32,640]{2,1,0:T(8,128)(2,1)S(1)}, bf16[1,32,640]{2,1,0:T(8,128)(2,1)S(1)}, u32[]{:S(2)}, u32[]{:S(2)}) collective-permute-start(bf16[1,32,640]{2,1,0:T(8,128)(2,1)S(1)} %shard_map.140.refs_0_), channel_id=1, source_target_pairs={{8,0},{13,1},{10,2},{15,3},{12,4},{9,5},{14,6},{11,7},{16,8},{21,9... | collective-permute-start | bytes 122888 | tf_op jit(solution)/shard_map/ppermute | solution.py:464
  8.6 3.4 %collective-permute-start.6 = (bf16[1,32,640]{2,1,0:T(8,128)(2,1)S(1)}, bf16[1,32,640]{2,1,0:T(8,128)(2,1)S(1)}, u32[]{:S(2)}, u32[]{:S(2)}) collective-permute-start(bf16[1,32,640]{2,1,0:T(8,128)(2,1)S(1)} %shard_map.140.refs_0_), channel_id=1, source_target_pairs={{5,0},{4,1},{7,2},{6,3},{1,4},{0,5},{3,6},{2,7},{13,8},{12,9},{15,... | collective-permute-start | bytes 122888 | tf_op jit(solution)/shard_map/ppermute | solution.py:464
  9.7 2.4 %collective-permute-start.5 = (bf16[1,32,640]{2,1,0:T(8,128)(2,1)S(1)}, bf16[1,32,640]{2,1,0:T(8,128)(2,1)S(1)}, u32[]{:S(2)}, u32[]{:S(2)}) collective-permute-start(bf16[1,32,640]{2,1,0:T(8,128)(2,1)S(1)} %collective-permute-done.4.refs_5_), channel_id=1, source_target_pairs={{0,1},{1,0},{2,3},{3,2},{4,5},{5,4},{6,7},{7,6},{8,9},{9,8},{10,11... | collective-permute-start | bytes 122888 | tf_op jit(solution)/shard_map/ppermute | solution.py:467
  10.9 1.2 %collective-permute-start.3 = (bf16[1,32,640]{2,1,0:T(8,128)(2,1)S(1)}, bf16[1,32,640]{2,1,0:T(8,128)(2,1)S(1)}, u32[]{:S(2)}, u32[]{:S(2)}) collective-permute-start(bf16[1,32,640]{2,1,0:T(8,128)(2,1)S(1)} %collective-permute-done.2.refs_3_), channel_id=1, source_target_pairs={{0,1},{1,0},{2,3},{3,2},{4,5},{5,4},{6,7},{7,6},{8,9},{9,8},{10,11... | collective-permute-start | bytes 122888 | tf_op jit(solution)/shard_map/ppermute | solution.py:467
  11.7 1.2 %collective-permute-start.1 = (bf16[1,32,640]{2,1,0:T(8,128)(2,1)S(1)}, bf16[1,32,640]{2,1,0:T(8,128)(2,1)S(1)}, u32[]{:S(2)}, u32[]{:S(2)}) collective-permute-start(bf16[1,32,640]{2,1,0:T(8,128)(2,1)S(1)} %collective-permute-done.refs_1_), channel_id=1, source_target_pairs={{0,1},{1,0},{2,3},{3,2},{4,5},{5,4},{6,7},{7,6},{8,9},{9,8},{10,11... | collective-permute-start | bytes 122888 | tf_op jit(solution)/shard_map/ppermute | solution.py:467
  14.4 1.3 %collective-permute-start.7 = (f32[8,640]{1,0:T(8,128)S(1)}, f32[8,640]{1,0:T(8,128)S(1)}, u32[]{:S(2)}, u32[]{:S(2)}) collective-permute-start(f32[8,640]{1,0:T(8,128)S(1)} %get-tuple-element.133), channel_id=1, source_target_pairs={{0,1},{1,0},{2,3},{3,2},{4,5},{5,4},{6,7},{7,6},{8,9},{9,8},{10,11... | collective-permute-start | bytes 61448 | tf_op jit(solution)/shard_map/ppermute | solution.py:467
  15.7 3.2 %collective-permute-start.8 = (f32[8,640]{1,0:T(8,128)S(1)}, f32[8,640]{1,0:T(8,128)S(1)}, u32[]{:S(2)}, u32[]{:S(2)}) collective-permute-start(f32[8,640]{1,0:T(8,128)S(1)} %add.3.over), channel_id=1, source_target_pairs={{0,3},{1,2},{2,1},{3,0},{4,7},{5,6},{6,5},{7,4},{8,11},{9,10},{10,... | collective-permute-start | bytes 61448 | tf_op jit(solution)/shard_map/ppermute | solution.py:496
  17.1 1.2 %collective-permute-start.9 = (f32[8,512]{1,0:T(8,128)S(1)}, f32[8,512]{1,0:T(8,128)S(1)}, u32[]{:S(2)}, u32[]{:S(2)}) collective-permute-start(f32[8,512]{1,0:T(8,128)S(1)} %get-tuple-element.135), channel_id=1, source_target_pairs={{0,1},{1,0},{2,3},{3,2},{4,5},{5,4},{6,7},{7,6},{8,9},{9,8},{10,11... | collective-permute-start | bytes 49160 | tf_op jit(solution)/shard_map/ppermute | solution.py:467

commit v8 on v6

--- a/solution.py
+++ b/solution.py
@@ -306,9 +306,9 @@
     spread = jnp.mean(values * values, axis=-1, keepdims=True)
     normed = (values * lax.rsqrt(spread + norm_eps) * gain[...]).astype(jnp.bfloat16)
 
+    vals = dot_t(w_value_t[...], normed).astype(jnp.bfloat16)
     queries = (dot(normed, w_query[...]) * (1.0 / math.sqrt(HDIM))).astype(jnp.bfloat16)
     keys = dot(normed, w_key[...]).astype(jnp.bfloat16)
-    vals = dot_t(w_value_t[...], normed).astype(jnp.bfloat16)
 
     gate = dot(normed, w_gate[...])
     up = dot(normed, w_up[...])

time: 19.7 us -> 19.8 us (level)
  no operation moved by 1% of the time
where the time goes in v8:
time: 19.8 us; the launch traced here: 19.6 us
  starting transfers between devices  9.07 us (46%)
  waiting for transfers between devices  5 us (25%)
  Pallas kernels  4.81 us (24%)
  between operations  0.68 us (3%)
    ppermute x4, starting transfers between devices, fetch(): return lax.ppermute(block, ('round', 'mp'), pairs)  6.37 us
    ppermute x5, waiting for transfers between devices, other_core(): return lax.ppermute(array, 'mp', [(m, m ^ 1) for m in range(models)])  2.76 us
    pallas_call x1, Pallas kernels, shards_whole(): pl.pallas_call(functools.partial(early_kernel, preparation), out_shape=ma...  1.73 us
    ppermute x4, waiting for transfers between devices, fetch(): return lax.ppermute(block, ('round', 'mp'), pairs)  1.6 us
    pallas_call x1, Pallas kernels, shards_whole(): pl.pallas_call(functools.partial(layer_kernel, cells, len(blocks)), out_s...  1.58 us
    ppermute x1, starting transfers between devices, shards_whole(): arrived = lax.ppermute(over, 'mp', [(m, m ^ 3) for m in range(models)])  1.38 us
    ppermute x5, starting transfers between devices, other_core(): return lax.ppermute(array, 'mp', [(m, m ^ 1) for m in range(models)])  1.32 us
    pallas_call x1, Pallas kernels, shards_whole(): pl.pallas_call(pack_kernel, out_shape=pltpu.VMEM((1, cells, width + LANES...  0.79 us
  transfers between devices with their start and end apart: 10, of which 8 were waited for; matrix products, arithmetic and copies ran while one was open for 0% of the time, Pallas kernels for 1%

profile of v8, /device:TPU:0, one launch (start us, length us, event | category | flops | bytes accessed | tf_op | source)
XLA Modules:
  0.0 19.6 jit_solution(16257041039546957084)
XLA Ops:
  0.6 0.8 %shard_map.140.refs_0_ = bf16[1,32,640]{2,1,0:T(8,128)(2,1)S(1)} custom-call(bf16[1,32,512]{2,1,0:T(8,128)(2,1)} %tokens.1, s32[1,2,8]{2,1,0:T(2,128)} %bitcast.11), custom_call_target="tpu_custom_call" | custom-call | tf_op jit(solution)/shard_map/pallas_call | solution.py:430
  1.4 1.7 %shard_map.141 = (f32[1,512]{1,0:T(1,128)S(1)}, bf16[512,512]{1,0:T(8,128)(2,1)S(1)}, bf16[128,512]{1,0:T(8,128)(2,1)S(1)}, f32[1,512]{1,0:T(1,128)S(1)}, bf16[5...) custom-call(s32[1,32]{1,0:T(1,128)} %bitcast.9, ...), custom_call_target="tpu_custom_call" | custom-call | tf_op jit(solution)/shard_map/pallas_call | solution.py:442
  3.2 1.5 %collective-permute-start.4 = (bf16[1,32,640]{2,1,0:T(8,128)(2,1)S(1)}, bf16[1,32,640]{2,1,0:T(8,128)(2,1)S(1)}, u32[]{:S(2)}, u32[]{:S(2)}) collective-permute-start(bf16[1,32,640]{2,1,0:T(8,128)(2,1)S(1)} %shard_map.140.refs_0_), channel_id=1, source_target_pairs={{24,0},{29,1},{26,2},{31,3},{28,4},{25,5},{30,6},{27,7},{0,8},{5,9... | collective-permute-start | bytes 122888 | tf_op jit(solution)/shard_map/ppermute | solution.py:460
  4.6 2.6 %collective-permute-start.2 = (bf16[1,32,640]{2,1,0:T(8,128)(2,1)S(1)}, bf16[1,32,640]{2,1,0:T(8,128)(2,1)S(1)}, u32[]{:S(2)}, u32[]{:S(2)}) collective-permute-start(bf16[1,32,640]{2,1,0:T(8,128)(2,1)S(1)} %shard_map.140.refs_0_), channel_id=1, source_target_pairs={{16,0},{21,1},{18,2},{23,3},{20,4},{17,5},{22,6},{19,7},{24,8},{29... | collective-permute-start | bytes 122888 | tf_op jit(solution)/shard_map/ppermute | solution.py:460
  7.2 1.3 %collective-permute-start = (bf16[1,32,640]{2,1,0:T(8,128)(2,1)S(1)}, bf16[1,32,640]{2,1,0:T(8,128)(2,1)S(1)}, u32[]{:S(2)}, u32[]{:S(2)}) collective-permute-start(bf16[1,32,640]{2,1,0:T(8,128)(2,1)S(1)} %shard_map.140.refs_0_), channel_id=1, source_target_pairs={{8,0},{13,1},{10,2},{15,3},{12,4},{9,5},{14,6},{11,7},{16,8},{21,9... | collective-permute-start | bytes 122888 | tf_op jit(solution)/shard_map/ppermute | solution.py:460
  8.6 1.0 %collective-permute-start.6 = (bf16[1,32,640]{2,1,0:T(8,128)(2,1)S(1)}, bf16[1,32,640]{2,1,0:T(8,128)(2,1)S(1)}, u32[]{:S(2)}, u32[]{:S(2)}) collective-permute-start(bf16[1,32,640]{2,1,0:T(8,128)(2,1)S(1)} %shard_map.140.refs_0_), channel_id=1, source_target_pairs={{5,0},{4,1},{7,2},{6,3},{1,4},{0,5},{3,6},{2,7},{13,8},{12,9},{15,... | collective-permute-start | bytes 122888 | tf_op jit(solution)/shard_map/ppermute | solution.py:460
  9.5 0.1 shard_map.142
  9.6 0.0 collective-permute-done.4.refs_5_
  9.7 0.7 %collective-permute-start.5 = (bf16[1,32,640]{2,1,0:T(8,128)(2,1)S(1)}, bf16[1,32,640]{2,1,0:T(8,128)(2,1)S(1)}, u32[]{:S(2)}, u32[]{:S(2)}) collective-permute-start(bf16[1,32,640]{2,1,0:T(8,128)(2,1)S(1)} %collective-permute-done.4.refs_5_), channel_id=1, source_target_pairs={{0,1},{1,0},{2,3},{3,2},{4,5},{5,4},{6,7},{7,6},{8,9},{9,8},{10,11... | collective-permute-start | bytes 122888 | tf_op jit(solution)/shard_map/ppermute | solution.py:463
  10.4 0.5 %collective-permute-done.2.refs_3_ = bf16[1,32,640]{2,1,0:T(8,128)(2,1)S(1)} collective-permute-done((bf16[1,32,640]{2,1,0:T(8,128)(2,1)S(1)}, bf16[1,32,640]{2,1,0:T(8,128)(2,1)S(1)}, u32[]{:S(2)}, u32[]{:S(2)}) %collective-permute-start.2) | collective-permute-done | bytes 40992 | tf_op jit(solution)/shard_map/ppermute | solution.py:460
  10.9 0.0 collective-permute-start.3
  10.9 0.8 %collective-permute-done.refs_1_ = bf16[1,32,640]{2,1,0:T(8,128)(2,1)S(1)} collective-permute-done((bf16[1,32,640]{2,1,0:T(8,128)(2,1)S(1)}, bf16[1,32,640]{2,1,0:T(8,128)(2,1)S(1)}, u32[]{:S(2)}, u32[]{:S(2)}) %collective-permute-start) | collective-permute-done | bytes 40992 | tf_op jit(solution)/shard_map/ppermute | solution.py:460
  11.7 0.0 collective-permute-start.1
  11.7 0.3 %collective-permute-done.6.refs_7_ = bf16[1,32,640]{2,1,0:T(8,128)(2,1)S(1)} collective-permute-done((bf16[1,32,640]{2,1,0:T(8,128)(2,1)S(1)}, bf16[1,32,640]{2,1,0:T(8,128)(2,1)S(1)}, u32[]{:S(2)}, u32[]{:S(2)}) %collective-permute-start.6) | collective-permute-done | bytes 40992 | tf_op jit(solution)/shard_map/ppermute | solution.py:460
  12.0 0.1 collective-permute-done.3.refs_4_
  12.1 0.8 %collective-permute-done.1.refs_2_ = bf16[1,32,640]{2,1,0:T(8,128)(2,1)S(1)} collective-permute-done((bf16[1,32,640]{2,1,0:T(8,128)(2,1)S(1)}, bf16[1,32,640]{2,1,0:T(8,128)(2,1)S(1)}, u32[]{:S(2)}, u32[]{:S(2)}) %collective-permute-start.1) | collective-permute-done | bytes 40992 | tf_op jit(solution)/shard_map/ppermute | solution.py:463
  12.9 1.6 %shard_map.143 = (f32[8,640]{1,0:T(8,128)S(1)}, f32[8,512]{1,0:T(8,128)S(1)}, f32[8,640]{1,0:T(8,128)S(1)}, f32[8,512]{1,0:T(8,128)S(1)}) custom-call(bf16[1,32,640]{2,1,0:T(8,128)(2,1)S(1)} %shard_map.140.refs_0_, bf16[1,32,640]{2,1,0:T(8,128)(2,1)S(1)} %collective-permute-done.refs_1_, bf16[1,32,640]{2,1,0:T(8,128)(2,1)S(1)} %collective-permute-done.1.refs_2_, ...), custom_call_target="tpu_custom_call" | custom-call | tf_op jit(solution)/shard_map/pallas_call | solution.py:484
  14.5 0.2 %collective-permute-start.7 = (f32[8,640]{1,0:T(8,128)S(1)}, f32[8,640]{1,0:T(8,128)S(1)}, u32[]{:S(2)}, u32[]{:S(2)}) collective-permute-start(f32[8,640]{1,0:T(8,128)S(1)} %get-tuple-element.141), channel_id=1, source_target_pairs={{0,1},{1,0},{2,3},{3,2},{4,5},{5,4},{6,7},{7,6},{8,9},{9,8},{10,11... | collective-permute-start | bytes 61448 | tf_op jit(solution)/shard_map/ppermute | solution.py:463
  14.7 1.0 %collective-permute-done.7 = f32[8,640]{1,0:T(8,128)S(1)} collective-permute-done((f32[8,640]{1,0:T(8,128)S(1)}, f32[8,640]{1,0:T(8,128)S(1)}, u32[]{:S(2)}, u32[]{:S(2)}) %collective-permute-start.7) | collective-permute-done | bytes 20512 | tf_op jit(solution)/shard_map/ppermute | solution.py:463
  15.8 1.4 %collective-permute-start.8 = (f32[8,640]{1,0:T(8,128)S(1)}, f32[8,640]{1,0:T(8,128)S(1)}, u32[]{:S(2)}, u32[]{:S(2)}) collective-permute-start(f32[8,640]{1,0:T(8,128)S(1)} %add.3.over), channel_id=1, source_target_pairs={{0,3},{1,2},{2,1},{3,0},{4,7},{5,6},{6,5},{7,4},{8,11},{9,10},{10,... | collective-permute-start | bytes 61448 | tf_op jit(solution)/shard_map/ppermute | solution.py:492
  17.1 0.3 %collective-permute-start.9 = (f32[8,512]{1,0:T(8,128)S(1)}, f32[8,512]{1,0:T(8,128)S(1)}, u32[]{:S(2)}, u32[]{:S(2)}) collective-permute-start(f32[8,512]{1,0:T(8,128)S(1)} %get-tuple-element.143), channel_id=1, source_target_pairs={{0,1},{1,0},{2,3},{3,2},{4,5},{5,4},{6,7},{7,6},{8,9},{9,8},{10,11... | collective-permute-start | bytes 49160 | tf_op jit(solution)/shard_map/ppermute | solution.py:463
  17.5 0.8 %collective-permute-done.9.other_stay = f32[8,512]{1,0:T(8,128)S(1)} collective-permute-done((f32[8,512]{1,0:T(8,128)S(1)}, f32[8,512]{1,0:T(8,128)S(1)}, u32[]{:S(2)}, u32[]{:S(2)}) %collective-permute-start.9) | collective-permute-done | bytes 16416 | tf_op jit(solution)/shard_map/ppermute | solution.py:463
  18.3 0.6 %collective-permute-done.8.arrived = f32[8,640]{1,0:T(8,128)S(1)} collective-permute-done((f32[8,640]{1,0:T(8,128)S(1)}, f32[8,640]{1,0:T(8,128)S(1)}, u32[]{:S(2)}, u32[]{:S(2)}) %collective-permute-start.8) | collective-permute-done | bytes 20512 | tf_op jit(solution)/shard_map/ppermute | solution.py:492
  19.0 0.6 %shard_map.144 = (bf16[2,4,512]{2,1,0:T(4,128)(2,1)}, f32[1,16]{1,0:T(1,128)}) custom-call(f32[8,640]{1,0:T(8,128)S(1)} %add.3.over, f32[8,640]{1,0:T(8,128)S(1)} %collective-permute-done.8.arrived, f32[8,512]{1,0:T(8,128)S(1)} %get-tuple-element.142.stay, f32[8,512]{1,0:T(8,128)S(1)} %collective-permute-done.9.other_stay), custom_call_target="tpu_custom_call" | custom-call | tf_op jit(solution)/shard_map/pallas_call | solution.py:494
  (2 shorter events, 0.0 us)
Async XLA Ops:
  3.2 6.5 %collective-permute-start.4 = (bf16[1,32,640]{2,1,0:T(8,128)(2,1)S(1)}, bf16[1,32,640]{2,1,0:T(8,128)(2,1)S(1)}, u32[]{:S(2)}, u32[]{:S(2)}) collective-permute-start(bf16[1,32,640]{2,1,0:T(8,128)(2,1)S(1)} %shard_map.140.refs_0_), channel_id=1, source_target_pairs={{24,0},{29,1},{26,2},{31,3},{28,4},{25,5},{30,6},{27,7},{0,8},{5,9... | collective-permute-start | bytes 122888 | tf_op jit(solution)/shard_map/ppermute | solution.py:460
  4.6 6.3 %collective-permute-start.2 = (bf16[1,32,640]{2,1,0:T(8,128)(2,1)S(1)}, bf16[1,32,640]{2,1,0:T(8,128)(2,1)S(1)}, u32[]{:S(2)}, u32[]{:S(2)}) collective-permute-start(bf16[1,32,640]{2,1,0:T(8,128)(2,1)S(1)} %shard_map.140.refs_0_), channel_id=1, source_target_pairs={{16,0},{21,1},{18,2},{23,3},{20,4},{17,5},{22,6},{19,7},{24,8},{29... | collective-permute-start | bytes 122888 | tf_op jit(solution)/shard_map/ppermute | solution.py:460
  7.2 4.5 %collective-permute-start = (bf16[1,32,640]{2,1,0:T(8,128)(2,1)S(1)}, bf16[1,32,640]{2,1,0:T(8,128)(2,1)S(1)}, u32[]{:S(2)}, u32[]{:S(2)}) collective-permute-start(bf16[1,32,640]{2,1,0:T(8,128)(2,1)S(1)} %shard_map.140.refs_0_), channel_id=1, source_target_pairs={{8,0},{13,1},{10,2},{15,3},{12,4},{9,5},{14,6},{11,7},{16,8},{21,9... | collective-permute-start | bytes 122888 | tf_op jit(solution)/shard_map/ppermute | solution.py:460
  8.6 3.4 %collective-permute-start.6 = (bf16[1,32,640]{2,1,0:T(8,128)(2,1)S(1)}, bf16[1,32,640]{2,1,0:T(8,128)(2,1)S(1)}, u32[]{:S(2)}, u32[]{:S(2)}) collective-permute-start(bf16[1,32,640]{2,1,0:T(8,128)(2,1)S(1)} %shard_map.140.refs_0_), channel_id=1, source_target_pairs={{5,0},{4,1},{7,2},{6,3},{1,4},{0,5},{3,6},{2,7},{13,8},{12,9},{15,... | collective-permute-start | bytes 122888 | tf_op jit(solution)/shard_map/ppermute | solution.py:460
  9.7 2.4 %collective-permute-start.5 = (bf16[1,32,640]{2,1,0:T(8,128)(2,1)S(1)}, bf16[1,32,640]{2,1,0:T(8,128)(2,1)S(1)}, u32[]{:S(2)}, u32[]{:S(2)}) collective-permute-start(bf16[1,32,640]{2,1,0:T(8,128)(2,1)S(1)} %collective-permute-done.4.refs_5_), channel_id=1, source_target_pairs={{0,1},{1,0},{2,3},{3,2},{4,5},{5,4},{6,7},{7,6},{8,9},{9,8},{10,11... | collective-permute-start | bytes 122888 | tf_op jit(solution)/shard_map/ppermute | solution.py:463
  10.9 1.2 %collective-permute-start.3 = (bf16[1,32,640]{2,1,0:T(8,128)(2,1)S(1)}, bf16[1,32,640]{2,1,0:T(8,128)(2,1)S(1)}, u32[]{:S(2)}, u32[]{:S(2)}) collective-permute-start(bf16[1,32,640]{2,1,0:T(8,128)(2,1)S(1)} %collective-permute-done.2.refs_3_), channel_id=1, source_target_pairs={{0,1},{1,0},{2,3},{3,2},{4,5},{5,4},{6,7},{7,6},{8,9},{9,8},{10,11... | collective-permute-start | bytes 122888 | tf_op jit(solution)/shard_map/ppermute | solution.py:463
  11.7 1.2 %collective-permute-start.1 = (bf16[1,32,640]{2,1,0:T(8,128)(2,1)S(1)}, bf16[1,32,640]{2,1,0:T(8,128)(2,1)S(1)}, u32[]{:S(2)}, u32[]{:S(2)}) collective-permute-start(bf16[1,32,640]{2,1,0:T(8,128)(2,1)S(1)} %collective-permute-done.refs_1_), channel_id=1, source_target_pairs={{0,1},{1,0},{2,3},{3,2},{4,5},{5,4},{6,7},{7,6},{8,9},{9,8},{10,11... | collective-permute-start | bytes 122888 | tf_op jit(solution)/shard_map/ppermute | solution.py:463
  14.5 1.3 %collective-permute-start.7 = (f32[8,640]{1,0:T(8,128)S(1)}, f32[8,640]{1,0:T(8,128)S(1)}, u32[]{:S(2)}, u32[]{:S(2)}) collective-permute-start(f32[8,640]{1,0:T(8,128)S(1)} %get-tuple-element.141), channel_id=1, source_target_pairs={{0,1},{1,0},{2,3},{3,2},{4,5},{5,4},{6,7},{7,6},{8,9},{9,8},{10,11... | collective-permute-start | bytes 61448 | tf_op jit(solution)/shard_map/ppermute | solution.py:463
  15.8 3.2 %collective-permute-start.8 = (f32[8,640]{1,0:T(8,128)S(1)}, f32[8,640]{1,0:T(8,128)S(1)}, u32[]{:S(2)}, u32[]{:S(2)}) collective-permute-start(f32[8,640]{1,0:T(8,128)S(1)} %add.3.over), channel_id=1, source_target_pairs={{0,3},{1,2},{2,1},{3,0},{4,7},{5,6},{6,5},{7,4},{8,11},{9,10},{10,... | collective-permute-start | bytes 61448 | tf_op jit(solution)/shard_map/ppermute | solution.py:492
  17.1 1.2 %collective-permute-start.9 = (f32[8,512]{1,0:T(8,128)S(1)}, f32[8,512]{1,0:T(8,128)S(1)}, u32[]{:S(2)}, u32[]{:S(2)}) collective-permute-start(f32[8,512]{1,0:T(8,128)S(1)} %get-tuple-element.143), channel_id=1, source_target_pairs={{0,1},{1,0},{2,3},{3,2},{4,5},{5,4},{6,7},{7,6},{8,9},{9,8},{10,11... | collective-permute-start | bytes 49160 | tf_op jit(solution)/shard_map/ppermute | solution.py:463
